TPU v7x, 512 devices: a whole 4x8x8 slice. The times are simulated.
512 devices in a mesh: gx: 4 (over x), gy: 4 (over z_lo), gz: 32 (over z_hi, y, core).
Axes of the slice: x: 4, y: 8, z: 8 (z_hi: 2, z_lo: 4; z = z_hi * 4 + z_lo), core: 2. Of those that a mesh axis runs over, the one named last changes fastest.
Arguments:
- layer_input: bfloat16 [16, 32, 256, 128], P('gx', 'gy', 'gz'), may hold values from -6 to 6
- pre_one: bfloat16 [16, 32, 256, 128], P('gx', 'gy', 'gz'), may hold values from -6 to 6
- pre_two: bfloat16 [16, 32, 256, 128], P('gx', 'gy', 'gz'), may hold values from -6 to 6
- out_grad: bfloat16 [16, 32, 256, 128], P('gx', 'gy', 'gz'), may hold values from -6 to 6
- weight_one: bfloat16 [3, 3, 3, 128, 128], replicated, may hold values from -0.109375 to 0.109375
- weight_two: bfloat16 [3, 3, 3, 128, 128], replicated, may hold values from -0.109375 to 0.109375
Outputs:
- input_grad: bfloat16 [16, 32, 256, 128], P('gx', 'gy', 'gz')
- grad_one: bfloat16 [3, 3, 3, 128, 128], replicated
- grad_two: bfloat16 [3, 3, 3, 128, 128], replicated
All inputs are finite; a program needn't handle non-finite values.
Results may differ from a plain program's by a relative error of at most 0.0053.
Values may be sent and summed in bfloat16 or wider, within the bound.
No kernel may reach another device: no remote copies, remote signals or barrier semaphores. Data moves between devices by JAX's collectives and lax.ppermute only.
A program may use at most 64 MiB of HBM per device.

v0:
```python
import jax
import jax.numpy as jnp
from jax import lax
from jax.sharding import PartitionSpec as P

slope_low = 0.3


def extended(array, sides, width):
    for axis, dim in sides:
        peers, length = (lax.axis_size(axis), array.shape[dim])
        up = [(i, (i + 1) % peers) for i in range(peers - 1)]
        down = [(j, i) for i, j in up]
        last = lax.slice_in_dim(array, length - width, length, axis=dim)
        initial = lax.slice_in_dim(array, 0, width, axis=dim)
        before = lax.ppermute(last, axis, up)
        after = lax.ppermute(initial, axis, down)
        array = jnp.concatenate([before, array, after], axis=dim)
    return array


def leak_slope(pre):
    return jnp.where(pre > 0, 1.0, slope_low).astype(jnp.float32)


def layer_back(act, padded, weight):
    size_x, size_y, size_z, chans = act.shape
    acts = act.reshape(-1, chans)
    kernel_rows = []
    d_input = jnp.zeros((size_x * size_y * size_z, chans), jnp.float32)
    for first in range(3):
        for second in range(3):
            for third in range(3):
                window = padded[
                    2 - first : 2 - first + size_x,
                    2 - second : 2 - second + size_y,
                    2 - third : 2 - third + size_z,
                ]
                window = window.reshape(-1, chans)
                kernel_rows.append(
                    lax.dot_general(
                        acts, window, (((0,), (0,)), ((), ())), preferred_element_type=jnp.float32
                    )
                )
                d_input = d_input + lax.dot_general(
                    window,
                    weight[first, second, third],
                    (((1,), (1,)), ((), ())),
                    preferred_element_type=jnp.float32,
                )
    kernel = jnp.stack(kernel_rows).reshape(3, 3, 3, chans, chans)
    return (kernel, d_input.reshape(size_x, size_y, size_z, chans))


def reduce_kernels(kernels):
    return lax.psum((kernels[0], kernels[1]), ("gx", "gy", "gz"))


def on_device(layer_input, pre_one, pre_two, out_grad, weight_one, weight_two):
    size_x, size_y, size_z, chans = layer_input.shape
    cells_all = (
        size_x * size_y * size_z * lax.axis_size("gx") * lax.axis_size("gy") * lax.axis_size("gz")
    )
    scale = 1.0 / jnp.sqrt(jnp.float32(cells_all))
    pre_one_f = pre_one.astype(jnp.float32)
    one_slope = leak_slope(pre_one_f)
    hidden = (pre_one_f * one_slope).astype(jnp.bfloat16)
    g_two = (out_grad.astype(jnp.float32) * leak_slope(pre_two.astype(jnp.float32))).astype(
        jnp.bfloat16
    )
    padded_two = extended(g_two, (("gx", 0), ("gy", 1), ("gz", 2)), 1)
    kernel_two, d_hidden = layer_back(hidden, padded_two, weight_two)
    g_one = (d_hidden * one_slope).astype(jnp.bfloat16)
    padded_one = extended(g_one, (("gx", 0), ("gy", 1), ("gz", 2)), 1)
    kernel_one, d_input = layer_back(layer_input, padded_one, weight_one)
    total_one, total_two = reduce_kernels((kernel_one * scale, kernel_two * scale))
    return (
        d_input.astype(jnp.bfloat16),
        total_one.astype(jnp.bfloat16),
        total_two.astype(jnp.bfloat16),
    )


def solution(mesh):
    return jax.shard_map(
        on_device,
        mesh=mesh,
        in_specs=(
            P("gx", "gy", "gz", None),
            P("gx", "gy", "gz", None),
            P("gx", "gy", "gz", None),
            P("gx", "gy", "gz", None),
            P(),
            P(),
        ),
        out_specs=(P("gx", "gy", "gz", None), P(), P()),
        check_vma=False,
    )
```

profile of v0, /device:TPU:1, one launch (start us, length us, event | category | flops | bytes accessed | tf_op | source)
XLA Modules:
  0.0 211.3 jit_solution(16623742647401796079)
XLA Ops:
  0.7 1.0 multiply_convert_fusion
  1.7 3.9 %collective-permute-start = (bf16[1,8,8,128]{3,2,1,0:T(8,128)(2,1)S(1)}, bf16[1,8,8,128]{3,2,1,0:T(8,128)(2,1)S(1)}, u32[]{:S(2)}, u32[]{:S(2)}) collective-permute-start(bf16[1,8,8,128]{3,2,1,0:T(8,128)(2,1)S(1)} %get-tuple-element.75), channel_id=1, source_target_pairs={{0,128},{128,256},{256,384},{1,129},{129,257},{257,385},{2,130},{1... | collective-permute-start | bytes 49160 | tf_op jit(solution)/shard_map/ppermute | solution.py:16
  5.6 1.3 collective-permute-start.1
  6.9 3.2 %collective-permute-done.1 = bf16[1,8,8,128]{3,2,1,0:T(8,128)(2,1)S(1)} collective-permute-done((bf16[1,8,8,128]{3,2,1,0:T(8,128)(2,1)S(1)}, bf16[1,8,8,128]{3,2,1,0:T(8,128)(2,1)S(1)}, u32[]{:S(2)}, u32[]{:S(2)}) %collective-permute-start.1) | collective-permute-done | bytes 16416 | tf_op jit(solution)/shard_map/ppermute | solution.py:17
  10.1 4.0 %collective-permute-start.2 = (bf16[6,1,8,128]{3,2,1,0:T(8,128)(2,1)S(1)}, bf16[6,1,8,128]{3,2,1,0:T(8,128)(2,1)S(1)}, u32[]{:S(2)}, u32[]{:S(2)}) collective-permute-start(bf16[6,1,8,128]{3,2,1,0:T(8,128)(2,1)S(1)} %get-tuple-element.67), channel_id=1, source_target_pairs={{0,32},{32,64},{64,96},{1,33},{33,65},{65,97},{2,34},{34,66},{66,9... | collective-permute-start | bytes 36872 | tf_op jit(solution)/shard_map/ppermute | solution.py:16
  14.1 1.3 collective-permute-start.3
  15.4 3.8 %collective-permute-done.3 = bf16[6,1,8,128]{3,2,1,0:T(8,128)(2,1)S(1)} collective-permute-done((bf16[6,1,8,128]{3,2,1,0:T(8,128)(2,1)S(1)}, bf16[6,1,8,128]{3,2,1,0:T(8,128)(2,1)S(1)}, u32[]{:S(2)}, u32[]{:S(2)}) %collective-permute-start.3) | collective-permute-done | bytes 12320 | tf_op jit(solution)/shard_map/ppermute | solution.py:17
  19.2 5.2 %collective-permute-start.4 = (bf16[6,10,1,128]{3,2,1,0:T(2,128)(2,1)S(1)}, bf16[6,10,1,128]{3,2,1,0:T(2,128)(2,1)S(1)}, u32[]{:S(2)}, u32[]{:S(2)}) collective-permute-start(bf16[6,10,1,128]{3,2,1,0:T(2,128)(2,1)S(1)} %get-tuple-element.47), channel_id=1, source_target_pairs={{1,0},{2,1},{3,2},{4,3},{5,4},{6,5},{7,6},{8,7},{9,8},{10,9},{11,1... | collective-permute-start | bytes 46088 | tf_op jit(solution)/shard_map/ppermute | solution.py:17
  24.4 3.1 %collective-permute-start.5 = (bf16[6,10,1,128]{3,2,1,0:T(2,128)(2,1)S(1)}, bf16[6,10,1,128]{3,2,1,0:T(2,128)(2,1)S(1)}, u32[]{:S(2)}, u32[]{:S(2)}) collective-permute-start(bf16[6,10,1,128]{3,2,1,0:T(2,128)(2,1)S(1)} %get-tuple-element.48), channel_id=1, source_target_pairs={{0,1},{1,2},{2,3},{3,4},{4,5},{5,6},{6,7},{7,8},{8,9},{9,10},{10,1... | collective-permute-start | bytes 46088 | tf_op jit(solution)/shard_map/ppermute | solution.py:16
  27.8 0.7 collective-permute-done.5
  29.2 0.2 fusion.39
  33.5 3.1 %collective-permute-start.6 = (bf16[1,8,8,128]{3,2,1,0:T(8,128)(2,1)S(1)}, bf16[1,8,8,128]{3,2,1,0:T(8,128)(2,1)S(1)}, u32[]{:S(2)}, u32[]{:S(2)}) collective-permute-start(bf16[1,8,8,128]{3,2,1,0:T(8,128)(2,1)S(1)} %get-tuple-element.71), channel_id=1, source_target_pairs={{0,128},{128,256},{256,384},{1,129},{129,257},{257,385},{2,130},{1... | collective-permute-start | bytes 49160 | tf_op jit(solution)/shard_map/ppermute | solution.py:16
  36.6 1.3 collective-permute-start.7
  38.2 0.2 fusion.37
  38.4 0.2 fusion.36
  38.6 0.2 fusion.35
  38.8 0.2 fusion.34
  39.1 0.2 fusion.33
  39.5 0.2 fusion.31
  39.7 0.2 fusion.30
  39.9 0.2 fusion.29
  40.2 0.2 fusion.28
  40.4 0.2 fusion.27
  40.8 0.2 fusion.25
  41.1 0.2 fusion.24
  41.5 0.2 fusion.22
  41.7 0.2 fusion.21
  42.2 0.2 fusion.19
  42.4 0.2 fusion.18
  42.6 0.2 fusion.17
  42.8 0.2 fusion.16
  43.1 0.2 fusion.15
  43.5 0.2 fusion.13
  43.7 1.4 broadcast_multiply_fusion
  45.1 2.5 %copy.37 = f32[3,3,3,128,128]{4,3,2,1,0:T(8,128)S(1)} copy(f32[3,3,3,128,128]{3,4,2,1,0:T(8,128)} %bitcast.737) | data formatting | bytes 3538944 | tf_op jit(solution)/shard_map/mul | solution.py:76
  47.6 4.0 %collective-permute-start.8 = (bf16[6,1,8,128]{3,2,1,0:T(8,128)(2,1)S(1)}, bf16[6,1,8,128]{3,2,1,0:T(8,128)(2,1)S(1)}, u32[]{:S(2)}, u32[]{:S(2)}) collective-permute-start(bf16[6,1,8,128]{3,2,1,0:T(8,128)(2,1)S(1)} %get-tuple-element.63), channel_id=1, source_target_pairs={{0,32},{32,64},{64,96},{1,33},{33,65},{65,97},{2,34},{34,66},{66,9... | collective-permute-start | bytes 36872 | tf_op jit(solution)/shard_map/ppermute | solution.py:16
  51.7 1.3 collective-permute-start.9
  53.0 3.6 %collective-permute-done.9 = bf16[6,1,8,128]{3,2,1,0:T(8,128)(2,1)S(1)} collective-permute-done((bf16[6,1,8,128]{3,2,1,0:T(8,128)(2,1)S(1)}, bf16[6,1,8,128]{3,2,1,0:T(8,128)(2,1)S(1)}, u32[]{:S(2)}, u32[]{:S(2)}) %collective-permute-start.9) | collective-permute-done | bytes 12320 | tf_op jit(solution)/shard_map/ppermute | solution.py:17
  56.7 2.3 %collective-permute-start.10 = (bf16[6,10,1,128]{3,2,1,0:T(2,128)(2,1)S(1)}, bf16[6,10,1,128]{3,2,1,0:T(2,128)(2,1)S(1)}, u32[]{:S(2)}, u32[]{:S(2)}) collective-permute-start(bf16[6,10,1,128]{3,2,1,0:T(2,128)(2,1)S(1)} %get-tuple-element.43), channel_id=1, source_target_pairs={{1,0},{2,1},{3,2},{4,3},{5,4},{6,5},{7,6},{8,7},{9,8},{10,9},{11,1... | collective-permute-start | bytes 46088 | tf_op jit(solution)/shard_map/ppermute | solution.py:17
  59.0 5.0 %collective-permute-start.11 = (bf16[6,10,1,128]{3,2,1,0:T(2,128)(2,1)S(1)}, bf16[6,10,1,128]{3,2,1,0:T(2,128)(2,1)S(1)}, u32[]{:S(2)}, u32[]{:S(2)}) collective-permute-start(bf16[6,10,1,128]{3,2,1,0:T(2,128)(2,1)S(1)} %get-tuple-element.44), channel_id=1, source_target_pairs={{0,1},{1,2},{2,3},{3,4},{4,5},{5,6},{6,7},{7,8},{8,9},{9,10},{10,1... | collective-permute-start | bytes 46088 | tf_op jit(solution)/shard_map/ppermute | solution.py:16
  64.1 0.7 fusion.256
  64.8 0.7 fusion.257
  65.8 0.8 fusion.253
  66.6 0.8 fusion.252
  67.7 0.2 fusion.58
  68.0 0.2 fusion.12
  68.4 0.2 fusion.56
  69.1 0.2 fusion.54
  69.7 0.2 fusion.52
  70.0 0.2 fusion.9
  70.4 0.2 fusion.50
  71.1 0.2 fusion.47
  71.7 0.2 fusion.45
  72.0 0.2 fusion.7
  72.4 0.2 fusion.43
  73.1 0.2 fusion.41
  73.7 1.4 broadcast_multiply_fusion.1
  75.2 2.9 %copy.9 = f32[3,3,3,128,128]{4,3,2,1,0:T(8,128)} copy(f32[3,3,3,128,128]{3,4,2,1,0:T(8,128)} %bitcast.738) | data formatting | bytes 3538944 | tf_op jit(solution)/shard_map/mul | solution.py:76
  78.0 1.0 convolution_add_fusion.23
  79.1 1.0 convolution_add_fusion.22
  80.1 1.0 convolution_add_fusion.21
  81.4 1.0 convolution_add_fusion.19
  85.6 0.8 fusion.4
  86.4 124.8 %all-reduce.2 = (bf16[3,3,3,128,128]{4,3,2,1,0:T(8,128)(2,1)}, bf16[3,3,3,128,128]{4,3,2,1,0:T(8,128)(2,1)}) all-reduce(f32[3,3,3,128,128]{4,3,2,1,0:T(8,128)} %copy.9, f32[3,3,3,128,128]{4,3,2,1,0:T(8,128)S(1)} %copy.37), channel_id=1, replica_groups=mesh['gx'=4,'gy'=4,'gz'=32] {'gx','gy','gz'}, use_global_device_ids=true, to_apply=%region_0.1 | all-reduce | flops 884736 | bytes 5308416 | tf_op jit(solution)/shard_map/psum | solution.py:56
  (129 shorter events, 13.4 us)
Async XLA Ops:
  0.6 67.1 %copy-start = (bf16[4,8,8,128]{3,2,1,0:T(8,128)(2,1)S(1)}, bf16[4,8,8,128]{3,2,1,0:T(8,128)(2,1)}, u32[]{:S(2)}) copy-start(bf16[4,8,8,128]{3,2,1,0:T(8,128)(2,1)} %param.6) | copy-start | bytes 196612
  0.6 27.0 %copy-start.1 = (bf16[3,3,3,128,128]{4,3,2,1,0:T(8,128)(2,1)S(1)}, bf16[3,3,3,128,128]{4,3,2,1,0:T(8,128)(2,1)}, u32[]{:S(2)}) copy-start(bf16[3,3,3,128,128]{4,3,2,1,0:T(8,128)(2,1)} %param.11) | copy-start | bytes 2654212
  1.7 5.3 %collective-permute-start = (bf16[1,8,8,128]{3,2,1,0:T(8,128)(2,1)S(1)}, bf16[1,8,8,128]{3,2,1,0:T(8,128)(2,1)S(1)}, u32[]{:S(2)}, u32[]{:S(2)}) collective-permute-start(bf16[1,8,8,128]{3,2,1,0:T(8,128)(2,1)S(1)} %get-tuple-element.75), channel_id=1, source_target_pairs={{0,128},{128,256},{256,384},{1,129},{129,257},{257,385},{2,130},{1... | collective-permute-start | bytes 49160 | tf_op jit(solution)/shard_map/ppermute | solution.py:16
  5.6 4.5 %collective-permute-start.1 = (bf16[1,8,8,128]{3,2,1,0:T(8,128)(2,1)S(1)}, bf16[1,8,8,128]{3,2,1,0:T(8,128)(2,1)S(1)}, u32[]{:S(2)}, u32[]{:S(2)}) collective-permute-start(bf16[1,8,8,128]{3,2,1,0:T(8,128)(2,1)S(1)} %get-tuple-element.76), channel_id=1, source_target_pairs={{128,0},{256,128},{384,256},{129,1},{257,129},{385,257},{130,2},{2... | collective-permute-start | bytes 49160 | tf_op jit(solution)/shard_map/ppermute | solution.py:17
  10.1 5.3 %collective-permute-start.2 = (bf16[6,1,8,128]{3,2,1,0:T(8,128)(2,1)S(1)}, bf16[6,1,8,128]{3,2,1,0:T(8,128)(2,1)S(1)}, u32[]{:S(2)}, u32[]{:S(2)}) collective-permute-start(bf16[6,1,8,128]{3,2,1,0:T(8,128)(2,1)S(1)} %get-tuple-element.67), channel_id=1, source_target_pairs={{0,32},{32,64},{64,96},{1,33},{33,65},{65,97},{2,34},{34,66},{66,9... | collective-permute-start | bytes 36872 | tf_op jit(solution)/shard_map/ppermute | solution.py:16
  14.1 5.1 %collective-permute-start.3 = (bf16[6,1,8,128]{3,2,1,0:T(8,128)(2,1)S(1)}, bf16[6,1,8,128]{3,2,1,0:T(8,128)(2,1)S(1)}, u32[]{:S(2)}, u32[]{:S(2)}) collective-permute-start(bf16[6,1,8,128]{3,2,1,0:T(8,128)(2,1)S(1)} %get-tuple-element.68), channel_id=1, source_target_pairs={{32,0},{64,32},{96,64},{33,1},{65,33},{97,65},{34,2},{66,34},{98,6... | collective-permute-start | bytes 36872 | tf_op jit(solution)/shard_map/ppermute | solution.py:17
  19.2 8.6 %collective-permute-start.4 = (bf16[6,10,1,128]{3,2,1,0:T(2,128)(2,1)S(1)}, bf16[6,10,1,128]{3,2,1,0:T(2,128)(2,1)S(1)}, u32[]{:S(2)}, u32[]{:S(2)}) collective-permute-start(bf16[6,10,1,128]{3,2,1,0:T(2,128)(2,1)S(1)} %get-tuple-element.47), channel_id=1, source_target_pairs={{1,0},{2,1},{3,2},{4,3},{5,4},{6,5},{7,6},{8,7},{9,8},{10,9},{11,1... | collective-permute-start | bytes 46088 | tf_op jit(solution)/shard_map/ppermute | solution.py:17
  24.4 4.1 %collective-permute-start.5 = (bf16[6,10,1,128]{3,2,1,0:T(2,128)(2,1)S(1)}, bf16[6,10,1,128]{3,2,1,0:T(2,128)(2,1)S(1)}, u32[]{:S(2)}, u32[]{:S(2)}) collective-permute-start(bf16[6,10,1,128]{3,2,1,0:T(2,128)(2,1)S(1)} %get-tuple-element.48), channel_id=1, source_target_pairs={{0,1},{1,2},{2,3},{3,4},{4,5},{5,6},{6,7},{7,8},{8,9},{9,10},{10,1... | collective-permute-start | bytes 46088 | tf_op jit(solution)/shard_map/ppermute | solution.py:16
  27.8 1.4 copy-start.17
  33.5 14.1 %collective-permute-start.6 = (bf16[1,8,8,128]{3,2,1,0:T(8,128)(2,1)S(1)}, bf16[1,8,8,128]{3,2,1,0:T(8,128)(2,1)S(1)}, u32[]{:S(2)}, u32[]{:S(2)}) collective-permute-start(bf16[1,8,8,128]{3,2,1,0:T(8,128)(2,1)S(1)} %get-tuple-element.71), channel_id=1, source_target_pairs={{0,128},{128,256},{256,384},{1,129},{129,257},{257,385},{2,130},{1... | collective-permute-start | bytes 49160 | tf_op jit(solution)/shard_map/ppermute | solution.py:16
  36.6 11.0 %collective-permute-start.7 = (bf16[1,8,8,128]{3,2,1,0:T(8,128)(2,1)S(1)}, bf16[1,8,8,128]{3,2,1,0:T(8,128)(2,1)S(1)}, u32[]{:S(2)}, u32[]{:S(2)}) collective-permute-start(bf16[1,8,8,128]{3,2,1,0:T(8,128)(2,1)S(1)} %get-tuple-element.72), channel_id=1, source_target_pairs={{128,0},{256,128},{384,256},{129,1},{257,129},{385,257},{130,2},{2... | collective-permute-start | bytes 49160 | tf_op jit(solution)/shard_map/ppermute | solution.py:17
  45.1 20.3 %copy-start.2 = (bf16[3,3,3,128,128]{4,3,2,1,0:T(8,128)(2,1)S(1)}, bf16[3,3,3,128,128]{4,3,2,1,0:T(8,128)(2,1)}, u32[]{:S(2)}) copy-start(bf16[3,3,3,128,128]{4,3,2,1,0:T(8,128)(2,1)} %param.10) | copy-start | bytes 2654212
  47.6 5.3 %collective-permute-start.8 = (bf16[6,1,8,128]{3,2,1,0:T(8,128)(2,1)S(1)}, bf16[6,1,8,128]{3,2,1,0:T(8,128)(2,1)S(1)}, u32[]{:S(2)}, u32[]{:S(2)}) collective-permute-start(bf16[6,1,8,128]{3,2,1,0:T(8,128)(2,1)S(1)} %get-tuple-element.63), channel_id=1, source_target_pairs={{0,32},{32,64},{64,96},{1,33},{33,65},{65,97},{2,34},{34,66},{66,9... | collective-permute-start | bytes 36872 | tf_op jit(solution)/shard_map/ppermute | solution.py:16
  51.7 5.0 %collective-permute-start.9 = (bf16[6,1,8,128]{3,2,1,0:T(8,128)(2,1)S(1)}, bf16[6,1,8,128]{3,2,1,0:T(8,128)(2,1)S(1)}, u32[]{:S(2)}, u32[]{:S(2)}) collective-permute-start(bf16[6,1,8,128]{3,2,1,0:T(8,128)(2,1)S(1)} %get-tuple-element.64), channel_id=1, source_target_pairs={{32,0},{64,32},{96,64},{33,1},{65,33},{97,65},{34,2},{66,34},{98,6... | collective-permute-start | bytes 36872 | tf_op jit(solution)/shard_map/ppermute | solution.py:17
  56.7 9.0 %collective-permute-start.10 = (bf16[6,10,1,128]{3,2,1,0:T(2,128)(2,1)S(1)}, bf16[6,10,1,128]{3,2,1,0:T(2,128)(2,1)S(1)}, u32[]{:S(2)}, u32[]{:S(2)}) collective-permute-start(bf16[6,10,1,128]{3,2,1,0:T(2,128)(2,1)S(1)} %get-tuple-element.43), channel_id=1, source_target_pairs={{1,0},{2,1},{3,2},{4,3},{5,4},{6,5},{7,6},{8,7},{9,8},{10,9},{11,1... | collective-permute-start | bytes 46088 | tf_op jit(solution)/shard_map/ppermute | solution.py:17
  59.0 6.7 %collective-permute-start.11 = (bf16[6,10,1,128]{3,2,1,0:T(2,128)(2,1)S(1)}, bf16[6,10,1,128]{3,2,1,0:T(2,128)(2,1)S(1)}, u32[]{:S(2)}, u32[]{:S(2)}) collective-permute-start(bf16[6,10,1,128]{3,2,1,0:T(2,128)(2,1)S(1)} %get-tuple-element.44), channel_id=1, source_target_pairs={{0,1},{1,2},{2,3},{3,4},{4,5},{5,6},{6,7},{7,8},{8,9},{9,10},{10,1... | collective-permute-start | bytes 46088 | tf_op jit(solution)/shard_map/ppermute | solution.py:16
  78.0 4.4 %copy-start.16 = (bf16[4,8,8,128]{3,2,1,0:T(8,128)(2,1)S(1)}, bf16[4,8,8,128]{3,2,1,0:T(8,128)(2,1)}, u32[]{:S(2)}) copy-start(bf16[4,8,8,128]{3,2,1,0:T(8,128)(2,1)} %get-tuple-element.51) | copy-start | bytes 196612
  78.0 4.6 %copy-start.11 = (bf16[4,8,8,128]{3,2,1,0:T(8,128)(2,1)S(1)}, bf16[4,8,8,128]{3,2,1,0:T(8,128)(2,1)}, u32[]{:S(2)}) copy-start(bf16[4,8,8,128]{3,2,1,0:T(8,128)(2,1)} %get-tuple-element.11) | copy-start | bytes 196612
  78.0 4.7 %copy-start.9 = (bf16[4,8,8,128]{3,2,1,0:T(8,128)(2,1)S(1)}, bf16[4,8,8,128]{3,2,1,0:T(8,128)(2,1)}, u32[]{:S(2)}) copy-start(bf16[4,8,8,128]{3,2,1,0:T(8,128)(2,1)} %get-tuple-element.19) | copy-start | bytes 196612
  78.0 4.9 %copy-start.15 = (bf16[4,8,8,128]{3,2,1,0:T(8,128)(2,1)S(1)}, bf16[4,8,8,128]{3,2,1,0:T(8,128)(2,1)}, u32[]{:S(2)}) copy-start(bf16[4,8,8,128]{3,2,1,0:T(8,128)(2,1)} %get-tuple-element.53) | copy-start | bytes 196612
  78.0 5.1 %copy-start.10 = (bf16[4,8,8,128]{3,2,1,0:T(8,128)(2,1)S(1)}, bf16[4,8,8,128]{3,2,1,0:T(8,128)(2,1)}, u32[]{:S(2)}) copy-start(bf16[4,8,8,128]{3,2,1,0:T(8,128)(2,1)} %get-tuple-element.10) | copy-start | bytes 196612
  79.1 4.2 %copy-start.7 = (bf16[4,8,8,128]{3,2,1,0:T(8,128)(2,1)S(1)}, bf16[4,8,8,128]{3,2,1,0:T(8,128)(2,1)}, u32[]{:S(2)}) copy-start(bf16[4,8,8,128]{3,2,1,0:T(8,128)(2,1)} %get-tuple-element.18) | copy-start | bytes 196612
  81.2 2.5 %copy-start.8 = (bf16[4,8,8,128]{3,2,1,0:T(8,128)(2,1)S(1)}, bf16[4,8,8,128]{3,2,1,0:T(8,128)(2,1)}, u32[]{:S(2)}) copy-start(bf16[4,8,8,128]{3,2,1,0:T(8,128)(2,1)} %get-tuple-element.9) | copy-start | bytes 196612
  81.2 2.7 %copy-start.5 = (bf16[4,8,8,128]{3,2,1,0:T(8,128)(2,1)S(1)}, bf16[4,8,8,128]{3,2,1,0:T(8,128)(2,1)}, u32[]{:S(2)}) copy-start(bf16[4,8,8,128]{3,2,1,0:T(8,128)(2,1)} %get-tuple-element.17) | copy-start | bytes 196612
  81.3 2.7 %copy-start.14 = (bf16[4,8,8,128]{3,2,1,0:T(8,128)(2,1)S(1)}, bf16[4,8,8,128]{3,2,1,0:T(8,128)(2,1)}, u32[]{:S(2)}) copy-start(bf16[4,8,8,128]{3,2,1,0:T(8,128)(2,1)} %get-tuple-element.50) | copy-start | bytes 196612
  82.4 1.8 copy-start.6
  82.6 1.8 copy-start.3
  82.8 1.8 copy-start.13
  83.0 1.8 copy-start.4
  83.9 1.6 copy-start.12
where the time goes:
time: 212 us; the launch traced here: 211 us
  blocking collectives  125 us (59%)
  starting transfers between devices  35.8 us (17%)
  matrix products  24.6 us (12%)
  waiting for transfers between devices  11.2 us (5%)
  local copies, waits for them, and re-layouts  8.72 us (4%)
  other arithmetic  4.34 us (2%)
    psum x1, blocking collectives, reduce_kernels(): return lax.psum((kernels[0], kernels[1]), ('gx', 'gy', 'gz'))  125 us
    ppermute x6, starting transfers between devices, extended(): before = lax.ppermute(last, axis, up)  23.2 us
    dot_general x54, matrix products, layer_back(): lax.dot_general(window, weight[first, second, third], (((1,), (1,)), ((),...  12.9 us
    ppermute x6, starting transfers between devices, extended(): after = lax.ppermute(initial, axis, down)  12.6 us
    dot_general x54, matrix products, layer_back(): lax.dot_general(acts, window, (((0,), (0,)), ((), ())), preferred_element...  11.7 us
    ppermute x6, waiting for transfers between devices, extended(): after = lax.ppermute(initial, axis, down)  10.6 us
  transfers between devices with their start and end apart: 12, of which 4 were waited for; matrix products, arithmetic and copies ran while one was open for 5% of the time, Pallas kernels for 0%

commit v1 on v0

v1 whole, which is shorter than its diff:
```python
import functools

import jax
import jax.numpy as jnp
from jax import lax
from jax.experimental import pallas as pl
from jax.experimental.pallas import tpu as pltpu
from jax.sharding import Mesh
from jax.sharding import PartitionSpec as P

slope_low = 0.3
Z = ("gh", "gw", "gc")
REDUCE = ("gx", "gy", "gh", "gw")
C = 128
PITCH = 16
F32 = jnp.float32
BF16 = jnp.bfloat16


def exchange(up, down, axis):
    peers = lax.axis_size(axis)
    right = [(i, i + 1) for i in range(peers - 1)]
    left = [(i + 1, i) for i in range(peers - 1)]
    return lax.ppermute(up, axis, right), lax.ppermute(down, axis, left)


def pack(g, s):
    lines = g.shape[2]
    return jnp.concatenate(
        [g.reshape(-1, lines, C), s.reshape(-1, lines, C)], axis=0
    )


def unpack(rows, g_shape, s_shape):
    n = g_shape[0] * g_shape[1]
    return rows[:n].reshape(g_shape), rows[n:].reshape(s_shape)


def extend(g, s):
    nx, ny, nz, _ = g.shape
    up, down = exchange(pack(g[-2:], s[-1:]), pack(g[:2], s[:1]), "gx")
    shapes = ((2, ny, nz, C), (1, ny, nz, C))
    (g_lo, s_lo), (g_hi, s_hi) = unpack(up, *shapes), unpack(down, *shapes)
    g = jnp.concatenate([g_lo, g, g_hi], axis=0)
    s = jnp.concatenate([s_lo, s, s_hi], axis=0)

    up, down = exchange(
        pack(g[:, -2:], s[:, -1:]), pack(g[:, :2], s[:, :1]), "gy"
    )
    shapes = ((nx + 4, 2, nz, C), (nx + 2, 1, nz, C))
    (g_lo, s_lo), (g_hi, s_hi) = unpack(up, *shapes), unpack(down, *shapes)
    g = jnp.concatenate([g_lo, g, g_hi], axis=1)
    s = jnp.concatenate([s_lo, s, s_hi], axis=1)

    def flat(g_face, s_face):
        return jnp.concatenate(
            [g_face.reshape(-1, C), s_face.reshape(-1, C)], axis=0
        )

    up, down = exchange(
        flat(g[:, :, -2:], s[:, :, -1:]), flat(g[:, :, :2], s[:, :, :1]), Z
    )
    n = g.shape[0] * g.shape[1] * 2

    def faces(rows):
        return (
            rows[:n].reshape(g.shape[:2] + (2, C)),
            rows[n:].reshape(s.shape[:2] + (1, C)),
        )

    (g_lo, s_lo), (g_hi, s_hi) = faces(up), faces(down)
    rest = PITCH - nz - 4
    g = jnp.concatenate(
        [g_lo, g, g_hi, jnp.zeros(g.shape[:2] + (rest, C), BF16)], axis=2
    )
    edge = jnp.zeros(s.shape[:2] + (1, C), BF16)
    edge_end = jnp.zeros(s.shape[:2] + (rest + 1, C), BF16)
    s = jnp.concatenate([edge, s_lo, s, s_hi, edge_end], axis=2)
    return g, s


def pitched(cells):
    nx, ny, nz, _ = cells.shape
    return jnp.pad(cells, ((0, 0), (0, 0), (2, PITCH - nz - 2), (0, 0)))


def shifted_into(out_ref, cells):
    lead = cells.shape[:-1]
    rows = cells.reshape(-1, C)
    n = rows.shape[0]
    out_ref[..., :C] = pltpu.roll(rows, n - 1, 0).astype(BF16).reshape(lead + (C,))
    out_ref[..., C : 2 * C] = cells.astype(BF16)
    out_ref[..., 2 * C :] = pltpu.roll(rows, 1, 0).astype(BF16).reshape(lead + (C,))


def taps():
    return [(a, b) for a in range(3) for b in range(3)]


def window(ref, start_x, start_y, nx, ny):
    return ref[start_x : start_x + nx, start_y : start_y + ny].reshape(
        nx * ny * PITCH, 3 * C
    )


def kernel_grads(act_t, ref, first_x, first_y, nx, ny, scale, out_ref, slot):
    for t, (a, b) in enumerate(taps()):
        part = jnp.dot(
            act_t,
            window(ref, first_x - a, first_y - b, nx, ny),
            preferred_element_type=F32,
        )
        part = (part * scale).astype(BF16)
        for k in range(3):
            out_ref[slot, t * 3 + k] = part[:, k * C : (k + 1) * C]


def input_grads(ref, w_ref, first_x, first_y, nx, ny):
    total = None
    for t, (a, b) in enumerate(taps()):
        part = jnp.dot(
            window(ref, first_x - a, first_y - b, nx, ny),
            w_ref[t],
            preferred_element_type=F32,
        )
        total = part if total is None else total + part
    return total


def main_kernel(
    scale, core_ref, g_ref, s_ref, hidden_ref, input_ref, w_ref, grads_ref, g_one_ref, wide_two, wide_one
):
    core = core_ref[0]
    nx, ny = hidden_ref.shape[:2]
    shifted_into(wide_two, g_ref[...].astype(F32))
    hidden_t = hidden_ref[...].reshape(-1, C).T
    kernel_grads(hidden_t, wide_two, 3, 3, nx, ny, scale, grads_ref, 1 - core)
    d_hidden = input_grads(wide_two, w_ref, 2, 2, nx + 2, ny + 2)
    side = s_ref[...].astype(F32).reshape(-1, C)
    slope = jnp.where(side > 0, 1.0, jnp.where(side < 0, slope_low, 0.0))
    g_one = (d_hidden * slope).astype(BF16).reshape(s_ref.shape)
    shifted_into(wide_one, g_one.astype(F32))
    g_one_ref[...] = wide_one[...]
    input_t = input_ref[...].reshape(-1, C).T
    kernel_grads(input_t, wide_one, 2, 2, nx, ny, scale, grads_ref, core)


def input_kernel(wide_ref, w_ref, out_ref):
    nx, ny, nz, _ = out_ref.shape
    total = input_grads(wide_ref, w_ref, 2, 2, nx, ny)
    out_ref[...] = total.reshape(nx, ny, PITCH, C)[:, :, 2 : 2 + nz].astype(BF16)


def vmem():
    return pl.BlockSpec(memory_space=pltpu.VMEM)


def wide_weight(weight):
    return weight.transpose(0, 1, 2, 4, 3).reshape(9, 3 * C, C)


def reduced(grads):
    got = lax.ppermute(grads[1], "gc", [(0, 1), (1, 0)])
    mine = (grads[0].astype(F32) + got.astype(F32)).astype(BF16)
    groups = lax.axis_size(REDUCE)
    rows = mine.reshape(-1, PITCH, C)
    used = rows.shape[0]
    rows = jnp.pad(rows, ((0, groups - used), (0, 0), (0, 0)))
    parts = lax.all_to_all(rows, REDUCE, 0, 0, tiled=True)
    total = jnp.sum(parts.astype(F32), axis=0).astype(BF16)
    spread = jnp.broadcast_to(total[None], (groups,) + total.shape)
    spread = lax.all_to_all(spread, REDUCE, 0, 0, tiled=True)
    return spread[:used].reshape(grads.shape[1:])


def on_device(cells_all, layer_input, pre_one, pre_two, out_grad, weight_one, weight_two):
    nx, ny, nz, _ = layer_input.shape
    core = lax.axis_index("gc")
    pre_one_f = pre_one.astype(F32)
    hidden = (pre_one_f * jnp.where(pre_one_f > 0, 1.0, slope_low)).astype(BF16)
    side = jnp.where(pre_one_f > 0, 1.0, -1.0).astype(BF16)
    slope_two = jnp.where(pre_two.astype(F32) > 0, 1.0, slope_low)
    g_two = (out_grad.astype(F32) * slope_two).astype(BF16)
    g_two, side = extend(g_two, side)

    taps_flops = 2 * 27 * C * C
    cells = nx * ny * PITCH
    grads, wide_one = pl.pallas_call(
        functools.partial(main_kernel, float(cells_all) ** -0.5),
        out_shape=(
            jax.ShapeDtypeStruct((2, 27, C, C), BF16),
            jax.ShapeDtypeStruct((nx + 2, ny + 2, PITCH, 3 * C), BF16),
        ),
        in_specs=[pl.BlockSpec(memory_space=pltpu.SMEM)] + [vmem()] * 5,
        out_specs=(vmem(), vmem()),
        scratch_shapes=[
            pltpu.VMEM((nx + 4, ny + 4, PITCH, 3 * C), BF16),
            pltpu.VMEM((nx + 2, ny + 2, PITCH, 3 * C), BF16),
        ],
        compiler_params=pltpu.CompilerParams(vmem_limit_bytes=40 * 2**20),
        cost_estimate=pl.CostEstimate(
            flops=4 * cells * taps_flops, bytes_accessed=6 * 2**20, transcendentals=0
        ),
        name="kernel_gradients",
    )(
        core.reshape(1).astype(jnp.int32),
        g_two,
        side,
        pitched(hidden),
        pitched(layer_input),
        wide_weight(weight_two),
    )
    input_grad = pl.pallas_call(
        input_kernel,
        out_shape=jax.ShapeDtypeStruct((nx, ny, nz, C), BF16),
        in_specs=[vmem()] * 2,
        out_specs=vmem(),
        compiler_params=pltpu.CompilerParams(vmem_limit_bytes=40 * 2**20),
        cost_estimate=pl.CostEstimate(
            flops=cells * taps_flops, bytes_accessed=2 * 2**20, transcendentals=0
        ),
        name="input_gradient",
    )(wide_one, wide_weight(weight_one))

    mine = reduced(grads)
    other = lax.ppermute(mine, "gc", [(0, 1), (1, 0)])
    first = core == 0
    shape = weight_one.shape
    grad_one = jnp.where(first, mine, other).reshape(shape)
    grad_two = jnp.where(first, other, mine).reshape(shape)
    return input_grad, grad_one, grad_two


def solution(mesh):
    sizes = mesh.devices.shape
    cores, rows = 2, sizes[2] // 4
    devices = mesh.devices.reshape(sizes[0], sizes[1], 2, rows, cores)
    fine = Mesh(devices, ("gx", "gy", "gh", "gw", "gc"))
    split = P("gx", "gy", Z, None)

    def whole(*arrays):
        cells_all = 1
        for size in arrays[0].shape[:3]:
            cells_all *= size
        return jax.shard_map(
            functools.partial(on_device, cells_all),
            mesh=fine,
            in_specs=(split, split, split, split, P(), P()),
            out_specs=(split, P(), P()),
            check_vma=False,
        )(*arrays)

    return whole
```

time: 212 us -> 152 us (0.72)
  blocking collectives: 125 us -> 96.3 us
  matrix products: 24.6 us -> 0 us
  starting transfers between devices: 35.8 us -> 26.4 us
  Pallas kernels: 0 us -> 5.26 us
  local copies, waits for them, and re-layouts: 8.72 us -> 4.53 us
    psum x1 -> x0, blocking collectives: 125 us -> none  [reduce_kernels(): return lax.psum((kernels[0], kernels[1]), ('gx', 'gy', 'gz'))]
    all_to_all x0 -> x2, blocking collectives: none -> 96.3 us  [the longest x1 57 us: reduced(): parts = lax.all_to_all(rows, REDUCE, 0, 0, tiled=True)]
    dot_general x108 -> x0, matrix products: 24.6 us -> none  [the longest x54 12.9 us: layer_back(): lax.dot_general(window, weight[first, second, third], (((1,), (1,)), ((),...]
    ppermute x12 -> x8, starting transfers between devices: 35.8 us -> 26.4 us  [the longest x6 18.8 us: exchange(): return (lax.ppermute(up, axis, right), lax.ppermute(down, axis, left))]
    mul x2 -> x0, local copies, waits for them, and re-layouts: 5.36 us -> none  [the longest x1 2.87 us: on_device(): kernel_one * scale]
    pallas_call x0 -> x2, Pallas kernels: none -> 5.26 us  [the longest x1 3.56 us: on_device(): pl.pallas_call(functools.partial(main_kernel, float(cells_all) ** (-0.5))...]
    slice x8 -> x11, local copies, waits for them, and re-layouts: 3.27 us -> 0.35 us  [the longest x1 0.16 us: extend(): s[:, :, -1:]]
    mul x2 -> x0, other arithmetic: 2.81 us -> none  [the longest x1 1.42 us: on_device(): kernel_one * scale]
  transfers between devices with their start and end apart: 12 -> 8, of which waited for: 4 -> 4; matrix products, arithmetic and copies ran while one was open for 5% -> 2% of each run, Pallas kernels for 0% -> 1%
where the time goes in v1:
time: 152 us; the launch traced here: 151 us
  blocking collectives  96.3 us (63%)
  starting transfers between devices  26.4 us (17%)
  waiting for transfers between devices  12.1 us (8%)
  other arithmetic  5.42 us (4%)
  Pallas kernels  5.26 us (3%)
  local copies, waits for them, and re-layouts  4.53 us (3%)
    all_to_all x1, blocking collectives, reduced(): parts = lax.all_to_all(rows, REDUCE, 0, 0, tiled=True)  57 us
    all_to_all x1, blocking collectives, reduced(): spread = lax.all_to_all(spread, REDUCE, 0, 0, tiled=True)  39.3 us
    ppermute x6, starting transfers between devices, exchange(): return (lax.ppermute(up, axis, right), lax.ppermute(down, axis, left))  18.8 us
    ppermute x6, waiting for transfers between devices, exchange(): return (lax.ppermute(up, axis, right), lax.ppermute(down, axis, left))  9.67 us
    ppermute x1, starting transfers between devices, on_device(): other = lax.ppermute(mine, 'gc', [(0, 1), (1, 0)])  5.66 us
    pallas_call x1, Pallas kernels, on_device(): pl.pallas_call(functools.partial(main_kernel, float(cells_all) ** (-0.5))...  3.56 us
  transfers between devices with their start and end apart: 8, of which 4 were waited for; matrix products, arithmetic and copies ran while one was open for 2% of the time, Pallas kernels for 1%

profile of v1, /device:TPU:1, one launch (start us, length us, event | category | flops | bytes accessed | tf_op | source)
XLA Modules:
  0.0 151.0 jit_solution(11952414286885332724)
XLA Ops:
  0.6 0.0 copy-start
  0.6 1.0 fusion.1
  1.6 0.9 multiply_convert_fusion
  2.5 3.9 %collective-permute-start = (bf16[24,8,128]{2,1,0:T(8,128)(2,1)S(1)}, bf16[24,8,128]{2,1,0:T(8,128)(2,1)S(1)}, u32[]{:S(2)}, u32[]{:S(2)}) collective-permute-start(bf16[24,8,128]{2,1,0:T(8,128)(2,1)S(1)} %pad_maximum_fusion.8), channel_id=1, source_target_pairs={{0,128},{128,256},{256,384},{1,129},{129,257},{257,385},{2,130},{1... | collective-permute-start | bytes 147464 | tf_op jit(solution)/shard_map/ppermute | solution.py:24
  6.5 1.3 collective-permute-start.1
  7.8 0.0 collective-permute-done
  7.8 3.5 %collective-permute-done.1 = bf16[24,8,128]{2,1,0:T(8,128)(2,1)S(1)} collective-permute-done((bf16[24,8,128]{2,1,0:T(8,128)(2,1)S(1)}, bf16[24,8,128]{2,1,0:T(8,128)(2,1)S(1)}, u32[]{:S(2)}, u32[]{:S(2)}) %collective-permute-start.1) | collective-permute-done | bytes 49184 | tf_op jit(solution)/shard_map/ppermute | solution.py:24
  11.4 0.0 copy-start.2
  11.4 4.0 %collective-permute-start.2 = (bf16[22,8,128]{2,1,0:T(8,128)(2,1)S(1)}, bf16[22,8,128]{2,1,0:T(8,128)(2,1)S(1)}, u32[]{:S(2)}, u32[]{:S(2)}) collective-permute-start(bf16[22,8,128]{2,1,0:T(8,128)(2,1)S(1)} %pad_maximum_fusion.10), channel_id=1, source_target_pairs={{0,32},{32,64},{64,96},{1,33},{33,65},{65,97},{2,34},{34,66},{66,9... | collective-permute-start | bytes 135176 | tf_op jit(solution)/shard_map/ppermute | solution.py:24
  15.5 1.3 collective-permute-start.3
  16.8 0.0 collective-permute-done.2
  16.8 4.1 %collective-permute-done.3 = bf16[22,8,128]{2,1,0:T(8,128)(2,1)S(1)} collective-permute-done((bf16[22,8,128]{2,1,0:T(8,128)(2,1)S(1)}, bf16[22,8,128]{2,1,0:T(8,128)(2,1)S(1)}, u32[]{:S(2)}, u32[]{:S(2)}) %collective-permute-start.3) | collective-permute-done | bytes 45088 | tf_op jit(solution)/shard_map/ppermute | solution.py:24
  20.9 0.2 slice_reduce_fusion.1
  21.1 0.1 pad_maximum_fusion.7
  21.2 6.3 %collective-permute-start.4 = (bf16[252,128]{1,0:T(8,128)(2,1)S(1)}, bf16[252,128]{1,0:T(8,128)(2,1)S(1)}, u32[]{:S(2)}, u32[]{:S(2)}) collective-permute-start(bf16[252,128]{1,0:T(8,128)(2,1)S(1)} %pad_maximum_fusion.1), channel_id=1, source_target_pairs={{0,1},{1,2},{2,3},{3,4},{4,5},{5,6},{6,7},{7,8},{8,9},{9,10},{10,1... | collective-permute-start | bytes 193544 | tf_op jit(solution)/shard_map/ppermute | solution.py:24
  27.6 1.9 %collective-permute-start.5 = (bf16[252,128]{1,0:T(8,128)(2,1)S(1)}, bf16[252,128]{1,0:T(8,128)(2,1)S(1)}, u32[]{:S(2)}, u32[]{:S(2)}) collective-permute-start(bf16[252,128]{1,0:T(8,128)(2,1)S(1)} %pad_maximum_fusion.2), channel_id=1, source_target_pairs={{1,0},{2,1},{3,2},{4,3},{5,4},{6,5},{7,6},{8,7},{9,8},{10,9},{11,1... | collective-permute-start | bytes 193544 | tf_op jit(solution)/shard_map/ppermute | solution.py:24
  29.6 0.0 copy-done
  29.6 1.4 copy.17
  31.0 0.0 copy-done.2
  31.1 0.1 pad.21.clone
  31.1 0.0 collective-permute-done.4
  31.2 2.0 %collective-permute-done.5 = bf16[252,128]{1,0:T(8,128)(2,1)S(1)} collective-permute-done((bf16[252,128]{1,0:T(8,128)(2,1)S(1)}, bf16[252,128]{1,0:T(8,128)(2,1)S(1)}, u32[]{:S(2)}, u32[]{:S(2)}) %collective-permute-start.5) | collective-permute-done | bytes 64544 | tf_op jit(solution)/shard_map/ppermute | solution.py:24
  33.2 0.3 maximum_maximum_fusion.g_ref
  33.6 0.7 concatenate.47.s_ref
  34.3 3.6 %kernel_gradients.1 = (bf16[2,27,128,128]{3,2,1,0:T(8,128)(2,1)S(1)}, bf16[6,10,16,384]{3,2,1,0:T(8,128)(2,1)S(1)}) custom-call(s32[1]{0:T(128)} %bitcast.core_ref, bf16[8,12,16,128]{3,2,1,0:T(8,128)(2,1)S(1)} %maximum_maximum_fusion.g_ref, bf16[6,10,16,128]{3,2,1,0:T(8,128)(2,1)S(1)} %concatenate.47.s_ref, bf16[4,8,16,128]{3,2,1,0:T(8,128)(2,1)S(1)} %pad.11.hidden_ref, ...), custom_call_target="tpu_custom_call" | custom-call | flops 1811939328 | bytes 6291456 | tf_op jit(solution)/shard_map/kernel_gradients/pallas_call | solution.py:188
  37.9 0.1 slice_bitcast_fusion
  38.0 1.9 %collective-permute-start.6 = (bf16[27,128,128]{2,1,0:T(8,128)(2,1)S(1)}, bf16[27,128,128]{2,1,0:T(8,128)(2,1)S(1)}, u32[]{:S(2)}, u32[]{:S(2)}) collective-permute-start(bf16[27,128,128]{2,1,0:T(8,128)(2,1)S(1)} %slice_bitcast_fusion), channel_id=1, source_target_pairs={{0,1},{1,0},{2,3},{3,2},{4,5},{5,4},{6,7},{7,6},{8,9},{9,8},{10,11... | collective-permute-start | bytes 2654216 | tf_op jit(solution)/shard_map/ppermute | solution.py:163
  39.9 2.4 %collective-permute-done.6 = bf16[27,128,128]{2,1,0:T(8,128)(2,1)S(1)} collective-permute-done((bf16[27,128,128]{2,1,0:T(8,128)(2,1)S(1)}, bf16[27,128,128]{2,1,0:T(8,128)(2,1)S(1)}, u32[]{:S(2)}, u32[]{:S(2)}) %collective-permute-start.6) | collective-permute-done | bytes 884768 | tf_op jit(solution)/shard_map/ppermute | solution.py:163
  42.3 0.4 fusion
  42.7 0.2 pad.13
  42.8 57.0 %all_to_all.10 = bf16[256,16,128]{2,1,0:T(8,128)(2,1)S(1)} all-to-all(bf16[256,16,128]{2,1,0:T(8,128)(2,1)S(1)} %pad.13), channel_id=1, replica_groups=mesh['gx'=4,'gy'=4,'gh'=2,'gw'=8,'gc'=2] {'gx','gy','gh','gw'}, dimensions={0} | all-to-all | bytes 2097152 | tf_op jit(solution)/shard_map/all_to_all | solution.py:169
  99.8 0.3 reduce_sum.12
  100.1 0.1 broadcast_in_dim.35
  100.2 0.0 copy-start.1
  100.2 39.3 %all_to_all.11 = bf16[256,16,128]{2,1,0:T(8,128)(2,1)S(1)} all-to-all(bf16[256,16,128]{2,1,0:T(8,128)(2,1)S(1)} %broadcast_in_dim.35), channel_id=1, replica_groups=mesh['gx'=4,'gy'=4,'gh'=2,'gw'=8,'gc'=2] {'gx','gy','gh','gw'}, dimensions={0} | all-to-all | bytes 2097152 | tf_op jit(solution)/shard_map/all_to_all | solution.py:172
  139.5 0.2 slice.126
  139.7 5.7 %collective-permute-start.7 = (bf16[27,128,128]{2,1,0:T(8,128)(2,1)S(1)}, bf16[27,128,128]{2,1,0:T(8,128)(2,1)}, u32[]{:S(2)}, u32[]{:S(2)}) collective-permute-start(bf16[27,128,128]{2,1,0:T(8,128)(2,1)S(1)} %bitcast.51), channel_id=1, source_target_pairs={{0,1},{1,0},{2,3},{3,2},{4,5},{5,4},{6,7},{7,6},{8,9},{9,8},{10,11... | collective-permute-start | bytes 2654216 | tf_op jit(solution)/shard_map/ppermute | solution.py:226
  145.4 0.0 copy-done.1
  145.4 1.4 copy.18
  146.8 1.7 %input_gradient.1 = bf16[4,8,8,128]{3,2,1,0:T(8,128)(2,1)} custom-call(bf16[6,10,16,384]{3,2,1,0:T(8,128)(2,1)S(1)} %get-tuple-element.5.wide_ref, bf16[9,384,128]{2,1,0:T(8,128)(2,1)S(1)} %bitcast.49), custom_call_target="tpu_custom_call" | custom-call | flops 452984832 | bytes 2097152 | tf_op jit(solution)/shard_map/input_gradient/pallas_call | solution.py:213
  148.5 0.0 collective-permute-done.7
  148.5 2.5 %broadcast_select_fusion = (bf16[27,128,128]{2,1,0:T(8,128)(2,1)}, bf16[27,128,128]{2,1,0:T(8,128)(2,1)}) fusion(bf16[27,128,128]{2,1,0:T(8,128)(2,1)} %collective-permute-done.7, pred[]{:T(512)S(6)} %eq.3, bf16[27,128,128]{2,1,0:T(8,128)(2,1)S(1)} %bitcast.52), kind=kLoop, calls=%fused_computation.3 | loop fusion | flops 884736 | bytes 3538945 | tf_op jit(solution)/shard_map/jit(_where)/select_n | solution.py:230
  (32 shorter events, 0.3 us)
Async XLA Ops:
  0.6 28.9 %copy-start = (bf16[3,3,3,128,128]{4,3,2,1,0:T(8,128)(2,1)S(1)}, bf16[3,3,3,128,128]{4,3,2,1,0:T(8,128)(2,1)}, u32[]{:S(2)}) copy-start(bf16[3,3,3,128,128]{4,3,2,1,0:T(8,128)(2,1)} %param.11) | copy-start | bytes 2654212
  2.5 5.3 %collective-permute-start = (bf16[24,8,128]{2,1,0:T(8,128)(2,1)S(1)}, bf16[24,8,128]{2,1,0:T(8,128)(2,1)S(1)}, u32[]{:S(2)}, u32[]{:S(2)}) collective-permute-start(bf16[24,8,128]{2,1,0:T(8,128)(2,1)S(1)} %pad_maximum_fusion.8), channel_id=1, source_target_pairs={{0,128},{128,256},{256,384},{1,129},{129,257},{257,385},{2,130},{1... | collective-permute-start | bytes 147464 | tf_op jit(solution)/shard_map/ppermute | solution.py:24
  6.5 4.8 %collective-permute-start.1 = (bf16[24,8,128]{2,1,0:T(8,128)(2,1)S(1)}, bf16[24,8,128]{2,1,0:T(8,128)(2,1)S(1)}, u32[]{:S(2)}, u32[]{:S(2)}) collective-permute-start(bf16[24,8,128]{2,1,0:T(8,128)(2,1)S(1)} %pad_maximum_fusion.9), channel_id=1, source_target_pairs={{128,0},{256,128},{384,256},{129,1},{257,129},{385,257},{130,2},{2... | collective-permute-start | bytes 147464 | tf_op jit(solution)/shard_map/ppermute | solution.py:24
  11.4 19.6 %copy-start.2 = (bf16[4,8,8,128]{3,2,1,0:T(8,128)(2,1)S(1)}, bf16[4,8,8,128]{3,2,1,0:T(8,128)(2,1)}, u32[]{:S(2)}) copy-start(bf16[4,8,8,128]{3,2,1,0:T(8,128)(2,1)} %param.6) | copy-start | bytes 196612
  11.4 5.3 %collective-permute-start.2 = (bf16[22,8,128]{2,1,0:T(8,128)(2,1)S(1)}, bf16[22,8,128]{2,1,0:T(8,128)(2,1)S(1)}, u32[]{:S(2)}, u32[]{:S(2)}) collective-permute-start(bf16[22,8,128]{2,1,0:T(8,128)(2,1)S(1)} %pad_maximum_fusion.10), channel_id=1, source_target_pairs={{0,32},{32,64},{64,96},{1,33},{33,65},{65,97},{2,34},{34,66},{66,9... | collective-permute-start | bytes 135176 | tf_op jit(solution)/shard_map/ppermute | solution.py:24
  15.5 5.4 %collective-permute-start.3 = (bf16[22,8,128]{2,1,0:T(8,128)(2,1)S(1)}, bf16[22,8,128]{2,1,0:T(8,128)(2,1)S(1)}, u32[]{:S(2)}, u32[]{:S(2)}) collective-permute-start(bf16[22,8,128]{2,1,0:T(8,128)(2,1)S(1)} %pad_maximum_fusion.11), channel_id=1, source_target_pairs={{32,0},{64,32},{96,64},{33,1},{65,33},{97,65},{34,2},{66,34},{98,6... | collective-permute-start | bytes 135176 | tf_op jit(solution)/shard_map/ppermute | solution.py:24
  21.2 9.9 %collective-permute-start.4 = (bf16[252,128]{1,0:T(8,128)(2,1)S(1)}, bf16[252,128]{1,0:T(8,128)(2,1)S(1)}, u32[]{:S(2)}, u32[]{:S(2)}) collective-permute-start(bf16[252,128]{1,0:T(8,128)(2,1)S(1)} %pad_maximum_fusion.1), channel_id=1, source_target_pairs={{0,1},{1,2},{2,3},{3,4},{4,5},{5,6},{6,7},{7,8},{8,9},{9,10},{10,1... | collective-permute-start | bytes 193544 | tf_op jit(solution)/shard_map/ppermute | solution.py:24
  27.6 5.6 %collective-permute-start.5 = (bf16[252,128]{1,0:T(8,128)(2,1)S(1)}, bf16[252,128]{1,0:T(8,128)(2,1)S(1)}, u32[]{:S(2)}, u32[]{:S(2)}) collective-permute-start(bf16[252,128]{1,0:T(8,128)(2,1)S(1)} %pad_maximum_fusion.2), channel_id=1, source_target_pairs={{1,0},{2,1},{3,2},{4,3},{5,4},{6,5},{7,6},{8,7},{9,8},{10,9},{11,1... | collective-permute-start | bytes 193544 | tf_op jit(solution)/shard_map/ppermute | solution.py:24
  38.0 4.3 %collective-permute-start.6 = (bf16[27,128,128]{2,1,0:T(8,128)(2,1)S(1)}, bf16[27,128,128]{2,1,0:T(8,128)(2,1)S(1)}, u32[]{:S(2)}, u32[]{:S(2)}) collective-permute-start(bf16[27,128,128]{2,1,0:T(8,128)(2,1)S(1)} %slice_bitcast_fusion), channel_id=1, source_target_pairs={{0,1},{1,0},{2,3},{3,2},{4,5},{5,4},{6,7},{7,6},{8,9},{9,8},{10,11... | collective-permute-start | bytes 2654216 | tf_op jit(solution)/shard_map/ppermute | solution.py:163
  100.2 45.2 %copy-start.1 = (bf16[3,3,3,128,128]{4,3,2,1,0:T(8,128)(2,1)S(1)}, bf16[3,3,3,128,128]{4,3,2,1,0:T(8,128)(2,1)}, u32[]{:S(2)}) copy-start(bf16[3,3,3,128,128]{4,3,2,1,0:T(8,128)(2,1)} %param.10) | copy-start | bytes 2654212
  139.7 8.8 %collective-permute-start.7 = (bf16[27,128,128]{2,1,0:T(8,128)(2,1)S(1)}, bf16[27,128,128]{2,1,0:T(8,128)(2,1)}, u32[]{:S(2)}, u32[]{:S(2)}) collective-permute-start(bf16[27,128,128]{2,1,0:T(8,128)(2,1)S(1)} %bitcast.51), channel_id=1, source_target_pairs={{0,1},{1,0},{2,3},{3,2},{4,5},{5,4},{6,7},{7,6},{8,9},{9,8},{10,11... | collective-permute-start | bytes 2654216 | tf_op jit(solution)/shard_map/ppermute | solution.py:226

commit v2 on v1

--- a/solution.py
+++ b/solution.py
@@ -10,7 +10,8 @@
 
 slope_low = 0.3
 Z = ("gh", "gw", "gc")
-REDUCE = ("gx", "gy", "gh", "gw")
+NEAR = ("gx", "gw")
+FAR = ("gy", "gh")
 C = 128
 PITCH = 16
 F32 = jnp.float32
@@ -131,6 +132,7 @@
     scale, core_ref, g_ref, s_ref, hidden_ref, input_ref, w_ref, grads_ref, g_one_ref, wide_two, wide_one
 ):
     core = core_ref[0]
+    grads_ref[:, 27] = jnp.zeros((2, C, C), BF16)
     nx, ny = hidden_ref.shape[:2]
     shifted_into(wide_two, g_ref[...].astype(F32))
     hidden_t = hidden_ref[...].reshape(-1, C).T
@@ -159,18 +161,23 @@
     return weight.transpose(0, 1, 2, 4, 3).reshape(9, 3 * C, C)
 
 
+def spread(rows, axes):
+    peers = lax.axis_size(axes)
+    copies = jnp.broadcast_to(rows[None], (peers,) + rows.shape)
+    return lax.all_to_all(copies, axes, 0, 0, tiled=True)
+
+
+def added(parts):
+    return jnp.sum(parts.astype(F32), axis=0).astype(BF16)
+
+
 def reduced(grads):
     got = lax.ppermute(grads[1], "gc", [(0, 1), (1, 0)])
     mine = (grads[0].astype(F32) + got.astype(F32)).astype(BF16)
-    groups = lax.axis_size(REDUCE)
-    rows = mine.reshape(-1, PITCH, C)
-    used = rows.shape[0]
-    rows = jnp.pad(rows, ((0, groups - used), (0, 0), (0, 0)))
-    parts = lax.all_to_all(rows, REDUCE, 0, 0, tiled=True)
-    total = jnp.sum(parts.astype(F32), axis=0).astype(BF16)
-    spread = jnp.broadcast_to(total[None], (groups,) + total.shape)
-    spread = lax.all_to_all(spread, REDUCE, 0, 0, tiled=True)
-    return spread[:used].reshape(grads.shape[1:])
+    rows = mine.reshape(lax.axis_size(NEAR), -1, C)
+    share = added(lax.all_to_all(rows, NEAR, 0, 0, tiled=True))
+    total = added(spread(share, FAR))
+    return spread(total, NEAR).reshape(grads.shape[1:])
 
 
 def on_device(cells_all, layer_input, pre_one, pre_two, out_grad, weight_one, weight_two):
@@ -188,7 +195,7 @@
     grads, wide_one = pl.pallas_call(
         functools.partial(main_kernel, float(cells_all) ** -0.5),
         out_shape=(
-            jax.ShapeDtypeStruct((2, 27, C, C), BF16),
+            jax.ShapeDtypeStruct((2, 28, C, C), BF16),
             jax.ShapeDtypeStruct((nx + 2, ny + 2, PITCH, 3 * C), BF16),
         ),
         in_specs=[pl.BlockSpec(memory_space=pltpu.SMEM)] + [vmem()] * 5,
@@ -225,6 +232,7 @@
     mine = reduced(grads)
     other = lax.ppermute(mine, "gc", [(0, 1), (1, 0)])
     first = core == 0
+    mine, other = mine[:27], other[:27]
     shape = weight_one.shape
     grad_one = jnp.where(first, mine, other).reshape(shape)
     grad_two = jnp.where(first, other, mine).reshape(shape)

time: 152 us -> 138 us (0.908); the launches traced: 151 us -> 135 us
  blocking collectives: 96.3 us -> 81.4 us
  waiting for transfers between devices: 12.1 us -> 4.69 us
  starting transfers between devices: 26.4 us -> 33.4 us
    all_to_all x2 -> x3, blocking collectives: 96.3 us -> 81.4 us  [the longest x1 42.1 us: reduced(): share = added(lax.all_to_all(rows, NEAR, 0, 0, tiled=True))]
    ppermute x6, waiting for transfers between devices: 9.67 us -> 2.24 us  [exchange(): return (lax.ppermute(up, axis, right), lax.ppermute(down, axis, left))]
    ppermute x6, starting transfers between devices: 18.8 us -> 22.9 us  [exchange(): return (lax.ppermute(up, axis, right), lax.ppermute(down, axis, left))]
    ppermute x1, starting transfers between devices: 5.66 us -> 8.59 us  [on_device(): other = lax.ppermute(mine, 'gc', [(0, 1), (1, 0)])]
  transfers between devices with their start and end apart: 8 -> 8, of which waited for: 4 -> 3; matrix products, arithmetic and copies ran while one was open for 2% -> 2% of each run, Pallas kernels for 1% -> 1%
where the time goes in v2:
time: 138 us; the launch traced here: 135 us
  blocking collectives  81.4 us (59%)
  starting transfers between devices  33.4 us (24%)
  other arithmetic  5.36 us (4%)
  Pallas kernels  5.26 us (4%)
  waiting for transfers between devices  4.69 us (3%)
  local copies, waits for them, and re-layouts  4.22 us (3%)
    all_to_all x1, blocking collectives, reduced(): share = added(lax.all_to_all(rows, NEAR, 0, 0, tiled=True))  42.1 us
    all_to_all x2, blocking collectives, spread(): return lax.all_to_all(copies, axes, 0, 0, tiled=True)  39.3 us
    ppermute x6, starting transfers between devices, exchange(): return (lax.ppermute(up, axis, right), lax.ppermute(down, axis, left))  22.9 us
    ppermute x1, starting transfers between devices, on_device(): other = lax.ppermute(mine, 'gc', [(0, 1), (1, 0)])  8.59 us
    pallas_call x1, Pallas kernels, on_device(): pl.pallas_call(functools.partial(main_kernel, float(cells_all) ** (-0.5))...  3.55 us
    transpose x2, local copies, waits for them, and re-layouts, wide_weight(): return weight.transpose(0, 1, 2, 4, 3).reshape(9, 3 * C, C)  2.77 us
  transfers between devices with their start and end apart: 8, of which 3 were waited for; matrix products, arithmetic and copies ran while one was open for 2% of the time, Pallas kernels for 1%

profile of v2, /device:TPU:1, one launch (start us, length us, event | category | flops | bytes accessed | tf_op | source)
XLA Modules:
  0.0 135.4 jit_solution(10559389157164788769)
XLA Ops:
  0.6 0.0 copy-start.2
  0.6 0.0 copy-start
  0.7 1.0 fusion.1
  1.6 0.9 multiply_convert_fusion
  2.6 1.3 collective-permute-start.1
  3.9 4.6 %collective-permute-start = (bf16[24,8,128]{2,1,0:T(8,128)(2,1)S(1)}, bf16[24,8,128]{2,1,0:T(8,128)(2,1)S(1)}, u32[]{:S(2)}, u32[]{:S(2)}) collective-permute-start(bf16[24,8,128]{2,1,0:T(8,128)(2,1)S(1)} %pad_maximum_fusion.8), channel_id=1, source_target_pairs={{0,128},{128,256},{256,384},{1,129},{129,257},{257,385},{2,130},{1... | collective-permute-start | bytes 147464 | tf_op jit(solution)/shard_map/ppermute | solution.py:25
  8.5 0.0 collective-permute-done.1
  8.5 1.1 collective-permute-done
  9.7 1.3 collective-permute-start.3
  11.0 4.9 %collective-permute-start.2 = (bf16[22,8,128]{2,1,0:T(8,128)(2,1)S(1)}, bf16[22,8,128]{2,1,0:T(8,128)(2,1)S(1)}, u32[]{:S(2)}, u32[]{:S(2)}) collective-permute-start(bf16[22,8,128]{2,1,0:T(8,128)(2,1)S(1)} %pad_maximum_fusion.10), channel_id=1, source_target_pairs={{0,32},{32,64},{64,96},{1,33},{33,65},{65,97},{2,34},{34,66},{66,9... | collective-permute-start | bytes 135176 | tf_op jit(solution)/shard_map/ppermute | solution.py:25
  15.9 0.0 collective-permute-done.3
  15.9 1.1 collective-permute-done.2
  17.0 0.2 slice_reduce_fusion.1
  17.3 0.1 pad_maximum_fusion.7
  17.4 5.8 %collective-permute-start.4 = (bf16[252,128]{1,0:T(8,128)(2,1)S(1)}, bf16[252,128]{1,0:T(8,128)(2,1)S(1)}, u32[]{:S(2)}, u32[]{:S(2)}) collective-permute-start(bf16[252,128]{1,0:T(8,128)(2,1)S(1)} %pad_maximum_fusion.1), channel_id=1, source_target_pairs={{0,1},{1,2},{2,3},{3,4},{4,5},{5,6},{6,7},{7,8},{8,9},{9,10},{10,1... | collective-permute-start | bytes 193544 | tf_op jit(solution)/shard_map/ppermute | solution.py:25
  23.1 5.1 %collective-permute-start.5 = (bf16[252,128]{1,0:T(8,128)(2,1)S(1)}, bf16[252,128]{1,0:T(8,128)(2,1)S(1)}, u32[]{:S(2)}, u32[]{:S(2)}) collective-permute-start(bf16[252,128]{1,0:T(8,128)(2,1)S(1)} %pad_maximum_fusion.2), channel_id=1, source_target_pairs={{1,0},{2,1},{3,2},{4,3},{5,4},{6,5},{7,6},{8,7},{9,8},{10,9},{11,1... | collective-permute-start | bytes 193544 | tf_op jit(solution)/shard_map/ppermute | solution.py:25
  28.3 0.0 copy-done.2
  28.4 0.0 copy-done
  28.4 1.4 %copy.23 = bf16[3,3,3,128,128]{4,3,2,1,0:T(8,128)(2,1)S(1)} copy(bf16[3,3,3,128,128]{3,4,2,1,0:T(8,128)(2,1)S(1)} %bitcast.51) | data formatting | bytes 1769472 | tf_op jit(solution)/shard_map/transpose | solution.py:161
  29.8 0.1 pad.16.clone
  29.9 0.0 collective-permute-done.4
  29.9 0.0 collective-permute-done.5
  30.0 0.3 maximum_maximum_fusion.g_ref
  30.3 0.7 concatenate.47.s_ref
  31.0 3.6 %kernel_gradients.1 = (bf16[2,28,128,128]{3,2,1,0:T(8,128)(2,1)S(1)}, bf16[6,10,16,384]{3,2,1,0:T(8,128)(2,1)S(1)}) custom-call(s32[1]{0:T(128)} %bitcast.core_ref, bf16[8,12,16,128]{3,2,1,0:T(8,128)(2,1)S(1)} %maximum_maximum_fusion.g_ref, bf16[6,10,16,128]{3,2,1,0:T(8,128)(2,1)S(1)} %concatenate.47.s_ref, bf16[4,8,16,128]{3,2,1,0:T(8,128)(2,1)S(1)} %pad.7.hidden_ref, ...), custom_call_target="tpu_custom_call" | custom-call | flops 1811939328 | bytes 6291456 | tf_op jit(solution)/shard_map/kernel_gradients/pallas_call | solution.py:195
  34.6 0.1 slice_bitcast_fusion
  34.7 1.9 %collective-permute-start.6 = (bf16[28,128,128]{2,1,0:T(8,128)(2,1)S(1)}, bf16[28,128,128]{2,1,0:T(8,128)(2,1)S(1)}, u32[]{:S(2)}, u32[]{:S(2)}) collective-permute-start(bf16[28,128,128]{2,1,0:T(8,128)(2,1)S(1)} %slice_bitcast_fusion), channel_id=1, source_target_pairs={{0,1},{1,0},{2,3},{3,2},{4,5},{5,4},{6,7},{7,6},{8,9},{9,8},{10,11... | collective-permute-start | bytes 2752520 | tf_op jit(solution)/shard_map/ppermute | solution.py:175
  36.6 2.4 %collective-permute-done.6 = bf16[28,128,128]{2,1,0:T(8,128)(2,1)S(1)} collective-permute-done((bf16[28,128,128]{2,1,0:T(8,128)(2,1)S(1)}, bf16[28,128,128]{2,1,0:T(8,128)(2,1)S(1)}, u32[]{:S(2)}, u32[]{:S(2)}) %collective-permute-start.6) | collective-permute-done | bytes 917536 | tf_op jit(solution)/shard_map/ppermute | solution.py:175
  39.1 0.4 fusion
  39.4 42.1 %all_to_all.15 = bf16[32,112,128]{2,1,0:T(8,128)(2,1)S(1)} all-to-all(bf16[32,112,128]{2,1,0:T(8,128)(2,1)S(1)} %bitcast.48), channel_id=1, replica_groups=mesh['gx'=4,'gy'=4,'gh'=2,'gw'=8,'gc'=2] {'gx','gw'}, dimensions={0} | all-to-all | bytes 1835008 | tf_op jit(solution)/shard_map/all_to_all | solution.py:178
  81.5 0.1 reduce_sum.24
  81.7 0.0 copy-start.1
  81.7 12.1 %all_to_all.16 = bf16[8,112,128]{2,1,0:T(8,128)(2,1)S(1)} all-to-all(bf16[8,112,128]{2,1,0:T(8,128)(2,1)S(1)} %broadcast_in_dim.41), channel_id=1, replica_groups=mesh['gx'=4,'gy'=4,'gh'=2,'gw'=8,'gc'=2] {'gy','gh'}, dimensions={0} | all-to-all | bytes 458752 | tf_op jit(solution)/shard_map/all_to_all | solution.py:167
  93.8 0.1 broadcast_in_dim.42
  94.0 27.3 %all_to_all.17 = bf16[32,112,128]{2,1,0:T(8,128)(2,1)S(1)} all-to-all(bf16[32,112,128]{2,1,0:T(8,128)(2,1)S(1)} %broadcast_in_dim.42), channel_id=1, replica_groups=mesh['gx'=4,'gy'=4,'gh'=2,'gw'=8,'gc'=2] {'gx','gw'}, dimensions={0} | all-to-all | bytes 1835008 | tf_op jit(solution)/shard_map/all_to_all | solution.py:167
  121.2 8.6 %collective-permute-start.7 = (bf16[28,128,128]{2,1,0:T(8,128)(2,1)S(1)}, bf16[28,128,128]{2,1,0:T(8,128)(2,1)}, u32[]{:S(2)}, u32[]{:S(2)}) collective-permute-start(bf16[28,128,128]{2,1,0:T(8,128)(2,1)S(1)} %bitcast.49), channel_id=1, source_target_pairs={{0,1},{1,0},{2,3},{3,2},{4,5},{5,4},{6,7},{7,6},{8,9},{9,8},{10,11... | collective-permute-start | bytes 2752520 | tf_op jit(solution)/shard_map/ppermute | solution.py:233
  129.8 0.0 copy-done.1
  129.8 1.4 %copy.24 = bf16[3,3,3,128,128]{4,3,2,1,0:T(8,128)(2,1)S(1)} copy(bf16[3,3,3,128,128]{3,4,2,1,0:T(8,128)(2,1)S(1)} %bitcast.52) | data formatting | bytes 1769472 | tf_op jit(solution)/shard_map/transpose | solution.py:161
  131.2 1.7 %input_gradient.1 = bf16[4,8,8,128]{3,2,1,0:T(8,128)(2,1)} custom-call(bf16[6,10,16,384]{3,2,1,0:T(8,128)(2,1)S(1)} %get-tuple-element.5.wide_ref, bf16[9,384,128]{2,1,0:T(8,128)(2,1)S(1)} %bitcast.46), custom_call_target="tpu_custom_call" | custom-call | flops 452984832 | bytes 2097152 | tf_op jit(solution)/shard_map/input_gradient/pallas_call | solution.py:220
  132.9 0.0 collective-permute-done.7
  132.9 2.5 %broadcast_select_fusion = (bf16[27,128,128]{2,1,0:T(8,128)(2,1)}, bf16[27,128,128]{2,1,0:T(8,128)(2,1)}) fusion(pred[]{:T(512)S(6)} %eq.3, bf16[28,128,128]{2,1,0:T(8,128)(2,1)} %collective-permute-done.7, bf16[28,128,128]{2,1,0:T(8,128)(2,1)S(1)} %bitcast.50), kind=kLoop, calls=%fused_computation.3 | loop fusion | flops 884736 | bytes 3538945 | tf_op jit(solution)/shard_map/jit(_where)/select_n | solution.py:238
  (34 shorter events, 0.4 us)
Async XLA Ops:
  0.6 27.7 %copy-start.2 = (bf16[4,8,8,128]{3,2,1,0:T(8,128)(2,1)S(1)}, bf16[4,8,8,128]{3,2,1,0:T(8,128)(2,1)}, u32[]{:S(2)}) copy-start(bf16[4,8,8,128]{3,2,1,0:T(8,128)(2,1)} %param.6) | copy-start | bytes 196612
  0.6 27.7 %copy-start = (bf16[3,3,3,128,128]{4,3,2,1,0:T(8,128)(2,1)S(1)}, bf16[3,3,3,128,128]{4,3,2,1,0:T(8,128)(2,1)}, u32[]{:S(2)}) copy-start(bf16[3,3,3,128,128]{4,3,2,1,0:T(8,128)(2,1)} %param.11) | copy-start | bytes 2654212
  2.6 5.9 %collective-permute-start.1 = (bf16[24,8,128]{2,1,0:T(8,128)(2,1)S(1)}, bf16[24,8,128]{2,1,0:T(8,128)(2,1)S(1)}, u32[]{:S(2)}, u32[]{:S(2)}) collective-permute-start(bf16[24,8,128]{2,1,0:T(8,128)(2,1)S(1)} %pad_maximum_fusion.9), channel_id=1, source_target_pairs={{128,0},{256,128},{384,256},{129,1},{257,129},{385,257},{130,2},{2... | collective-permute-start | bytes 147464 | tf_op jit(solution)/shard_map/ppermute | solution.py:25
  3.9 5.7 %collective-permute-start = (bf16[24,8,128]{2,1,0:T(8,128)(2,1)S(1)}, bf16[24,8,128]{2,1,0:T(8,128)(2,1)S(1)}, u32[]{:S(2)}, u32[]{:S(2)}) collective-permute-start(bf16[24,8,128]{2,1,0:T(8,128)(2,1)S(1)} %pad_maximum_fusion.8), channel_id=1, source_target_pairs={{0,128},{128,256},{256,384},{1,129},{129,257},{257,385},{2,130},{1... | collective-permute-start | bytes 147464 | tf_op jit(solution)/shard_map/ppermute | solution.py:25
  9.7 6.2 %collective-permute-start.3 = (bf16[22,8,128]{2,1,0:T(8,128)(2,1)S(1)}, bf16[22,8,128]{2,1,0:T(8,128)(2,1)S(1)}, u32[]{:S(2)}, u32[]{:S(2)}) collective-permute-start(bf16[22,8,128]{2,1,0:T(8,128)(2,1)S(1)} %pad_maximum_fusion.11), channel_id=1, source_target_pairs={{32,0},{64,32},{96,64},{33,1},{65,33},{97,65},{34,2},{66,34},{98,6... | collective-permute-start | bytes 135176 | tf_op jit(solution)/shard_map/ppermute | solution.py:25
  11.0 6.0 %collective-permute-start.2 = (bf16[22,8,128]{2,1,0:T(8,128)(2,1)S(1)}, bf16[22,8,128]{2,1,0:T(8,128)(2,1)S(1)}, u32[]{:S(2)}, u32[]{:S(2)}) collective-permute-start(bf16[22,8,128]{2,1,0:T(8,128)(2,1)S(1)} %pad_maximum_fusion.10), channel_id=1, source_target_pairs={{0,32},{32,64},{64,96},{1,33},{33,65},{65,97},{2,34},{34,66},{66,9... | collective-permute-start | bytes 135176 | tf_op jit(solution)/shard_map/ppermute | solution.py:25
  17.4 12.5 %collective-permute-start.4 = (bf16[252,128]{1,0:T(8,128)(2,1)S(1)}, bf16[252,128]{1,0:T(8,128)(2,1)S(1)}, u32[]{:S(2)}, u32[]{:S(2)}) collective-permute-start(bf16[252,128]{1,0:T(8,128)(2,1)S(1)} %pad_maximum_fusion.1), channel_id=1, source_target_pairs={{0,1},{1,2},{2,3},{3,4},{4,5},{5,6},{6,7},{7,8},{8,9},{9,10},{10,1... | collective-permute-start | bytes 193544 | tf_op jit(solution)/shard_map/ppermute | solution.py:25
  23.1 6.8 %collective-permute-start.5 = (bf16[252,128]{1,0:T(8,128)(2,1)S(1)}, bf16[252,128]{1,0:T(8,128)(2,1)S(1)}, u32[]{:S(2)}, u32[]{:S(2)}) collective-permute-start(bf16[252,128]{1,0:T(8,128)(2,1)S(1)} %pad_maximum_fusion.2), channel_id=1, source_target_pairs={{1,0},{2,1},{3,2},{4,3},{5,4},{6,5},{7,6},{8,7},{9,8},{10,9},{11,1... | collective-permute-start | bytes 193544 | tf_op jit(solution)/shard_map/ppermute | solution.py:25
  34.7 4.4 %collective-permute-start.6 = (bf16[28,128,128]{2,1,0:T(8,128)(2,1)S(1)}, bf16[28,128,128]{2,1,0:T(8,128)(2,1)S(1)}, u32[]{:S(2)}, u32[]{:S(2)}) collective-permute-start(bf16[28,128,128]{2,1,0:T(8,128)(2,1)S(1)} %slice_bitcast_fusion), channel_id=1, source_target_pairs={{0,1},{1,0},{2,3},{3,2},{4,5},{5,4},{6,7},{7,6},{8,9},{9,8},{10,11... | collective-permute-start | bytes 2752520 | tf_op jit(solution)/shard_map/ppermute | solution.py:175
  81.7 48.1 %copy-start.1 = (bf16[3,3,3,128,128]{4,3,2,1,0:T(8,128)(2,1)S(1)}, bf16[3,3,3,128,128]{4,3,2,1,0:T(8,128)(2,1)}, u32[]{:S(2)}) copy-start(bf16[3,3,3,128,128]{4,3,2,1,0:T(8,128)(2,1)} %param.10) | copy-start | bytes 2654212
  121.2 11.7 %collective-permute-start.7 = (bf16[28,128,128]{2,1,0:T(8,128)(2,1)S(1)}, bf16[28,128,128]{2,1,0:T(8,128)(2,1)}, u32[]{:S(2)}, u32[]{:S(2)}) collective-permute-start(bf16[28,128,128]{2,1,0:T(8,128)(2,1)S(1)} %bitcast.49), channel_id=1, source_target_pairs={{0,1},{1,0},{2,3},{3,2},{4,5},{5,4},{6,7},{7,6},{8,9},{9,8},{10,11... | collective-permute-start | bytes 2752520 | tf_op jit(solution)/shard_map/ppermute | solution.py:233

commit v3 on v2

--- a/solution.py
+++ b/solution.py
@@ -10,7 +10,6 @@
 
 slope_low = 0.3
 Z = ("gh", "gw", "gc")
-NEAR = ("gx", "gw")
 FAR = ("gy", "gh")
 C = 128
 PITCH = 16
@@ -37,7 +36,7 @@
     return rows[:n].reshape(g_shape), rows[n:].reshape(s_shape)
 
 
-def extend(g, s):
+def extend(g, s, upper):
     nx, ny, nz, _ = g.shape
     up, down = exchange(pack(g[-2:], s[-1:]), pack(g[:2], s[:1]), "gx")
     shapes = ((2, ny, nz, C), (1, ny, nz, C))
@@ -53,31 +52,18 @@
     g = jnp.concatenate([g_lo, g, g_hi], axis=1)
     s = jnp.concatenate([s_lo, s, s_hi], axis=1)
 
-    def flat(g_face, s_face):
-        return jnp.concatenate(
-            [g_face.reshape(-1, C), s_face.reshape(-1, C)], axis=0
-        )
-
-    up, down = exchange(
-        flat(g[:, :, -2:], s[:, :, -1:]), flat(g[:, :, :2], s[:, :, :1]), Z
-    )
-    n = g.shape[0] * g.shape[1] * 2
-
-    def faces(rows):
-        return (
-            rows[:n].reshape(g.shape[:2] + (2, C)),
-            rows[n:].reshape(s.shape[:2] + (1, C)),
-        )
-
-    (g_lo, s_lo), (g_hi, s_hi) = faces(up), faces(down)
-    rest = PITCH - nz - 4
-    g = jnp.concatenate(
-        [g_lo, g, g_hi, jnp.zeros(g.shape[:2] + (rest, C), BF16)], axis=2
-    )
-    edge = jnp.zeros(s.shape[:2] + (1, C), BF16)
-    edge_end = jnp.zeros(s.shape[:2] + (rest + 1, C), BF16)
-    s = jnp.concatenate([edge, s_lo, s, s_hi, edge_end], axis=2)
-    return g, s
+    lines = pack(g, s)
+    last, first = lines[:, -2:], lines[:, :2]
+    outer, inner = [], []
+    for i in range(1, lax.axis_size(Z) - 1, 2):
+        outer += [(i, i + 1), (i + 1, i)]
+    for i in range(0, lax.axis_size(Z), 2):
+        inner += [(i, i + 1), (i + 1, i)]
+    far = lax.ppermute(jnp.where(upper, last, first), Z, outer)
+    near = lax.ppermute(jnp.where(upper, first, last), Z, inner)
+    lo, hi = jnp.where(upper, near, far), jnp.where(upper, far, near)
+    rest = jnp.zeros((lines.shape[0], PITCH - nz - 4, C), BF16)
+    return jnp.concatenate([lo, lines, hi, rest], axis=1)
 
 
 def pitched(cells):
@@ -119,9 +105,11 @@
 def input_grads(ref, w_ref, first_x, first_y, nx, ny):
     total = None
     for t, (a, b) in enumerate(taps()):
-        part = jnp.dot(
+        weight = jnp.concatenate([w_ref[3 * t + k] for k in range(3)], axis=1)
+        part = lax.dot_general(
             window(ref, first_x - a, first_y - b, nx, ny),
-            w_ref[t],
+            weight,
+            (((1,), (1,)), ((), ())),
             preferred_element_type=F32,
         )
         total = part if total is None else total + part
@@ -129,18 +117,19 @@
 
 
 def main_kernel(
-    scale, core_ref, g_ref, s_ref, hidden_ref, input_ref, w_ref, grads_ref, g_one_ref, wide_two, wide_one
+    scale, core_ref, lines_ref, hidden_ref, input_ref, w_ref, grads_ref, g_one_ref, wide_two, wide_one
 ):
     core = core_ref[0]
     grads_ref[:, 27] = jnp.zeros((2, C, C), BF16)
     nx, ny = hidden_ref.shape[:2]
-    shifted_into(wide_two, g_ref[...].astype(F32))
+    split = (nx + 4) * (ny + 4)
+    shifted_into(wide_two, lines_ref[:split].astype(F32).reshape(nx + 4, ny + 4, PITCH, C))
     hidden_t = hidden_ref[...].reshape(-1, C).T
     kernel_grads(hidden_t, wide_two, 3, 3, nx, ny, scale, grads_ref, 1 - core)
     d_hidden = input_grads(wide_two, w_ref, 2, 2, nx + 2, ny + 2)
-    side = s_ref[...].astype(F32).reshape(-1, C)
+    side = lines_ref[split:].astype(F32).reshape(-1, C)
     slope = jnp.where(side > 0, 1.0, jnp.where(side < 0, slope_low, 0.0))
-    g_one = (d_hidden * slope).astype(BF16).reshape(s_ref.shape)
+    g_one = (d_hidden * slope).astype(BF16).reshape(nx + 2, ny + 2, PITCH, C)
     shifted_into(wide_one, g_one.astype(F32))
     g_one_ref[...] = wide_one[...]
     input_t = input_ref[...].reshape(-1, C).T
@@ -157,8 +146,27 @@
     return pl.BlockSpec(memory_space=pltpu.VMEM)
 
 
-def wide_weight(weight):
-    return weight.transpose(0, 1, 2, 4, 3).reshape(9, 3 * C, C)
+def place_kernel(core_ref, mine_ref, other_ref, one_ref, two_ref, sems):
+    n = one_ref.shape[0]
+    parts = sems.shape[1]
+    step = n // parts
+    for core, (one, two) in enumerate(((mine_ref, other_ref), (other_ref, mine_ref))):
+
+        @pl.when(core_ref[0] == core)
+        def _():
+            copies = []
+            for part in range(parts):
+                rows = pl.ds(part * step, step)
+                for i, (source, result) in enumerate(((one, one_ref), (two, two_ref))):
+                    copies.append(
+                        pltpu.make_async_copy(
+                            source.at[rows], result.at[rows], sems.at[i, part]
+                        )
+                    )
+            for copy in copies:
+                copy.start()
+            for copy in copies:
+                copy.wait()
 
 
 def spread(rows, axes):
@@ -167,6 +175,11 @@
     return lax.all_to_all(copies, axes, 0, 0, tiled=True)
 
 
+def scattered(rows, axis):
+    pieces = rows.reshape(lax.axis_size(axis), -1, C)
+    return lax.all_to_all(pieces, axis, 0, 0, tiled=True)
+
+
 def added(parts):
     return jnp.sum(parts.astype(F32), axis=0).astype(BF16)
 
@@ -174,21 +187,22 @@
 def reduced(grads):
     got = lax.ppermute(grads[1], "gc", [(0, 1), (1, 0)])
     mine = (grads[0].astype(F32) + got.astype(F32)).astype(BF16)
-    rows = mine.reshape(lax.axis_size(NEAR), -1, C)
-    share = added(lax.all_to_all(rows, NEAR, 0, 0, tiled=True))
+    share = added(scattered(mine.reshape(-1, C), "gx"))
+    share = added(scattered(share, "gw"))
     total = added(spread(share, FAR))
-    return spread(total, NEAR).reshape(grads.shape[1:])
+    total = spread(total, "gw").reshape(-1, C)
+    return spread(total, "gx").reshape(grads.shape[1:])
 
 
 def on_device(cells_all, layer_input, pre_one, pre_two, out_grad, weight_one, weight_two):
     nx, ny, nz, _ = layer_input.shape
-    core = lax.axis_index("gc")
+    core = lax.axis_index("gc").reshape(1).astype(jnp.int32)
     pre_one_f = pre_one.astype(F32)
     hidden = (pre_one_f * jnp.where(pre_one_f > 0, 1.0, slope_low)).astype(BF16)
     side = jnp.where(pre_one_f > 0, 1.0, -1.0).astype(BF16)
     slope_two = jnp.where(pre_two.astype(F32) > 0, 1.0, slope_low)
     g_two = (out_grad.astype(F32) * slope_two).astype(BF16)
-    g_two, side = extend(g_two, side)
+    lines = extend(g_two, side, core[0] == 1)
 
     taps_flops = 2 * 27 * C * C
     cells = nx * ny * PITCH
@@ -198,45 +212,51 @@
             jax.ShapeDtypeStruct((2, 28, C, C), BF16),
             jax.ShapeDtypeStruct((nx + 2, ny + 2, PITCH, 3 * C), BF16),
         ),
-        in_specs=[pl.BlockSpec(memory_space=pltpu.SMEM)] + [vmem()] * 5,
+        in_specs=[pl.BlockSpec(memory_space=pltpu.SMEM)] + [vmem()] * 4,
         out_specs=(vmem(), vmem()),
         scratch_shapes=[
             pltpu.VMEM((nx + 4, ny + 4, PITCH, 3 * C), BF16),
             pltpu.VMEM((nx + 2, ny + 2, PITCH, 3 * C), BF16),
         ],
-        compiler_params=pltpu.CompilerParams(vmem_limit_bytes=40 * 2**20),
+        compiler_params=pltpu.CompilerParams(vmem_limit_bytes=16 * 2**20),
         cost_estimate=pl.CostEstimate(
             flops=4 * cells * taps_flops, bytes_accessed=6 * 2**20, transcendentals=0
         ),
         name="kernel_gradients",
     )(
-        core.reshape(1).astype(jnp.int32),
-        g_two,
-        side,
+        core,
+        lines,
         pitched(hidden),
         pitched(layer_input),
-        wide_weight(weight_two),
+        weight_two.reshape(27, C, C),
     )
     input_grad = pl.pallas_call(
         input_kernel,
         out_shape=jax.ShapeDtypeStruct((nx, ny, nz, C), BF16),
         in_specs=[vmem()] * 2,
         out_specs=vmem(),
-        compiler_params=pltpu.CompilerParams(vmem_limit_bytes=40 * 2**20),
+        compiler_params=pltpu.CompilerParams(vmem_limit_bytes=8 * 2**20),
         cost_estimate=pl.CostEstimate(
             flops=cells * taps_flops, bytes_accessed=2 * 2**20, transcendentals=0
         ),
         name="input_gradient",
-    )(wide_one, wide_weight(weight_one))
+    )(wide_one, weight_one.reshape(27, C, C))
 
     mine = reduced(grads)
     other = lax.ppermute(mine, "gc", [(0, 1), (1, 0)])
-    first = core == 0
-    mine, other = mine[:27], other[:27]
+    total_type = jax.ShapeDtypeStruct((27, C, C), BF16)
+    grad_one, grad_two = pl.pallas_call(
+        place_kernel,
+        out_shape=(total_type, total_type),
+        in_specs=[pl.BlockSpec(memory_space=pltpu.SMEM)]
+        + [pl.BlockSpec(memory_space=pl.ANY)] * 2,
+        out_specs=(pl.BlockSpec(memory_space=pl.ANY),) * 2,
+        scratch_shapes=[pltpu.SemaphoreType.DMA((2, 9))],
+        compiler_params=pltpu.CompilerParams(vmem_limit_bytes=2**20),
+        name="place_totals",
+    )(core, mine, other)
     shape = weight_one.shape
-    grad_one = jnp.where(first, mine, other).reshape(shape)
-    grad_two = jnp.where(first, other, mine).reshape(shape)
-    return input_grad, grad_one, grad_two
+    return input_grad, grad_one.reshape(shape), grad_two.reshape(shape)
 
 
 def solution(mesh):

time: 138 us -> 123 us (0.89); the launches traced: 135 us -> 122 us
  blocking collectives: 81.4 us -> 72 us
  local copies, waits for them, and re-layouts: 4.22 us -> 0.47 us
  other arithmetic: 5.36 us -> 3.19 us
  Pallas kernels: 5.26 us -> 6.65 us
    ppermute x6 -> x4, starting transfers between devices: 22.9 us -> 12 us  [exchange(): return (lax.ppermute(up, axis, right), lax.ppermute(down, axis, left))]
    ppermute x0 -> x2, starting transfers between devices: none -> 10.4 us  [the longest x1 5.88 us: extend(): far = lax.ppermute(jnp.where(upper, last, first), Z, outer)]
    all_to_all x1 -> x2, blocking collectives: 42.1 us -> 35.5 us  [scattered(): return lax.all_to_all(pieces, axis, 0, 0, tiled=True)]
    all_to_all x2 -> x3, blocking collectives: 39.3 us -> 36.5 us  [spread(): return lax.all_to_all(copies, axes, 0, 0, tiled=True)]
    transpose x2 -> x0, local copies, waits for them, and re-layouts: 2.77 us -> none  [wide_weight(): return weight.transpose(0, 1, 2, 4, 3).reshape(9, 3 * C, C)]
    select_n x1 -> x3, other arithmetic: 2.49 us -> 0.21 us  [the longest x1 0.15 us: extend(): near = lax.ppermute(jnp.where(upper, first, last), Z, inner)]
  transfers between devices with their start and end apart: 8 -> 8, of which waited for: 3 -> 5; matrix products, arithmetic and copies ran while one was open for 2% -> 0% of each run, Pallas kernels for 1% -> 1%
where the time goes in v3:
time: 123 us; the launch traced here: 122 us
  blocking collectives  72 us (59%)
  starting transfers between devices  33.5 us (27%)
  Pallas kernels  6.65 us (5%)
  waiting for transfers between devices  5.39 us (4%)
  other arithmetic  3.19 us (3%)
    all_to_all x3, blocking collectives, spread(): return lax.all_to_all(copies, axes, 0, 0, tiled=True)  36.5 us
    all_to_all x2, blocking collectives, scattered(): return lax.all_to_all(pieces, axis, 0, 0, tiled=True)  35.5 us
    ppermute x4, starting transfers between devices, exchange(): return (lax.ppermute(up, axis, right), lax.ppermute(down, axis, left))  12 us
    ppermute x1, starting transfers between devices, on_device(): other = lax.ppermute(mine, 'gc', [(0, 1), (1, 0)])  8.83 us
    ppermute x1, starting transfers between devices, extend(): far = lax.ppermute(jnp.where(upper, last, first), Z, outer)  5.88 us
    ppermute x1, starting transfers between devices, extend(): near = lax.ppermute(jnp.where(upper, first, last), Z, inner)  4.5 us
    pallas_call x1, Pallas kernels, on_device(): pl.pallas_call(functools.partial(main_kernel, float(cells_all) ** (-0.5))...  3.58 us
  transfers between devices with their start and end apart: 8, of which 5 were waited for; matrix products, arithmetic and copies ran while one was open for 0% of the time, Pallas kernels for 1%

profile of v3, /device:TPU:1, one launch (start us, length us, event | category | flops | bytes accessed | tf_op | source)
XLA Modules:
  0.0 122.1 jit_solution(13347473795684139792)
XLA Ops:
  0.6 0.9 multiply_convert_fusion
  1.5 0.9 fusion.1
  2.4 0.0 copy-start.2
  2.5 1.3 %collective-permute-start.1 = (bf16[24,8,128]{2,1,0:T(8,128)(2,1)S(1)}, bf16[24,8,128]{2,1,0:T(8,128)(2,1)S(1)}, u32[]{:S(2)}, u32[]{:S(2)}) collective-permute-start(bf16[24,8,128]{2,1,0:T(8,128)(2,1)S(1)} %pad_maximum_fusion.5), channel_id=1, source_target_pairs={{128,0},{256,128},{384,256},{129,1},{257,129},{385,257},{130,2},{2... | collective-permute-start | bytes 147464 | tf_op jit(solution)/shard_map/ppermute | solution.py:24
  3.8 4.6 %collective-permute-start = (bf16[24,8,128]{2,1,0:T(8,128)(2,1)S(1)}, bf16[24,8,128]{2,1,0:T(8,128)(2,1)S(1)}, u32[]{:S(2)}, u32[]{:S(2)}) collective-permute-start(bf16[24,8,128]{2,1,0:T(8,128)(2,1)S(1)} %pad_maximum_fusion.4), channel_id=1, source_target_pairs={{0,128},{128,256},{256,384},{1,129},{129,257},{257,385},{2,130},{1... | collective-permute-start | bytes 147464 | tf_op jit(solution)/shard_map/ppermute | solution.py:24
  8.4 0.0 collective-permute-done.1
  8.4 1.1 collective-permute-done
  9.6 1.3 %collective-permute-start.3 = (bf16[22,8,128]{2,1,0:T(8,128)(2,1)S(1)}, bf16[22,8,128]{2,1,0:T(8,128)(2,1)S(1)}, u32[]{:S(2)}, u32[]{:S(2)}) collective-permute-start(bf16[22,8,128]{2,1,0:T(8,128)(2,1)S(1)} %pad_maximum_fusion.7), channel_id=1, source_target_pairs={{32,0},{64,32},{96,64},{33,1},{65,33},{97,65},{34,2},{66,34},{98,6... | collective-permute-start | bytes 135176 | tf_op jit(solution)/shard_map/ppermute | solution.py:24
  10.9 4.9 %collective-permute-start.2 = (bf16[22,8,128]{2,1,0:T(8,128)(2,1)S(1)}, bf16[22,8,128]{2,1,0:T(8,128)(2,1)S(1)}, u32[]{:S(2)}, u32[]{:S(2)}) collective-permute-start(bf16[22,8,128]{2,1,0:T(8,128)(2,1)S(1)} %pad_maximum_fusion.6), channel_id=1, source_target_pairs={{0,32},{32,64},{64,96},{1,33},{33,65},{65,97},{2,34},{34,66},{66,9... | collective-permute-start | bytes 135176 | tf_op jit(solution)/shard_map/ppermute | solution.py:24
  15.8 0.0 collective-permute-done.3
  15.8 1.1 collective-permute-done.2
  17.0 0.0 copy-start.1
  17.0 0.1 broadcast_select_fusion.3
  17.2 5.9 %collective-permute-start.5 = (bf16[156,2,128]{2,1,0:T(2,128)(2,1)S(1)}, bf16[156,2,128]{2,1,0:T(2,128)(2,1)S(1)}, u32[]{:S(2)}, u32[]{:S(2)}) collective-permute-start(bf16[156,2,128]{2,1,0:T(2,128)(2,1)S(1)} %bitcast.78), channel_id=1, source_target_pairs={{1,2},{2,1},{3,4},{4,3},{5,6},{6,5},{7,8},{8,7},{9,10},{10,9},{11,... | collective-permute-start | bytes 239624 | tf_op jit(solution)/shard_map/ppermute | solution.py:62
  23.1 4.5 %collective-permute-start.4 = (bf16[156,2,128]{2,1,0:T(2,128)(2,1)S(1)}, bf16[156,2,128]{2,1,0:T(2,128)(2,1)S(1)}, u32[]{:S(2)}, u32[]{:S(2)}) collective-permute-start(bf16[156,2,128]{2,1,0:T(2,128)(2,1)S(1)} %get-tuple-element.11), channel_id=1, source_target_pairs={{0,1},{1,0},{2,3},{3,2},{4,5},{5,4},{6,7},{7,6},{8,9},{9,8},{10,11... | collective-permute-start | bytes 239624 | tf_op jit(solution)/shard_map/ppermute | solution.py:63
  27.6 0.0 copy-done.2
  27.7 0.1 pad.13.clone
  27.8 0.0 collective-permute-done.5
  27.8 0.7 collective-permute-done.4
  28.5 0.5 maximum_maximum_fusion.lines_ref
  29.0 0.0 copy-done.1
  29.0 3.6 %kernel_gradients.1 = (bf16[2,28,128,128]{3,2,1,0:T(8,128)(2,1)S(1)}, bf16[6,10,16,384]{3,2,1,0:T(8,128)(2,1)S(1)}) custom-call(s32[1]{0:T(128)} %bitcast.core_ref, bf16[156,16,128]{2,1,0:T(8,128)(2,1)S(1)} %maximum_maximum_fusion.lines_ref, bf16[4,8,16,128]{3,2,1,0:T(8,128)(2,1)S(1)} %pad.7.hidden_ref, bf16[4,8,16,128]{3,2,1,0:T(8,128)(2,1)S(1)} %pad.8.input_ref, ...), custom_call_target="tpu_custom_call" | custom-call | flops 1811939328 | bytes 6291456 | tf_op jit(solution)/shard_map/kernel_gradients/pallas_call | solution.py:209
  32.6 0.1 slice_bitcast_fusion
  32.7 2.3 %collective-permute-start.6 = (bf16[28,128,128]{2,1,0:T(8,128)(2,1)S(1)}, bf16[28,128,128]{2,1,0:T(8,128)(2,1)S(1)}, u32[]{:S(2)}, u32[]{:S(2)}) collective-permute-start(bf16[28,128,128]{2,1,0:T(8,128)(2,1)S(1)} %slice_bitcast_fusion), channel_id=1, source_target_pairs={{0,1},{1,0},{2,3},{3,2},{4,5},{5,4},{6,7},{7,6},{8,9},{9,8},{10,11... | collective-permute-start | bytes 2752520 | tf_op jit(solution)/shard_map/ppermute | solution.py:188
  35.0 2.1 %collective-permute-done.6 = bf16[28,128,128]{2,1,0:T(8,128)(2,1)S(1)} collective-permute-done((bf16[28,128,128]{2,1,0:T(8,128)(2,1)S(1)}, bf16[28,128,128]{2,1,0:T(8,128)(2,1)S(1)}, u32[]{:S(2)}, u32[]{:S(2)}) %collective-permute-start.6) | collective-permute-done | bytes 917536 | tf_op jit(solution)/shard_map/ppermute | solution.py:188
  37.1 0.3 fusion
  37.4 16.0 %all_to_all.25 = bf16[4,896,128]{2,1,0:T(8,128)(2,1)S(1)} all-to-all(bf16[4,896,128]{2,1,0:T(8,128)(2,1)S(1)} %bitcast.55), channel_id=1, replica_groups=mesh['gx'=4,'gy'=4,'gh'=2,'gw'=8,'gc'=2] {'gx'}, dimensions={0} | all-to-all | bytes 1835008 | tf_op jit(solution)/shard_map/all_to_all | solution.py:180
  53.4 0.2 reduce_sum.36
  53.7 19.4 %all_to_all.26 = bf16[8,112,128]{2,1,0:T(8,128)(2,1)S(1)} all-to-all(bf16[8,112,128]{2,1,0:T(8,128)(2,1)S(1)} %bitcast.60), channel_id=1, replica_groups=mesh['gx'=4,'gy'=4,'gh'=2,'gw'=8,'gc'=2] {'gw'}, dimensions={0} | all-to-all | bytes 458752 | tf_op jit(solution)/shard_map/all_to_all | solution.py:180
  73.2 13.5 %all_to_all.27 = bf16[8,112,128]{2,1,0:T(8,128)(2,1)S(1)} all-to-all(bf16[8,112,128]{2,1,0:T(8,128)(2,1)S(1)} %broadcast_in_dim.40), channel_id=1, replica_groups=mesh['gx'=4,'gy'=4,'gh'=2,'gw'=8,'gc'=2] {'gy','gh'}, dimensions={0} | all-to-all | bytes 458752 | tf_op jit(solution)/shard_map/all_to_all | solution.py:175
  86.8 11.4 %all_to_all.28 = bf16[8,112,128]{2,1,0:T(8,128)(2,1)S(1)} all-to-all(bf16[8,112,128]{2,1,0:T(8,128)(2,1)S(1)} %broadcast_in_dim.41), channel_id=1, replica_groups=mesh['gx'=4,'gy'=4,'gh'=2,'gw'=8,'gc'=2] {'gw'}, dimensions={0} | all-to-all | bytes 458752 | tf_op jit(solution)/shard_map/all_to_all | solution.py:175
  98.2 0.0 copy-start
  98.2 0.1 broadcast_in_dim.43
  98.3 11.6 %all_to_all.29 = bf16[4,896,128]{2,1,0:T(8,128)(2,1)S(1)} all-to-all(bf16[4,896,128]{2,1,0:T(8,128)(2,1)S(1)} %broadcast_in_dim.43), channel_id=1, replica_groups=mesh['gx'=4,'gy'=4,'gh'=2,'gw'=8,'gc'=2] {'gx'}, dimensions={0} | all-to-all | bytes 1835008 | tf_op jit(solution)/shard_map/all_to_all | solution.py:175
  109.9 8.8 %collective-permute-start.7 = (bf16[28,128,128]{2,1,0:T(8,128)(2,1)S(1)}, bf16[28,128,128]{2,1,0:T(8,128)(2,1)S(1)}, u32[]{:S(2)}, u32[]{:S(2)}) collective-permute-start(bf16[28,128,128]{2,1,0:T(8,128)(2,1)S(1)} %bitcast.51), channel_id=1, source_target_pairs={{0,1},{1,0},{2,3},{3,2},{4,5},{5,4},{6,7},{7,6},{8,9},{9,8},{10,11... | collective-permute-start | bytes 2752520 | tf_op jit(solution)/shard_map/ppermute | solution.py:246
  118.7 0.0 copy-done
  118.7 1.7 %input_gradient.1 = bf16[4,8,8,128]{3,2,1,0:T(8,128)(2,1)} custom-call(bf16[6,10,16,384]{3,2,1,0:T(8,128)(2,1)S(1)} %get-tuple-element.7.wide_ref, bf16[27,128,128]{2,1,0:T(8,128)(2,1)S(1)} %bitcast.53), custom_call_target="tpu_custom_call" | custom-call | flops 452984832 | bytes 2097152 | tf_op jit(solution)/shard_map/input_gradient/pallas_call | solution.py:233
  120.5 0.3 collective-permute-done.7.other_ref
  120.8 1.3 %place_totals.1 = (bf16[27,128,128]{2,1,0:T(8,128)(2,1)}, bf16[27,128,128]{2,1,0:T(8,128)(2,1)}) custom-call(s32[1]{0:T(128)} %bitcast.core_ref, bf16[28,128,128]{2,1,0:T(8,128)(2,1)S(1)} %bitcast.52, bf16[28,128,128]{2,1,0:T(8,128)(2,1)S(1)} %collective-permute-done.7.other_ref), custom_call_target="tpu_custom_call" | custom-call | tf_op jit(solution)/shard_map/place_totals/pallas_call | solution.py:248
  (27 shorter events, 0.4 us)
Async XLA Ops:
  2.4 25.2 %copy-start.2 = (bf16[4,8,8,128]{3,2,1,0:T(8,128)(2,1)S(1)}, bf16[4,8,8,128]{3,2,1,0:T(8,128)(2,1)}, u32[]{:S(2)}) copy-start(bf16[4,8,8,128]{3,2,1,0:T(8,128)(2,1)} %param.6) | copy-start | bytes 196612
  2.5 5.9 %collective-permute-start.1 = (bf16[24,8,128]{2,1,0:T(8,128)(2,1)S(1)}, bf16[24,8,128]{2,1,0:T(8,128)(2,1)S(1)}, u32[]{:S(2)}, u32[]{:S(2)}) collective-permute-start(bf16[24,8,128]{2,1,0:T(8,128)(2,1)S(1)} %pad_maximum_fusion.5), channel_id=1, source_target_pairs={{128,0},{256,128},{384,256},{129,1},{257,129},{385,257},{130,2},{2... | collective-permute-start | bytes 147464 | tf_op jit(solution)/shard_map/ppermute | solution.py:24
  3.8 5.7 %collective-permute-start = (bf16[24,8,128]{2,1,0:T(8,128)(2,1)S(1)}, bf16[24,8,128]{2,1,0:T(8,128)(2,1)S(1)}, u32[]{:S(2)}, u32[]{:S(2)}) collective-permute-start(bf16[24,8,128]{2,1,0:T(8,128)(2,1)S(1)} %pad_maximum_fusion.4), channel_id=1, source_target_pairs={{0,128},{128,256},{256,384},{1,129},{129,257},{257,385},{2,130},{1... | collective-permute-start | bytes 147464 | tf_op jit(solution)/shard_map/ppermute | solution.py:24
  9.6 6.2 %collective-permute-start.3 = (bf16[22,8,128]{2,1,0:T(8,128)(2,1)S(1)}, bf16[22,8,128]{2,1,0:T(8,128)(2,1)S(1)}, u32[]{:S(2)}, u32[]{:S(2)}) collective-permute-start(bf16[22,8,128]{2,1,0:T(8,128)(2,1)S(1)} %pad_maximum_fusion.7), channel_id=1, source_target_pairs={{32,0},{64,32},{96,64},{33,1},{65,33},{97,65},{34,2},{66,34},{98,6... | collective-permute-start | bytes 135176 | tf_op jit(solution)/shard_map/ppermute | solution.py:24
  10.9 6.0 %collective-permute-start.2 = (bf16[22,8,128]{2,1,0:T(8,128)(2,1)S(1)}, bf16[22,8,128]{2,1,0:T(8,128)(2,1)S(1)}, u32[]{:S(2)}, u32[]{:S(2)}) collective-permute-start(bf16[22,8,128]{2,1,0:T(8,128)(2,1)S(1)} %pad_maximum_fusion.6), channel_id=1, source_target_pairs={{0,32},{32,64},{64,96},{1,33},{33,65},{65,97},{2,34},{34,66},{66,9... | collective-permute-start | bytes 135176 | tf_op jit(solution)/shard_map/ppermute | solution.py:24
  17.0 12.0 %copy-start.1 = (bf16[3,3,3,128,128]{4,3,2,1,0:T(8,128)(2,1)S(1)}, bf16[3,3,3,128,128]{4,3,2,1,0:T(8,128)(2,1)}, u32[]{:S(2)}) copy-start(bf16[3,3,3,128,128]{4,3,2,1,0:T(8,128)(2,1)} %param.11) | copy-start | bytes 2654212
  17.2 10.6 %collective-permute-start.5 = (bf16[156,2,128]{2,1,0:T(2,128)(2,1)S(1)}, bf16[156,2,128]{2,1,0:T(2,128)(2,1)S(1)}, u32[]{:S(2)}, u32[]{:S(2)}) collective-permute-start(bf16[156,2,128]{2,1,0:T(2,128)(2,1)S(1)} %bitcast.78), channel_id=1, source_target_pairs={{1,2},{2,1},{3,4},{4,3},{5,6},{6,5},{7,8},{8,7},{9,10},{10,9},{11,... | collective-permute-start | bytes 239624 | tf_op jit(solution)/shard_map/ppermute | solution.py:62
  23.1 5.4 %collective-permute-start.4 = (bf16[156,2,128]{2,1,0:T(2,128)(2,1)S(1)}, bf16[156,2,128]{2,1,0:T(2,128)(2,1)S(1)}, u32[]{:S(2)}, u32[]{:S(2)}) collective-permute-start(bf16[156,2,128]{2,1,0:T(2,128)(2,1)S(1)} %get-tuple-element.11), channel_id=1, source_target_pairs={{0,1},{1,0},{2,3},{3,2},{4,5},{5,4},{6,7},{7,6},{8,9},{9,8},{10,11... | collective-permute-start | bytes 239624 | tf_op jit(solution)/shard_map/ppermute | solution.py:63
  32.7 4.4 %collective-permute-start.6 = (bf16[28,128,128]{2,1,0:T(8,128)(2,1)S(1)}, bf16[28,128,128]{2,1,0:T(8,128)(2,1)S(1)}, u32[]{:S(2)}, u32[]{:S(2)}) collective-permute-start(bf16[28,128,128]{2,1,0:T(8,128)(2,1)S(1)} %slice_bitcast_fusion), channel_id=1, source_target_pairs={{0,1},{1,0},{2,3},{3,2},{4,5},{5,4},{6,7},{7,6},{8,9},{9,8},{10,11... | collective-permute-start | bytes 2752520 | tf_op jit(solution)/shard_map/ppermute | solution.py:188
  98.2 20.6 %copy-start = (bf16[3,3,3,128,128]{4,3,2,1,0:T(8,128)(2,1)S(1)}, bf16[3,3,3,128,128]{4,3,2,1,0:T(8,128)(2,1)}, u32[]{:S(2)}) copy-start(bf16[3,3,3,128,128]{4,3,2,1,0:T(8,128)(2,1)} %param.10) | copy-start | bytes 2654212
  109.9 10.9 %collective-permute-start.7 = (bf16[28,128,128]{2,1,0:T(8,128)(2,1)S(1)}, bf16[28,128,128]{2,1,0:T(8,128)(2,1)S(1)}, u32[]{:S(2)}, u32[]{:S(2)}) collective-permute-start(bf16[28,128,128]{2,1,0:T(8,128)(2,1)S(1)} %bitcast.51), channel_id=1, source_target_pairs={{0,1},{1,0},{2,3},{3,2},{4,5},{5,4},{6,7},{7,6},{8,9},{9,8},{10,11... | collective-permute-start | bytes 2752520 | tf_op jit(solution)/shard_map/ppermute | solution.py:246

commit v4 on v3

v4 whole, which is shorter than its diff:
```python
import functools

import jax
import jax.numpy as jnp
from jax import lax
from jax.experimental import pallas as pl
from jax.experimental.pallas import tpu as pltpu
from jax.sharding import Mesh
from jax.sharding import PartitionSpec as P

slope_low = 0.3
Z = ("gh", "gw", "gc")
RING = ("gy", "gh")
C = 128
GROUP = 2
PITCH = 16
F32 = jnp.float32
BF16 = jnp.bfloat16


def exchange(up, down, axis):
    peers = lax.axis_size(axis)
    right = [(i, i + 1) for i in range(peers - 1)]
    left = [(i + 1, i) for i in range(peers - 1)]
    return lax.ppermute(up, axis, right), lax.ppermute(down, axis, left)


def pack(g, s):
    lines = g.shape[2]
    return jnp.concatenate(
        [g.reshape(-1, lines, C), s.reshape(-1, lines, C)], axis=0
    )


def unpack(rows, g_shape, s_shape):
    n = g_shape[0] * g_shape[1]
    return rows[:n].reshape(g_shape), rows[n:].reshape(s_shape)


def extend(g, s, upper):
    nx, ny, nz, _ = g.shape
    up, down = exchange(pack(g[-2:], s[-1:]), pack(g[:2], s[:1]), "gx")
    shapes = ((2, ny, nz, C), (1, ny, nz, C))
    (g_lo, s_lo), (g_hi, s_hi) = unpack(up, *shapes), unpack(down, *shapes)
    g = jnp.concatenate([g_lo, g, g_hi], axis=0)
    s = jnp.concatenate([s_lo, s, s_hi], axis=0)

    up, down = exchange(
        pack(g[:, -2:], s[:, -1:]), pack(g[:, :2], s[:, :1]), "gy"
    )
    shapes = ((nx + 4, 2, nz, C), (nx + 2, 1, nz, C))
    (g_lo, s_lo), (g_hi, s_hi) = unpack(up, *shapes), unpack(down, *shapes)
    g = jnp.concatenate([g_lo, g, g_hi], axis=1)
    s = jnp.concatenate([s_lo, s, s_hi], axis=1)

    lines = pack(g, s)
    last, first = lines[:, -2:], lines[:, :2]
    outer, inner = [], []
    for i in range(1, lax.axis_size(Z) - 1, 2):
        outer += [(i, i + 1), (i + 1, i)]
    for i in range(0, lax.axis_size(Z), 2):
        inner += [(i, i + 1), (i + 1, i)]
    far = lax.ppermute(jnp.where(upper, last, first), Z, outer)
    near = lax.ppermute(jnp.where(upper, first, last), Z, inner)
    lo, hi = jnp.where(upper, near, far), jnp.where(upper, far, near)
    rest = jnp.zeros((lines.shape[0], PITCH - nz - 4, C), BF16)
    return jnp.concatenate([lo, lines, hi, rest], axis=1)


def paired(cells):
    half = cells.shape[1] // 2
    return jnp.concatenate([cells[:, :half], cells[:, half:]], axis=2)


def moved(rows, by):
    n = rows.shape[0]
    return rows if by == 0 else pltpu.roll(rows, (n - by) % n, 0)


def wide_into(out_ref, cells):
    rows = cells.reshape(-1, C)
    for k in range(3):
        out_ref[..., k * C : (k + 1) * C] = (
            moved(rows, 1 - k).astype(BF16).reshape(cells.shape)
        )


def pairs_into(out_ref, cells, first):
    nx, ny = cells.shape[:2]
    rows = cells.reshape(-1, C)
    held = out_ref.shape[1]
    half = held - 2
    for k in range(3):
        lines = moved(rows, 3 - k).reshape(nx, ny, PITCH, C)[:, :, : PITCH // 2]
        low = lines[:, first : first + held]
        high = lines[:, first + half : first + half + held]
        out_ref[..., k * C : (k + 1) * C] = jnp.concatenate(
            [low, high], axis=2
        ).astype(BF16)


def taps():
    return [(a, b) for a in range(3) for b in range(3)]


def window(ref, tap, nx, ny):
    a, b = tap
    return ref[2 - a : 2 - a + nx, 2 - b : 2 - b + ny].reshape(nx * ny * PITCH, 3 * C)


def kernel_grads(act_t, ref, scale, out_ref, slot):
    nx, half = ref.shape[0] - 2, ref.shape[1] - 2
    for t, tap in enumerate(taps()):
        part = jnp.dot(
            act_t, window(ref, tap, nx, half), preferred_element_type=F32
        )
        part = (part * scale).astype(BF16)
        for k in range(3):
            out_ref[slot, t * 3 + k] = part[:, k * C : (k + 1) * C]


def input_grads(ref, w_ref, nx, ny):
    total = None
    for group in range(0, 9, GROUP):
        numbers = range(group, min(group + GROUP, 9))
        cells = [window(ref, taps()[t], nx, ny) for t in numbers]
        weights = [w_ref[3 * t + k] for t in numbers for k in range(3)]
        part = lax.dot_general(
            jnp.concatenate(cells, axis=1),
            jnp.concatenate(weights, axis=1),
            (((1,), (1,)), ((), ())),
            preferred_element_type=F32,
        )
        total = part if total is None else total + part
    return total


def main_kernel(
    scale, core_ref, lines_ref, hidden_ref, input_ref, w_ref, grads_ref, pair_one, wide, pair_two
):
    core = core_ref[0]
    nx, half = hidden_ref.shape[:2]
    ny = 2 * half
    split = (nx + 4) * (ny + 4)
    lines = lines_ref[:split].astype(F32).reshape(nx + 4, ny + 4, PITCH, C)
    wide_into(wide, lines)
    pairs_into(pair_two, lines[1 : nx + 3], 1)
    d_hidden = input_grads(wide, w_ref, nx + 2, ny + 2)
    side = lines_ref[split:].astype(F32).reshape(-1, C)
    slope = jnp.where(side > 0, 1.0, jnp.where(side < 0, slope_low, 0.0))
    g_one = (d_hidden * slope).astype(BF16).astype(F32)
    pairs_into(pair_one, g_one.reshape(nx + 2, ny + 2, PITCH, C), 0)
    hidden_t = hidden_ref[...].reshape(-1, C).T
    kernel_grads(hidden_t, pair_two, scale, grads_ref, 1 - core)
    input_t = input_ref[...].reshape(-1, C).T
    kernel_grads(input_t, pair_one, scale, grads_ref, core)


def input_kernel(core_ref, pair_ref, w_ref, mine_ref, out_ref, one_ref, two_ref, sems):
    def start(target):
        for copy in chunks(mine_ref, target, sems):
            copy.start()

    def finish(target):
        for copy in chunks(mine_ref, target, sems):
            copy.wait()

    on_core(core_ref, one_ref, two_ref, start)
    nx, ny, nz, _ = out_ref.shape
    half = ny // 2
    total = input_grads(pair_ref, w_ref, nx, half)
    total = total.reshape(nx, half, PITCH, C).astype(BF16)
    out_ref[:, :half] = total[:, :, :nz]
    out_ref[:, half:] = total[:, :, nz:]
    on_core(core_ref, one_ref, two_ref, finish)


def vmem():
    return pl.BlockSpec(memory_space=pltpu.VMEM)


def chunks(source, target, sems):
    step = target.shape[0] // sems.shape[0]
    copies = []
    for part in range(sems.shape[0]):
        rows = pl.ds(part * step, step)
        copies.append(
            pltpu.make_async_copy(source.at[rows], target.at[rows], sems.at[part])
        )
    return copies


def on_core(core_ref, first, second, act):
    for core, target in enumerate((first, second)):

        @pl.when(core_ref[0] == core)
        def _():
            act(target)


def place_kernel(core_ref, other_ref, _, __, one_ref, two_ref, sems):
    def run(target):
        copies = chunks(other_ref, target, sems)
        for copy in copies:
            copy.start()
        for copy in copies:
            copy.wait()

    on_core(core_ref, two_ref, one_ref, run)


def spread(rows, axes):
    peers = lax.axis_size(axes)
    copies = jnp.broadcast_to(rows[None], (peers,) + rows.shape)
    return lax.all_to_all(copies, axes, 0, 0, tiled=True)


def scattered(rows, axis):
    pieces = rows.reshape(lax.axis_size(axis), -1, C)
    return lax.all_to_all(pieces, axis, 0, 0, tiled=True)


def added(parts):
    return jnp.sum(parts.astype(F32), axis=0).astype(BF16)


def reduced(grads):
    got = lax.ppermute(grads[1], "gc", [(0, 1), (1, 0)])
    mine = (grads[0].astype(F32) + got.astype(F32)).astype(BF16)
    share = added(scattered(mine.reshape(-1, C), "gx"))
    used = share.shape[0]
    rest = -used % (lax.axis_size(RING) * PITCH)
    share = added(scattered(jnp.pad(share, ((0, rest), (0, 0))), RING))
    total = added(spread(share, "gw"))
    total = spread(total, RING).reshape(-1, C)[:used]
    return spread(total, "gx").reshape(grads.shape[1:])


def on_device(cells_all, layer_input, pre_one, pre_two, out_grad, weight_one, weight_two):
    nx, ny, nz, _ = layer_input.shape
    core = lax.axis_index("gc").reshape(1).astype(jnp.int32)
    pre_one_f = pre_one.astype(F32)
    hidden = (pre_one_f * jnp.where(pre_one_f > 0, 1.0, slope_low)).astype(BF16)
    side = jnp.where(pre_one_f > 0, 1.0, -1.0).astype(BF16)
    slope_two = jnp.where(pre_two.astype(F32) > 0, 1.0, slope_low)
    g_two = (out_grad.astype(F32) * slope_two).astype(BF16)
    both = lax.optimization_barrier(jnp.concatenate([g_two, side], axis=0))
    g_two, side = both[:nx], both[nx:]
    lines = extend(g_two, side, core[0] == 1)

    taps_flops = 2 * 27 * C * C
    cells = nx * ny * nz
    pair_type = (nx + 2, ny // 2 + 2, PITCH, 3 * C)
    grads, pair_one = pl.pallas_call(
        functools.partial(main_kernel, float(cells_all) ** -0.5),
        out_shape=(
            jax.ShapeDtypeStruct((2, 27, C, C), BF16),
            jax.ShapeDtypeStruct(pair_type, BF16),
        ),
        in_specs=[pl.BlockSpec(memory_space=pltpu.SMEM)] + [vmem()] * 4,
        out_specs=(vmem(), vmem()),
        scratch_shapes=[
            pltpu.VMEM((nx + 4, ny + 4, PITCH, 3 * C), BF16),
            pltpu.VMEM(pair_type, BF16),
        ],
        compiler_params=pltpu.CompilerParams(vmem_limit_bytes=16 * 2**20),
        cost_estimate=pl.CostEstimate(
            flops=4 * cells * taps_flops, bytes_accessed=6 * 2**20, transcendentals=0
        ),
        name="kernel_gradients",
    )(
        core,
        lines,
        paired(hidden),
        paired(layer_input),
        weight_two.reshape(27, C, C),
    )
    mine = reduced(grads)
    other = lax.ppermute(mine, "gc", [(0, 1), (1, 0)])
    smem = pl.BlockSpec(memory_space=pltpu.SMEM)
    anywhere = pl.BlockSpec(memory_space=pl.ANY)
    total_type = jax.ShapeDtypeStruct((27, C, C), BF16)
    input_grad, grad_one, grad_two = pl.pallas_call(
        input_kernel,
        out_shape=(
            jax.ShapeDtypeStruct((nx, ny, nz, C), BF16),
            total_type,
            total_type,
        ),
        in_specs=[smem, vmem(), vmem(), anywhere],
        out_specs=(vmem(), anywhere, anywhere),
        scratch_shapes=[pltpu.SemaphoreType.DMA((9,))],
        compiler_params=pltpu.CompilerParams(vmem_limit_bytes=8 * 2**20),
        cost_estimate=pl.CostEstimate(
            flops=cells * taps_flops, bytes_accessed=2 * 2**20, transcendentals=0
        ),
        name="input_gradient",
    )(core, pair_one, weight_one.reshape(27, C, C), mine)
    grad_one, grad_two = pl.pallas_call(
        place_kernel,
        out_shape=(total_type, total_type),
        in_specs=[smem] + [anywhere] * 3,
        out_specs=(anywhere, anywhere),
        scratch_shapes=[pltpu.SemaphoreType.DMA((9,))],
        input_output_aliases={2: 0, 3: 1},
        compiler_params=pltpu.CompilerParams(vmem_limit_bytes=2**20),
        name="place_totals",
    )(core, other, grad_one, grad_two)
    shape = weight_one.shape
    return input_grad, grad_one.reshape(shape), grad_two.reshape(shape)


def solution(mesh):
    sizes = mesh.devices.shape
    cores, rows = 2, sizes[2] // 4
    devices = mesh.devices.reshape(sizes[0], sizes[1], 2, rows, cores)
    fine = Mesh(devices, ("gx", "gy", "gh", "gw", "gc"))
    split = P("gx", "gy", Z, None)

    def whole(*arrays):
        cells_all = 1
        for size in arrays[0].shape[:3]:
            cells_all *= size
        return jax.shard_map(
            functools.partial(on_device, cells_all),
            mesh=fine,
            in_specs=(split, split, split, split, P(), P()),
            out_specs=(split, P(), P()),
            check_vma=False,
        )(*arrays)

    return whole
```

time: 123 us -> 120 us (0.976)
    all_to_all x3, blocking collectives: 36.5 us -> 33.4 us  [spread(): return lax.all_to_all(copies, axes, 0, 0, tiled=True)]
    all_to_all x2, blocking collectives: 35.5 us -> 37.5 us  [scattered(): return lax.all_to_all(pieces, axis, 0, 0, tiled=True)]
  transfers between devices with their start and end apart: 8 -> 8, of which waited for: 5 -> 4; matrix products, arithmetic and copies ran while one was open for 0% -> 0% of each run, Pallas kernels for 1% -> 2%
where the time goes in v4:
time: 120 us; the launch traced here: 119 us
  blocking collectives  70.9 us (59%)
  starting transfers between devices  33.1 us (28%)
  Pallas kernels  6.46 us (5%)
  waiting for transfers between devices  5 us (4%)
  other arithmetic  2.41 us (2%)
    all_to_all x2, blocking collectives, scattered(): return lax.all_to_all(pieces, axis, 0, 0, tiled=True)  37.5 us
    all_to_all x3, blocking collectives, spread(): return lax.all_to_all(copies, axes, 0, 0, tiled=True)  33.4 us
    ppermute x4, starting transfers between devices, exchange(): return (lax.ppermute(up, axis, right), lax.ppermute(down, axis, left))  12 us
    ppermute x1, starting transfers between devices, on_device(): other = lax.ppermute(mine, 'gc', [(0, 1), (1, 0)])  8.38 us
    ppermute x1, starting transfers between devices, extend(): far = lax.ppermute(jnp.where(upper, last, first), Z, outer)  5.88 us
    ppermute x1, starting transfers between devices, extend(): near = lax.ppermute(jnp.where(upper, first, last), Z, inner)  4.5 us
    pallas_call x1, Pallas kernels, on_device(): pl.pallas_call(functools.partial(main_kernel, float(cells_all) ** (-0.5))...  3.34 us
  transfers between devices with their start and end apart: 8, of which 4 were waited for; matrix products, arithmetic and copies ran while one was open for 0% of the time, Pallas kernels for 2%

profile of v4, /device:TPU:1, one launch (start us, length us, event | category | flops | bytes accessed | tf_op | source)
XLA Modules:
  0.0 119.3 jit_solution(218482400038420824)
XLA Ops:
  0.6 0.0 copy-start.2
  0.6 1.0 fusion.1
  1.7 1.3 %collective-permute-start.1 = (bf16[24,8,128]{2,1,0:T(8,128)(2,1)S(1)}, bf16[24,8,128]{2,1,0:T(8,128)(2,1)S(1)}, u32[]{:S(2)}, u32[]{:S(2)}) collective-permute-start(bf16[24,8,128]{2,1,0:T(8,128)(2,1)S(1)} %pad_maximum_fusion.8), channel_id=1, source_target_pairs={{128,0},{256,128},{384,256},{129,1},{257,129},{385,257},{130,2},{2... | collective-permute-start | bytes 147464 | tf_op jit(solution)/shard_map/ppermute | solution.py:25
  3.0 4.6 %collective-permute-start = (bf16[24,8,128]{2,1,0:T(8,128)(2,1)S(1)}, bf16[24,8,128]{2,1,0:T(8,128)(2,1)S(1)}, u32[]{:S(2)}, u32[]{:S(2)}) collective-permute-start(bf16[24,8,128]{2,1,0:T(8,128)(2,1)S(1)} %pad_maximum_fusion.7), channel_id=1, source_target_pairs={{0,128},{128,256},{256,384},{1,129},{129,257},{257,385},{2,130},{1... | collective-permute-start | bytes 147464 | tf_op jit(solution)/shard_map/ppermute | solution.py:25
  7.6 0.0 copy-done.2
  7.7 0.0 collective-permute-done.1
  7.7 1.1 collective-permute-done
  8.8 1.3 %collective-permute-start.3 = (bf16[22,8,128]{2,1,0:T(8,128)(2,1)S(1)}, bf16[22,8,128]{2,1,0:T(8,128)(2,1)S(1)}, u32[]{:S(2)}, u32[]{:S(2)}) collective-permute-start(bf16[22,8,128]{2,1,0:T(8,128)(2,1)S(1)} %pad_maximum_fusion.10), channel_id=1, source_target_pairs={{32,0},{64,32},{96,64},{33,1},{65,33},{97,65},{34,2},{66,34},{98,6... | collective-permute-start | bytes 135176 | tf_op jit(solution)/shard_map/ppermute | solution.py:25
  10.1 4.9 %collective-permute-start.2 = (bf16[22,8,128]{2,1,0:T(8,128)(2,1)S(1)}, bf16[22,8,128]{2,1,0:T(8,128)(2,1)S(1)}, u32[]{:S(2)}, u32[]{:S(2)}) collective-permute-start(bf16[22,8,128]{2,1,0:T(8,128)(2,1)S(1)} %pad_maximum_fusion.9), channel_id=1, source_target_pairs={{0,32},{32,64},{64,96},{1,33},{33,65},{65,97},{2,34},{34,66},{66,9... | collective-permute-start | bytes 135176 | tf_op jit(solution)/shard_map/ppermute | solution.py:25
  15.1 0.1 pad.13.clone
  15.1 0.0 collective-permute-done.3
  15.1 1.0 collective-permute-done.2
  16.2 0.0 copy-start.1
  16.3 0.1 broadcast_select_fusion.3
  16.4 5.9 %collective-permute-start.5 = (bf16[156,2,128]{2,1,0:T(2,128)(2,1)S(1)}, bf16[156,2,128]{2,1,0:T(2,128)(2,1)S(1)}, u32[]{:S(2)}, u32[]{:S(2)}) collective-permute-start(bf16[156,2,128]{2,1,0:T(2,128)(2,1)S(1)} %bitcast.80), channel_id=1, source_target_pairs={{1,2},{2,1},{3,4},{4,3},{5,6},{6,5},{7,8},{8,7},{9,10},{10,9},{11,... | collective-permute-start | bytes 239624 | tf_op jit(solution)/shard_map/ppermute | solution.py:63
  22.3 4.5 %collective-permute-start.4 = (bf16[156,2,128]{2,1,0:T(2,128)(2,1)S(1)}, bf16[156,2,128]{2,1,0:T(2,128)(2,1)S(1)}, u32[]{:S(2)}, u32[]{:S(2)}) collective-permute-start(bf16[156,2,128]{2,1,0:T(2,128)(2,1)S(1)} %get-tuple-element.17), channel_id=1, source_target_pairs={{0,1},{1,0},{2,3},{3,2},{4,5},{5,4},{6,7},{7,6},{8,9},{9,8},{10,11... | collective-permute-start | bytes 239624 | tf_op jit(solution)/shard_map/ppermute | solution.py:64
  26.9 0.0 collective-permute-done.5
  26.9 0.9 collective-permute-done.4
  27.8 0.5 maximum_maximum_fusion.lines_ref
  28.3 0.0 copy-done.1
  28.3 3.3 %kernel_gradients.1 = (bf16[2,27,128,128]{3,2,1,0:T(8,128)(2,1)S(1)}, bf16[6,6,16,384]{3,2,1,0:T(8,128)(2,1)S(1)}) custom-call(s32[1]{0:T(128)} %bitcast.core_ref, bf16[156,16,128]{2,1,0:T(8,128)(2,1)S(1)} %maximum_maximum_fusion.lines_ref, bf16[4,4,16,128]{3,2,1,0:T(8,128)(2,1)S(1)} %pad_maximum_fusion.5.hidden_ref, ...), custom_call_target="tpu_custom_call" | custom-call | flops 905969664 | bytes 6291456 | tf_op jit(solution)/shard_map/kernel_gradients/pallas_call | solution.py:254
  31.6 0.1 slice_bitcast_fusion
  31.7 2.3 %collective-permute-start.6 = (bf16[27,128,128]{2,1,0:T(8,128)(2,1)S(1)}, bf16[27,128,128]{2,1,0:T(8,128)(2,1)S(1)}, u32[]{:S(2)}, u32[]{:S(2)}) collective-permute-start(bf16[27,128,128]{2,1,0:T(8,128)(2,1)S(1)} %slice_bitcast_fusion), channel_id=1, source_target_pairs={{0,1},{1,0},{2,3},{3,2},{4,5},{5,4},{6,7},{7,6},{8,9},{9,8},{10,11... | collective-permute-start | bytes 2654216 | tf_op jit(solution)/shard_map/ppermute | solution.py:228
  34.0 2.0 %collective-permute-done.6 = bf16[27,128,128]{2,1,0:T(8,128)(2,1)S(1)} collective-permute-done((bf16[27,128,128]{2,1,0:T(8,128)(2,1)S(1)}, bf16[27,128,128]{2,1,0:T(8,128)(2,1)S(1)}, u32[]{:S(2)}, u32[]{:S(2)}) %collective-permute-start.6) | collective-permute-done | bytes 884768 | tf_op jit(solution)/shard_map/ppermute | solution.py:228
  36.0 0.3 fusion
  36.3 15.7 %all_to_all.25 = bf16[4,864,128]{2,1,0:T(8,128)(2,1)S(1)} all-to-all(bf16[4,864,128]{2,1,0:T(8,128)(2,1)S(1)} %bitcast.55), channel_id=1, replica_groups=mesh['gx'=4,'gy'=4,'gh'=2,'gw'=8,'gc'=2] {'gx'}, dimensions={0} | all-to-all | bytes 1769472 | tf_op jit(solution)/shard_map/all_to_all | solution.py:220
  52.0 0.2 reduce_sum.36
  52.3 21.7 %all_to_all.26 = bf16[8,112,128]{2,1,0:T(8,128)(2,1)S(1)} all-to-all(bf16[8,112,128]{2,1,0:T(8,128)(2,1)S(1)} %bitcast.60), channel_id=1, replica_groups=mesh['gx'=4,'gy'=4,'gh'=2,'gw'=8,'gc'=2] {'gy','gh'}, dimensions={0} | all-to-all | bytes 458752 | tf_op jit(solution)/shard_map/all_to_all | solution.py:220
  74.1 11.4 %all_to_all.27 = bf16[8,112,128]{2,1,0:T(8,128)(2,1)S(1)} all-to-all(bf16[8,112,128]{2,1,0:T(8,128)(2,1)S(1)} %broadcast_in_dim.39), channel_id=1, replica_groups=mesh['gx'=4,'gy'=4,'gh'=2,'gw'=8,'gc'=2] {'gw'}, dimensions={0} | all-to-all | bytes 458752 | tf_op jit(solution)/shard_map/all_to_all | solution.py:215
  85.6 10.6 %all_to_all.28 = bf16[8,112,128]{2,1,0:T(8,128)(2,1)S(1)} all-to-all(bf16[8,112,128]{2,1,0:T(8,128)(2,1)S(1)} %broadcast_in_dim.40), channel_id=1, replica_groups=mesh['gx'=4,'gy'=4,'gh'=2,'gw'=8,'gc'=2] {'gy','gh'}, dimensions={0} | all-to-all | bytes 458752 | tf_op jit(solution)/shard_map/all_to_all | solution.py:215
  96.2 0.0 copy-start
  96.2 0.1 broadcast_in_dim.41
  96.4 11.4 %all_to_all.29 = bf16[4,864,128]{2,1,0:T(8,128)(2,1)S(1)} all-to-all(bf16[4,864,128]{2,1,0:T(8,128)(2,1)S(1)} %broadcast_in_dim.41), channel_id=1, replica_groups=mesh['gx'=4,'gy'=4,'gh'=2,'gw'=8,'gc'=2] {'gx'}, dimensions={0} | all-to-all | bytes 1769472 | tf_op jit(solution)/shard_map/all_to_all | solution.py:215
  107.8 8.4 %collective-permute-start.7 = (bf16[27,128,128]{2,1,0:T(8,128)(2,1)S(1)}, bf16[27,128,128]{2,1,0:T(8,128)(2,1)S(1)}, u32[]{:S(2)}, u32[]{:S(2)}) collective-permute-start(bf16[27,128,128]{2,1,0:T(8,128)(2,1)S(1)} %bitcast.51), channel_id=1, source_target_pairs={{0,1},{1,0},{2,3},{3,2},{4,5},{5,4},{6,7},{7,6},{8,9},{9,8},{10,11... | collective-permute-start | bytes 2654216 | tf_op jit(solution)/shard_map/ppermute | solution.py:279
  116.2 0.0 copy-done
  116.2 2.1 %input_gradient.1 = (bf16[4,8,8,128]{3,2,1,0:T(8,128)(2,1)}, bf16[27,128,128]{2,1,0:T(8,128)(2,1)}, bf16[27,128,128]{2,1,0:T(8,128)(2,1)}) custom-call(s32[1]{0:T(128)} %bitcast.core_ref, bf16[6,6,16,384]{3,2,1,0:T(8,128)(2,1)S(1)} %get-tuple-element.10.pair_ref, bf16[27,128,128]{2,1,0:T(8,128)(2,1)S(1)} %bitcast.53, bf16[27,128,128]{2,1,0:T(8,128)(2,1)S(1)} %bitcast.52), custom_call_target="tpu_custom_call" | custom-call | flops 226492416 | bytes 2097152 | tf_op jit(solution)/shard_map/input_gradient/pallas_call | solution.py:283
  118.3 0.0 collective-permute-done.7.other_ref
  118.3 1.0 place_totals.1
  (33 shorter events, 0.5 us)
Async XLA Ops:
  0.6 7.0 %copy-start.2 = (bf16[4,8,8,128]{3,2,1,0:T(8,128)(2,1)S(1)}, bf16[4,8,8,128]{3,2,1,0:T(8,128)(2,1)}, u32[]{:S(2)}) copy-start(bf16[4,8,8,128]{3,2,1,0:T(8,128)(2,1)} %param.6) | copy-start | bytes 196612
  1.7 6.0 %collective-permute-start.1 = (bf16[24,8,128]{2,1,0:T(8,128)(2,1)S(1)}, bf16[24,8,128]{2,1,0:T(8,128)(2,1)S(1)}, u32[]{:S(2)}, u32[]{:S(2)}) collective-permute-start(bf16[24,8,128]{2,1,0:T(8,128)(2,1)S(1)} %pad_maximum_fusion.8), channel_id=1, source_target_pairs={{128,0},{256,128},{384,256},{129,1},{257,129},{385,257},{130,2},{2... | collective-permute-start | bytes 147464 | tf_op jit(solution)/shard_map/ppermute | solution.py:25
  3.0 5.7 %collective-permute-start = (bf16[24,8,128]{2,1,0:T(8,128)(2,1)S(1)}, bf16[24,8,128]{2,1,0:T(8,128)(2,1)S(1)}, u32[]{:S(2)}, u32[]{:S(2)}) collective-permute-start(bf16[24,8,128]{2,1,0:T(8,128)(2,1)S(1)} %pad_maximum_fusion.7), channel_id=1, source_target_pairs={{0,128},{128,256},{256,384},{1,129},{129,257},{257,385},{2,130},{1... | collective-permute-start | bytes 147464 | tf_op jit(solution)/shard_map/ppermute | solution.py:25
  8.8 6.3 %collective-permute-start.3 = (bf16[22,8,128]{2,1,0:T(8,128)(2,1)S(1)}, bf16[22,8,128]{2,1,0:T(8,128)(2,1)S(1)}, u32[]{:S(2)}, u32[]{:S(2)}) collective-permute-start(bf16[22,8,128]{2,1,0:T(8,128)(2,1)S(1)} %pad_maximum_fusion.10), channel_id=1, source_target_pairs={{32,0},{64,32},{96,64},{33,1},{65,33},{97,65},{34,2},{66,34},{98,6... | collective-permute-start | bytes 135176 | tf_op jit(solution)/shard_map/ppermute | solution.py:25
  10.1 6.0 %collective-permute-start.2 = (bf16[22,8,128]{2,1,0:T(8,128)(2,1)S(1)}, bf16[22,8,128]{2,1,0:T(8,128)(2,1)S(1)}, u32[]{:S(2)}, u32[]{:S(2)}) collective-permute-start(bf16[22,8,128]{2,1,0:T(8,128)(2,1)S(1)} %pad_maximum_fusion.9), channel_id=1, source_target_pairs={{0,32},{32,64},{64,96},{1,33},{33,65},{65,97},{2,34},{34,66},{66,9... | collective-permute-start | bytes 135176 | tf_op jit(solution)/shard_map/ppermute | solution.py:25
  16.2 12.1 %copy-start.1 = (bf16[3,3,3,128,128]{4,3,2,1,0:T(8,128)(2,1)S(1)}, bf16[3,3,3,128,128]{4,3,2,1,0:T(8,128)(2,1)}, u32[]{:S(2)}) copy-start(bf16[3,3,3,128,128]{4,3,2,1,0:T(8,128)(2,1)} %param.11) | copy-start | bytes 2654212
  16.4 10.4 %collective-permute-start.5 = (bf16[156,2,128]{2,1,0:T(2,128)(2,1)S(1)}, bf16[156,2,128]{2,1,0:T(2,128)(2,1)S(1)}, u32[]{:S(2)}, u32[]{:S(2)}) collective-permute-start(bf16[156,2,128]{2,1,0:T(2,128)(2,1)S(1)} %bitcast.80), channel_id=1, source_target_pairs={{1,2},{2,1},{3,4},{4,3},{5,6},{6,5},{7,8},{8,7},{9,10},{10,9},{11,... | collective-permute-start | bytes 239624 | tf_op jit(solution)/shard_map/ppermute | solution.py:63
  22.3 5.4 %collective-permute-start.4 = (bf16[156,2,128]{2,1,0:T(2,128)(2,1)S(1)}, bf16[156,2,128]{2,1,0:T(2,128)(2,1)S(1)}, u32[]{:S(2)}, u32[]{:S(2)}) collective-permute-start(bf16[156,2,128]{2,1,0:T(2,128)(2,1)S(1)} %get-tuple-element.17), channel_id=1, source_target_pairs={{0,1},{1,0},{2,3},{3,2},{4,5},{5,4},{6,7},{7,6},{8,9},{9,8},{10,11... | collective-permute-start | bytes 239624 | tf_op jit(solution)/shard_map/ppermute | solution.py:64
  31.7 4.3 %collective-permute-start.6 = (bf16[27,128,128]{2,1,0:T(8,128)(2,1)S(1)}, bf16[27,128,128]{2,1,0:T(8,128)(2,1)S(1)}, u32[]{:S(2)}, u32[]{:S(2)}) collective-permute-start(bf16[27,128,128]{2,1,0:T(8,128)(2,1)S(1)} %slice_bitcast_fusion), channel_id=1, source_target_pairs={{0,1},{1,0},{2,3},{3,2},{4,5},{5,4},{6,7},{7,6},{8,9},{9,8},{10,11... | collective-permute-start | bytes 2654216 | tf_op jit(solution)/shard_map/ppermute | solution.py:228
  96.2 19.9 %copy-start = (bf16[3,3,3,128,128]{4,3,2,1,0:T(8,128)(2,1)S(1)}, bf16[3,3,3,128,128]{4,3,2,1,0:T(8,128)(2,1)}, u32[]{:S(2)}) copy-start(bf16[3,3,3,128,128]{4,3,2,1,0:T(8,128)(2,1)} %param.10) | copy-start | bytes 2654212
  107.8 10.5 %collective-permute-start.7 = (bf16[27,128,128]{2,1,0:T(8,128)(2,1)S(1)}, bf16[27,128,128]{2,1,0:T(8,128)(2,1)S(1)}, u32[]{:S(2)}, u32[]{:S(2)}) collective-permute-start(bf16[27,128,128]{2,1,0:T(8,128)(2,1)S(1)} %bitcast.51), channel_id=1, source_target_pairs={{0,1},{1,0},{2,3},{3,2},{4,5},{5,4},{6,7},{7,6},{8,9},{9,8},{10,11... | collective-permute-start | bytes 2654216 | tf_op jit(solution)/shard_map/ppermute | solution.py:279

commit v5 on v4

--- a/solution.py
+++ b/solution.py
@@ -7,12 +7,13 @@
 from jax.experimental.pallas import tpu as pltpu
 from jax.sharding import Mesh
 from jax.sharding import PartitionSpec as P
+import numpy as np
 
 slope_low = 0.3
 Z = ("gh", "gw", "gc")
-RING = ("gy", "gh")
+EVERY = ("gx", "gy", "gh", "gw", "gc")
 C = 128
-GROUP = 2
+GROUP = 9
 PITCH = 16
 F32 = jnp.float32
 BF16 = jnp.bfloat16
@@ -135,6 +136,37 @@
     return total
 
 
+def two_planes(ref, w_ref, nx, ny):
+    plane = ny * PITCH
+    parts = [None] * nx
+    rest = None
+    for b in range(3):
+        weights = [
+            jnp.concatenate([w_ref[(a * 3 + b) * 3 + k] for k in range(3)], axis=1)
+            for a in range(3)
+        ]
+        cells = ref[1:, 2 - b : 2 - b + ny].reshape(-1, 3 * C)
+        both = lax.dot_general(
+            cells,
+            jnp.concatenate(weights[:2], axis=0),
+            (((1,), (1,)), ((), ())),
+            preferred_element_type=F32,
+        )
+        for x in range(nx):
+            for a in range(2):
+                first = (x + 1 - a) * plane
+                part = both[first : first + plane, a * C : (a + 1) * C]
+                parts[x] = part if parts[x] is None else parts[x] + part
+        last = lax.dot_general(
+            window(ref, (2, b), nx, ny),
+            weights[2],
+            (((1,), (1,)), ((), ())),
+            preferred_element_type=F32,
+        )
+        rest = last if rest is None else rest + last
+    return jnp.concatenate(parts, axis=0) + rest
+
+
 def main_kernel(
     scale, core_ref, lines_ref, hidden_ref, input_ref, w_ref, grads_ref, pair_one, wide, pair_two
 ):
@@ -145,7 +177,7 @@
     lines = lines_ref[:split].astype(F32).reshape(nx + 4, ny + 4, PITCH, C)
     wide_into(wide, lines)
     pairs_into(pair_two, lines[1 : nx + 3], 1)
-    d_hidden = input_grads(wide, w_ref, nx + 2, ny + 2)
+    d_hidden = two_planes(wide, w_ref, nx + 2, ny + 2)
     side = lines_ref[split:].astype(F32).reshape(-1, C)
     slope = jnp.where(side > 0, 1.0, jnp.where(side < 0, slope_low, 0.0))
     g_one = (d_hidden * slope).astype(BF16).astype(F32)
@@ -209,15 +241,38 @@
     on_core(core_ref, two_ref, one_ref, run)
 
 
-def spread(rows, axes):
-    peers = lax.axis_size(axes)
-    copies = jnp.broadcast_to(rows[None], (peers,) + rows.shape)
-    return lax.all_to_all(copies, axes, 0, 0, tiled=True)
-
-
-def scattered(rows, axis):
-    pieces = rows.reshape(lax.axis_size(axis), -1, C)
-    return lax.all_to_all(pieces, axis, 0, 0, tiled=True)
+def steps():
+    sizes = [lax.axis_size(axis) for axis in EVERY]
+    number = np.arange(np.prod(sizes)).reshape(sizes)
+    nx, ny, nh, nw, _ = sizes
+
+    def groups(devices, axes):
+        size = np.prod([devices.shape[axis] for axis in axes])
+        last = range(devices.ndim - len(axes), devices.ndim)
+        return np.moveaxis(devices, axes, last).reshape(-1, size)
+
+    zero = number[..., 0]
+    one = number[..., 1].reshape(nx, ny // 2, 2, nh, nw // 2, 2)
+    near = groups(zero, (0,)), groups(one, (2, 5))
+    ring = groups(zero, (1, 2)), groups(one, (0, 1))
+    far = groups(zero, (3,)), groups(one, (3, 4))
+    return [np.concatenate(both).tolist() for both in (near, ring, far)]
+
+
+def exchanged(pieces, groups):
+    return lax.all_to_all(
+        pieces, EVERY, 0, 0, axis_index_groups=groups, tiled=True
+    )
+
+
+def spread(rows, groups):
+    return exchanged(
+        jnp.broadcast_to(rows[None], (len(groups[0]),) + rows.shape), groups
+    )
+
+
+def scattered(rows, groups):
+    return exchanged(rows.reshape(len(groups[0]), -1, C), groups)
 
 
 def added(parts):
@@ -227,13 +282,14 @@
 def reduced(grads):
     got = lax.ppermute(grads[1], "gc", [(0, 1), (1, 0)])
     mine = (grads[0].astype(F32) + got.astype(F32)).astype(BF16)
-    share = added(scattered(mine.reshape(-1, C), "gx"))
+    near, ring, far = steps()
+    share = added(scattered(mine.reshape(-1, C), near))
     used = share.shape[0]
-    rest = -used % (lax.axis_size(RING) * PITCH)
-    share = added(scattered(jnp.pad(share, ((0, rest), (0, 0))), RING))
-    total = added(spread(share, "gw"))
-    total = spread(total, RING).reshape(-1, C)[:used]
-    return spread(total, "gx").reshape(grads.shape[1:])
+    rest = -used % (len(ring[0]) * PITCH)
+    share = added(scattered(jnp.pad(share, ((0, rest), (0, 0))), ring))
+    total = added(spread(share, far))
+    total = spread(total, ring).reshape(-1, C)[:used]
+    return spread(total, near).reshape(grads.shape[1:])
 
 
 def on_device(cells_all, layer_input, pre_one, pre_two, out_grad, weight_one, weight_two):

time: 120 us -> 118 us (0.983)
  starting transfers between devices: 33.1 us -> 28.3 us
  blocking collectives: 70.9 us -> 75.1 us
    ppermute x1, starting transfers between devices: 8.38 us -> 3.63 us  [on_device(): other = lax.ppermute(mine, 'gc', [(0, 1), (1, 0)])]
    all_to_all x5, blocking collectives: 70.9 us -> 75.1 us  [exchanged(): lax.all_to_all(pieces, EVERY, 0, 0, axis_index_groups=groups, tiled=True)]
where the time goes in v5:
time: 118 us
  blocking collectives  75.1 us (64%)
  starting transfers between devices  28.3 us (24%)
  Pallas kernels  5.57 us (5%)
  waiting for transfers between devices  5 us (4%)
  other arithmetic  2.41 us (2%)
    all_to_all x5, blocking collectives, exchanged(): lax.all_to_all(pieces, EVERY, 0, 0, axis_index_groups=groups, tiled=True)  75.1 us
    ppermute x4, starting transfers between devices, exchange(): return (lax.ppermute(up, axis, right), lax.ppermute(down, axis, left))  12 us
    ppermute x1, starting transfers between devices, extend(): far = lax.ppermute(jnp.where(upper, last, first), Z, outer)  5.88 us
    ppermute x1, starting transfers between devices, extend(): near = lax.ppermute(jnp.where(upper, first, last), Z, inner)  4.5 us
    ppermute x1, starting transfers between devices, on_device(): other = lax.ppermute(mine, 'gc', [(0, 1), (1, 0)])  3.63 us
    pallas_call x1, Pallas kernels, on_device(): pl.pallas_call(functools.partial(main_kernel, float(cells_all) ** (-0.5))...  2.48 us
  transfers between devices with their start and end apart: 8, of which 4 were waited for; matrix products, arithmetic and copies ran while one was open for 0% of the time, Pallas kernels for 2%

profile of v5, /device:TPU:1, one launch (start us, length us, event | category | flops | bytes accessed | tf_op | source)
XLA Modules:
  0.0 117.9 jit_solution(4457467808911500608)
XLA Ops:
  0.6 0.0 copy-start.2
  0.6 1.0 fusion.1
  1.7 1.3 %collective-permute-start.1 = (bf16[24,8,128]{2,1,0:T(8,128)(2,1)S(1)}, bf16[24,8,128]{2,1,0:T(8,128)(2,1)S(1)}, u32[]{:S(2)}, u32[]{:S(2)}) collective-permute-start(bf16[24,8,128]{2,1,0:T(8,128)(2,1)S(1)} %pad_maximum_fusion.8), channel_id=1, source_target_pairs={{128,0},{256,128},{384,256},{129,1},{257,129},{385,257},{130,2},{2... | collective-permute-start | bytes 147464 | tf_op jit(solution)/shard_map/ppermute | solution.py:26
  3.0 4.6 %collective-permute-start = (bf16[24,8,128]{2,1,0:T(8,128)(2,1)S(1)}, bf16[24,8,128]{2,1,0:T(8,128)(2,1)S(1)}, u32[]{:S(2)}, u32[]{:S(2)}) collective-permute-start(bf16[24,8,128]{2,1,0:T(8,128)(2,1)S(1)} %pad_maximum_fusion.7), channel_id=1, source_target_pairs={{0,128},{128,256},{256,384},{1,129},{129,257},{257,385},{2,130},{1... | collective-permute-start | bytes 147464 | tf_op jit(solution)/shard_map/ppermute | solution.py:26
  7.6 0.0 copy-done.2
  7.7 0.0 collective-permute-done.1
  7.7 1.1 collective-permute-done
  8.8 1.3 %collective-permute-start.3 = (bf16[22,8,128]{2,1,0:T(8,128)(2,1)S(1)}, bf16[22,8,128]{2,1,0:T(8,128)(2,1)S(1)}, u32[]{:S(2)}, u32[]{:S(2)}) collective-permute-start(bf16[22,8,128]{2,1,0:T(8,128)(2,1)S(1)} %pad_maximum_fusion.10), channel_id=1, source_target_pairs={{32,0},{64,32},{96,64},{33,1},{65,33},{97,65},{34,2},{66,34},{98,6... | collective-permute-start | bytes 135176 | tf_op jit(solution)/shard_map/ppermute | solution.py:26
  10.1 4.9 %collective-permute-start.2 = (bf16[22,8,128]{2,1,0:T(8,128)(2,1)S(1)}, bf16[22,8,128]{2,1,0:T(8,128)(2,1)S(1)}, u32[]{:S(2)}, u32[]{:S(2)}) collective-permute-start(bf16[22,8,128]{2,1,0:T(8,128)(2,1)S(1)} %pad_maximum_fusion.9), channel_id=1, source_target_pairs={{0,32},{32,64},{64,96},{1,33},{33,65},{65,97},{2,34},{34,66},{66,9... | collective-permute-start | bytes 135176 | tf_op jit(solution)/shard_map/ppermute | solution.py:26
  15.1 0.1 pad.13.clone
  15.1 0.0 collective-permute-done.3
  15.1 1.0 collective-permute-done.2
  16.2 0.0 copy-start.1
  16.3 0.1 broadcast_select_fusion.3
  16.4 5.9 %collective-permute-start.5 = (bf16[156,2,128]{2,1,0:T(2,128)(2,1)S(1)}, bf16[156,2,128]{2,1,0:T(2,128)(2,1)S(1)}, u32[]{:S(2)}, u32[]{:S(2)}) collective-permute-start(bf16[156,2,128]{2,1,0:T(2,128)(2,1)S(1)} %bitcast.80), channel_id=1, source_target_pairs={{1,2},{2,1},{3,4},{4,3},{5,6},{6,5},{7,8},{8,7},{9,10},{10,9},{11,... | collective-permute-start | bytes 239624 | tf_op jit(solution)/shard_map/ppermute | solution.py:64
  22.3 4.5 %collective-permute-start.4 = (bf16[156,2,128]{2,1,0:T(2,128)(2,1)S(1)}, bf16[156,2,128]{2,1,0:T(2,128)(2,1)S(1)}, u32[]{:S(2)}, u32[]{:S(2)}) collective-permute-start(bf16[156,2,128]{2,1,0:T(2,128)(2,1)S(1)} %get-tuple-element.17), channel_id=1, source_target_pairs={{0,1},{1,0},{2,3},{3,2},{4,5},{5,4},{6,7},{7,6},{8,9},{9,8},{10,11... | collective-permute-start | bytes 239624 | tf_op jit(solution)/shard_map/ppermute | solution.py:65
  26.9 0.0 collective-permute-done.5
  26.9 0.9 collective-permute-done.4
  27.8 0.5 maximum_maximum_fusion.lines_ref
  28.3 0.0 copy-done.1
  28.3 2.5 %kernel_gradients.1 = (bf16[2,27,128,128]{3,2,1,0:T(8,128)(2,1)S(1)}, bf16[6,6,16,384]{3,2,1,0:T(8,128)(2,1)S(1)}) custom-call(s32[1]{0:T(128)} %bitcast.core_ref, bf16[156,16,128]{2,1,0:T(8,128)(2,1)S(1)} %maximum_maximum_fusion.lines_ref, bf16[4,4,16,128]{3,2,1,0:T(8,128)(2,1)S(1)} %pad_maximum_fusion.5.hidden_ref, ...), custom_call_target="tpu_custom_call" | custom-call | flops 905969664 | bytes 6291456 | tf_op jit(solution)/shard_map/kernel_gradients/pallas_call | solution.py:310
  30.8 0.1 slice_bitcast_fusion
  30.8 2.3 %collective-permute-start.6 = (bf16[27,128,128]{2,1,0:T(8,128)(2,1)S(1)}, bf16[27,128,128]{2,1,0:T(8,128)(2,1)S(1)}, u32[]{:S(2)}, u32[]{:S(2)}) collective-permute-start(bf16[27,128,128]{2,1,0:T(8,128)(2,1)S(1)} %slice_bitcast_fusion), channel_id=1, source_target_pairs={{0,1},{1,0},{2,3},{3,2},{4,5},{5,4},{6,7},{7,6},{8,9},{9,8},{10,11... | collective-permute-start | bytes 2654216 | tf_op jit(solution)/shard_map/ppermute | solution.py:283
  33.1 2.0 %collective-permute-done.6 = bf16[27,128,128]{2,1,0:T(8,128)(2,1)S(1)} collective-permute-done((bf16[27,128,128]{2,1,0:T(8,128)(2,1)S(1)}, bf16[27,128,128]{2,1,0:T(8,128)(2,1)S(1)}, u32[]{:S(2)}, u32[]{:S(2)}) %collective-permute-start.6) | collective-permute-done | bytes 884768 | tf_op jit(solution)/shard_map/ppermute | solution.py:283
  35.2 0.3 fusion
  35.5 11.4 %all_to_all.25 = bf16[4,864,128]{2,1,0:T(8,128)(2,1)S(1)} all-to-all(bf16[4,864,128]{2,1,0:T(8,128)(2,1)S(1)} %bitcast.55), channel_id=1, replica_groups={{0,128,256,384},{2,130,258,386},{4,132,260,388},{6,134,262,390},{8,136,..., dimensions={0} | all-to-all | bytes 1769472 | tf_op jit(solution)/shard_map/all_to_all | solution.py:263
  46.9 0.2 reduce_sum.36
  47.1 14.7 %all_to_all.26 = bf16[8,112,128]{2,1,0:T(8,128)(2,1)S(1)} all-to-all(bf16[8,112,128]{2,1,0:T(8,128)(2,1)S(1)} %bitcast.60), channel_id=1, replica_groups={{0,16,32,48,64,80,96,112},{2,18,34,50,66,82,98,114},{4,20,36,52,68,84,1..., dimensions={0} | all-to-all | bytes 458752 | tf_op jit(solution)/shard_map/all_to_all | solution.py:263
  61.9 27.4 %all_to_all.27 = bf16[8,112,128]{2,1,0:T(8,128)(2,1)S(1)} all-to-all(bf16[8,112,128]{2,1,0:T(8,128)(2,1)S(1)} %broadcast_in_dim.39), channel_id=1, replica_groups={{0,2,4,6,8,10,12,14},{16,18,20,22,24,26,28,30},{32,34,36,38,40,42,44,46..., dimensions={0} | all-to-all | bytes 458752 | tf_op jit(solution)/shard_map/all_to_all | solution.py:263
  89.4 10.7 %all_to_all.28 = bf16[8,112,128]{2,1,0:T(8,128)(2,1)S(1)} all-to-all(bf16[8,112,128]{2,1,0:T(8,128)(2,1)S(1)} %broadcast_in_dim.40), channel_id=1, replica_groups={{0,16,32,48,64,80,96,112},{2,18,34,50,66,82,98,114},{4,20,36,52,68,84,1..., dimensions={0} | all-to-all | bytes 458752 | tf_op jit(solution)/shard_map/all_to_all | solution.py:263
  100.1 0.0 copy-start
  100.1 0.1 broadcast_in_dim.41
  100.3 10.8 %all_to_all.29 = bf16[4,864,128]{2,1,0:T(8,128)(2,1)S(1)} all-to-all(bf16[4,864,128]{2,1,0:T(8,128)(2,1)S(1)} %broadcast_in_dim.41), channel_id=1, replica_groups={{0,128,256,384},{2,130,258,386},{4,132,260,388},{6,134,262,390},{8,136,..., dimensions={0} | all-to-all | bytes 1769472 | tf_op jit(solution)/shard_map/all_to_all | solution.py:263
  111.1 3.6 %collective-permute-start.7 = (bf16[27,128,128]{2,1,0:T(8,128)(2,1)S(1)}, bf16[27,128,128]{2,1,0:T(8,128)(2,1)S(1)}, u32[]{:S(2)}, u32[]{:S(2)}) collective-permute-start(bf16[27,128,128]{2,1,0:T(8,128)(2,1)S(1)} %bitcast.51), channel_id=1, source_target_pairs={{0,1},{1,0},{2,3},{3,2},{4,5},{5,4},{6,7},{7,6},{8,9},{9,8},{10,11... | collective-permute-start | bytes 2654216 | tf_op jit(solution)/shard_map/ppermute | solution.py:335
  114.7 0.0 copy-done
  114.7 2.1 %input_gradient.1 = (bf16[4,8,8,128]{3,2,1,0:T(8,128)(2,1)}, bf16[27,128,128]{2,1,0:T(8,128)(2,1)}, bf16[27,128,128]{2,1,0:T(8,128)(2,1)}) custom-call(s32[1]{0:T(128)} %bitcast.core_ref, bf16[6,6,16,384]{3,2,1,0:T(8,128)(2,1)S(1)} %get-tuple-element.10.pair_ref, bf16[27,128,128]{2,1,0:T(8,128)(2,1)S(1)} %bitcast.53, bf16[27,128,128]{2,1,0:T(8,128)(2,1)S(1)} %bitcast.52), custom_call_target="tpu_custom_call" | custom-call | flops 226492416 | bytes 2097152 | tf_op jit(solution)/shard_map/input_gradient/pallas_call | solution.py:339
  116.8 0.0 collective-permute-done.7.other_ref
  116.9 1.0 place_totals.1
  (33 shorter events, 0.5 us)
Async XLA Ops:
  0.6 7.0 %copy-start.2 = (bf16[4,8,8,128]{3,2,1,0:T(8,128)(2,1)S(1)}, bf16[4,8,8,128]{3,2,1,0:T(8,128)(2,1)}, u32[]{:S(2)}) copy-start(bf16[4,8,8,128]{3,2,1,0:T(8,128)(2,1)} %param.6) | copy-start | bytes 196612
  1.7 6.0 %collective-permute-start.1 = (bf16[24,8,128]{2,1,0:T(8,128)(2,1)S(1)}, bf16[24,8,128]{2,1,0:T(8,128)(2,1)S(1)}, u32[]{:S(2)}, u32[]{:S(2)}) collective-permute-start(bf16[24,8,128]{2,1,0:T(8,128)(2,1)S(1)} %pad_maximum_fusion.8), channel_id=1, source_target_pairs={{128,0},{256,128},{384,256},{129,1},{257,129},{385,257},{130,2},{2... | collective-permute-start | bytes 147464 | tf_op jit(solution)/shard_map/ppermute | solution.py:26
  3.0 5.7 %collective-permute-start = (bf16[24,8,128]{2,1,0:T(8,128)(2,1)S(1)}, bf16[24,8,128]{2,1,0:T(8,128)(2,1)S(1)}, u32[]{:S(2)}, u32[]{:S(2)}) collective-permute-start(bf16[24,8,128]{2,1,0:T(8,128)(2,1)S(1)} %pad_maximum_fusion.7), channel_id=1, source_target_pairs={{0,128},{128,256},{256,384},{1,129},{129,257},{257,385},{2,130},{1... | collective-permute-start | bytes 147464 | tf_op jit(solution)/shard_map/ppermute | solution.py:26
  8.8 6.3 %collective-permute-start.3 = (bf16[22,8,128]{2,1,0:T(8,128)(2,1)S(1)}, bf16[22,8,128]{2,1,0:T(8,128)(2,1)S(1)}, u32[]{:S(2)}, u32[]{:S(2)}) collective-permute-start(bf16[22,8,128]{2,1,0:T(8,128)(2,1)S(1)} %pad_maximum_fusion.10), channel_id=1, source_target_pairs={{32,0},{64,32},{96,64},{33,1},{65,33},{97,65},{34,2},{66,34},{98,6... | collective-permute-start | bytes 135176 | tf_op jit(solution)/shard_map/ppermute | solution.py:26
  10.1 6.0 %collective-permute-start.2 = (bf16[22,8,128]{2,1,0:T(8,128)(2,1)S(1)}, bf16[22,8,128]{2,1,0:T(8,128)(2,1)S(1)}, u32[]{:S(2)}, u32[]{:S(2)}) collective-permute-start(bf16[22,8,128]{2,1,0:T(8,128)(2,1)S(1)} %pad_maximum_fusion.9), channel_id=1, source_target_pairs={{0,32},{32,64},{64,96},{1,33},{33,65},{65,97},{2,34},{34,66},{66,9... | collective-permute-start | bytes 135176 | tf_op jit(solution)/shard_map/ppermute | solution.py:26
  16.2 12.1 %copy-start.1 = (bf16[3,3,3,128,128]{4,3,2,1,0:T(8,128)(2,1)S(1)}, bf16[3,3,3,128,128]{4,3,2,1,0:T(8,128)(2,1)}, u32[]{:S(2)}) copy-start(bf16[3,3,3,128,128]{4,3,2,1,0:T(8,128)(2,1)} %param.11) | copy-start | bytes 2654212
  16.4 10.4 %collective-permute-start.5 = (bf16[156,2,128]{2,1,0:T(2,128)(2,1)S(1)}, bf16[156,2,128]{2,1,0:T(2,128)(2,1)S(1)}, u32[]{:S(2)}, u32[]{:S(2)}) collective-permute-start(bf16[156,2,128]{2,1,0:T(2,128)(2,1)S(1)} %bitcast.80), channel_id=1, source_target_pairs={{1,2},{2,1},{3,4},{4,3},{5,6},{6,5},{7,8},{8,7},{9,10},{10,9},{11,... | collective-permute-start | bytes 239624 | tf_op jit(solution)/shard_map/ppermute | solution.py:64
  22.3 5.4 %collective-permute-start.4 = (bf16[156,2,128]{2,1,0:T(2,128)(2,1)S(1)}, bf16[156,2,128]{2,1,0:T(2,128)(2,1)S(1)}, u32[]{:S(2)}, u32[]{:S(2)}) collective-permute-start(bf16[156,2,128]{2,1,0:T(2,128)(2,1)S(1)} %get-tuple-element.17), channel_id=1, source_target_pairs={{0,1},{1,0},{2,3},{3,2},{4,5},{5,4},{6,7},{7,6},{8,9},{9,8},{10,11... | collective-permute-start | bytes 239624 | tf_op jit(solution)/shard_map/ppermute | solution.py:65
  30.8 4.3 %collective-permute-start.6 = (bf16[27,128,128]{2,1,0:T(8,128)(2,1)S(1)}, bf16[27,128,128]{2,1,0:T(8,128)(2,1)S(1)}, u32[]{:S(2)}, u32[]{:S(2)}) collective-permute-start(bf16[27,128,128]{2,1,0:T(8,128)(2,1)S(1)} %slice_bitcast_fusion), channel_id=1, source_target_pairs={{0,1},{1,0},{2,3},{3,2},{4,5},{5,4},{6,7},{7,6},{8,9},{9,8},{10,11... | collective-permute-start | bytes 2654216 | tf_op jit(solution)/shard_map/ppermute | solution.py:283
  100.1 14.6 %copy-start = (bf16[3,3,3,128,128]{4,3,2,1,0:T(8,128)(2,1)S(1)}, bf16[3,3,3,128,128]{4,3,2,1,0:T(8,128)(2,1)}, u32[]{:S(2)}) copy-start(bf16[3,3,3,128,128]{4,3,2,1,0:T(8,128)(2,1)} %param.10) | copy-start | bytes 2654212
  111.1 5.7 %collective-permute-start.7 = (bf16[27,128,128]{2,1,0:T(8,128)(2,1)S(1)}, bf16[27,128,128]{2,1,0:T(8,128)(2,1)S(1)}, u32[]{:S(2)}, u32[]{:S(2)}) collective-permute-start(bf16[27,128,128]{2,1,0:T(8,128)(2,1)S(1)} %bitcast.51), channel_id=1, source_target_pairs={{0,1},{1,0},{2,3},{3,2},{4,5},{5,4},{6,7},{7,6},{8,9},{9,8},{10,11... | collective-permute-start | bytes 2654216 | tf_op jit(solution)/shard_map/ppermute | solution.py:335

commit v6 on v5

--- a/solution.py
+++ b/solution.py
@@ -138,32 +138,30 @@
 
 def two_planes(ref, w_ref, nx, ny):
     plane = ny * PITCH
-    parts = [None] * nx
-    rest = None
-    for b in range(3):
-        weights = [
-            jnp.concatenate([w_ref[(a * 3 + b) * 3 + k] for k in range(3)], axis=1)
-            for a in range(3)
-        ]
-        cells = ref[1:, 2 - b : 2 - b + ny].reshape(-1, 3 * C)
-        both = lax.dot_general(
-            cells,
-            jnp.concatenate(weights[:2], axis=0),
-            (((1,), (1,)), ((), ())),
-            preferred_element_type=F32,
-        )
-        for x in range(nx):
-            for a in range(2):
-                first = (x + 1 - a) * plane
-                part = both[first : first + plane, a * C : (a + 1) * C]
-                parts[x] = part if parts[x] is None else parts[x] + part
-        last = lax.dot_general(
-            window(ref, (2, b), nx, ny),
-            weights[2],
-            (((1,), (1,)), ((), ())),
-            preferred_element_type=F32,
-        )
-        rest = last if rest is None else rest + last
+    weights = [
+        jnp.concatenate(
+            [w_ref[(a * 3 + b) * 3 + k] for b in range(3) for k in range(3)], axis=1
+        )
+        for a in range(3)
+    ]
+    cells = [ref[1:, 2 - b : 2 - b + ny].reshape(-1, 3 * C) for b in range(3)]
+    both = lax.dot_general(
+        jnp.concatenate(cells, axis=1),
+        jnp.concatenate(weights[:2], axis=0),
+        (((1,), (1,)), ((), ())),
+        preferred_element_type=F32,
+    )
+    cells = [window(ref, (2, b), nx, ny) for b in range(3)]
+    rest = lax.dot_general(
+        jnp.concatenate(cells, axis=1),
+        weights[2],
+        (((1,), (1,)), ((), ())),
+        preferred_element_type=F32,
+    )
+    parts = []
+    for x in range(nx):
+        one, two = (x + 1) * plane, x * plane
+        parts.append(both[one : one + plane, :C] + both[two : two + plane, C:])
     return jnp.concatenate(parts, axis=0) + rest
 
 

time: 118 us -> 118 us (level)
  no operation moved by 1% of the time
where the time goes in v6:
time: 118 us
  blocking collectives  75 us (64%)
  starting transfers between devices  28.4 us (24%)
  Pallas kernels  5.36 us (5%)
  waiting for transfers between devices  5 us (4%)
  other arithmetic  2.41 us (2%)
    all_to_all x5, blocking collectives, exchanged(): lax.all_to_all(pieces, EVERY, 0, 0, axis_index_groups=groups, tiled=True)  75 us
    ppermute x4, starting transfers between devices, exchange(): return (lax.ppermute(up, axis, right), lax.ppermute(down, axis, left))  12 us
    ppermute x1, starting transfers between devices, extend(): far = lax.ppermute(jnp.where(upper, last, first), Z, outer)  5.88 us
    ppermute x1, starting transfers between devices, extend(): near = lax.ppermute(jnp.where(upper, first, last), Z, inner)  4.5 us
    ppermute x1, starting transfers between devices, on_device(): other = lax.ppermute(mine, 'gc', [(0, 1), (1, 0)])  3.73 us
  transfers between devices with their start and end apart: 8, of which 4 were waited for; matrix products, arithmetic and copies ran while one was open for 0% of the time, Pallas kernels for 2%

profile of v6, /device:TPU:1, one launch (start us, length us, event | category | flops | bytes accessed | tf_op | source)
XLA Modules:
  0.0 117.7 jit_solution(15795699514243824167)
XLA Ops:
  0.6 0.0 copy-start.2
  0.6 1.0 fusion.1
  1.7 1.3 %collective-permute-start.1 = (bf16[24,8,128]{2,1,0:T(8,128)(2,1)S(1)}, bf16[24,8,128]{2,1,0:T(8,128)(2,1)S(1)}, u32[]{:S(2)}, u32[]{:S(2)}) collective-permute-start(bf16[24,8,128]{2,1,0:T(8,128)(2,1)S(1)} %pad_maximum_fusion.8), channel_id=1, source_target_pairs={{128,0},{256,128},{384,256},{129,1},{257,129},{385,257},{130,2},{2... | collective-permute-start | bytes 147464 | tf_op jit(solution)/shard_map/ppermute | solution.py:26
  3.0 4.6 %collective-permute-start = (bf16[24,8,128]{2,1,0:T(8,128)(2,1)S(1)}, bf16[24,8,128]{2,1,0:T(8,128)(2,1)S(1)}, u32[]{:S(2)}, u32[]{:S(2)}) collective-permute-start(bf16[24,8,128]{2,1,0:T(8,128)(2,1)S(1)} %pad_maximum_fusion.7), channel_id=1, source_target_pairs={{0,128},{128,256},{256,384},{1,129},{129,257},{257,385},{2,130},{1... | collective-permute-start | bytes 147464 | tf_op jit(solution)/shard_map/ppermute | solution.py:26
  7.6 0.0 copy-done.2
  7.7 0.0 collective-permute-done.1
  7.7 1.1 collective-permute-done
  8.8 1.3 %collective-permute-start.3 = (bf16[22,8,128]{2,1,0:T(8,128)(2,1)S(1)}, bf16[22,8,128]{2,1,0:T(8,128)(2,1)S(1)}, u32[]{:S(2)}, u32[]{:S(2)}) collective-permute-start(bf16[22,8,128]{2,1,0:T(8,128)(2,1)S(1)} %pad_maximum_fusion.10), channel_id=1, source_target_pairs={{32,0},{64,32},{96,64},{33,1},{65,33},{97,65},{34,2},{66,34},{98,6... | collective-permute-start | bytes 135176 | tf_op jit(solution)/shard_map/ppermute | solution.py:26
  10.1 4.9 %collective-permute-start.2 = (bf16[22,8,128]{2,1,0:T(8,128)(2,1)S(1)}, bf16[22,8,128]{2,1,0:T(8,128)(2,1)S(1)}, u32[]{:S(2)}, u32[]{:S(2)}) collective-permute-start(bf16[22,8,128]{2,1,0:T(8,128)(2,1)S(1)} %pad_maximum_fusion.9), channel_id=1, source_target_pairs={{0,32},{32,64},{64,96},{1,33},{33,65},{65,97},{2,34},{34,66},{66,9... | collective-permute-start | bytes 135176 | tf_op jit(solution)/shard_map/ppermute | solution.py:26
  15.1 0.1 pad.13.clone
  15.1 0.0 collective-permute-done.3
  15.1 1.0 collective-permute-done.2
  16.2 0.0 copy-start.1
  16.3 0.1 broadcast_select_fusion.3
  16.4 5.9 %collective-permute-start.5 = (bf16[156,2,128]{2,1,0:T(2,128)(2,1)S(1)}, bf16[156,2,128]{2,1,0:T(2,128)(2,1)S(1)}, u32[]{:S(2)}, u32[]{:S(2)}) collective-permute-start(bf16[156,2,128]{2,1,0:T(2,128)(2,1)S(1)} %bitcast.80), channel_id=1, source_target_pairs={{1,2},{2,1},{3,4},{4,3},{5,6},{6,5},{7,8},{8,7},{9,10},{10,9},{11,... | collective-permute-start | bytes 239624 | tf_op jit(solution)/shard_map/ppermute | solution.py:64
  22.3 4.5 %collective-permute-start.4 = (bf16[156,2,128]{2,1,0:T(2,128)(2,1)S(1)}, bf16[156,2,128]{2,1,0:T(2,128)(2,1)S(1)}, u32[]{:S(2)}, u32[]{:S(2)}) collective-permute-start(bf16[156,2,128]{2,1,0:T(2,128)(2,1)S(1)} %get-tuple-element.17), channel_id=1, source_target_pairs={{0,1},{1,0},{2,3},{3,2},{4,5},{5,4},{6,7},{7,6},{8,9},{9,8},{10,11... | collective-permute-start | bytes 239624 | tf_op jit(solution)/shard_map/ppermute | solution.py:65
  26.9 0.0 collective-permute-done.5
  26.9 0.9 collective-permute-done.4
  27.8 0.5 maximum_maximum_fusion.lines_ref
  28.3 0.0 copy-done.1
  28.3 2.3 %kernel_gradients.1 = (bf16[2,27,128,128]{3,2,1,0:T(8,128)(2,1)S(1)}, bf16[6,6,16,384]{3,2,1,0:T(8,128)(2,1)S(1)}) custom-call(s32[1]{0:T(128)} %bitcast.core_ref, bf16[156,16,128]{2,1,0:T(8,128)(2,1)S(1)} %maximum_maximum_fusion.lines_ref, bf16[4,4,16,128]{3,2,1,0:T(8,128)(2,1)S(1)} %pad_maximum_fusion.5.hidden_ref, ...), custom_call_target="tpu_custom_call" | custom-call | flops 905969664 | bytes 6291456 | tf_op jit(solution)/shard_map/kernel_gradients/pallas_call | solution.py:308
  30.5 0.1 slice_bitcast_fusion
  30.6 2.3 %collective-permute-start.6 = (bf16[27,128,128]{2,1,0:T(8,128)(2,1)S(1)}, bf16[27,128,128]{2,1,0:T(8,128)(2,1)S(1)}, u32[]{:S(2)}, u32[]{:S(2)}) collective-permute-start(bf16[27,128,128]{2,1,0:T(8,128)(2,1)S(1)} %slice_bitcast_fusion), channel_id=1, source_target_pairs={{0,1},{1,0},{2,3},{3,2},{4,5},{5,4},{6,7},{7,6},{8,9},{9,8},{10,11... | collective-permute-start | bytes 2654216 | tf_op jit(solution)/shard_map/ppermute | solution.py:281
  32.9 2.0 %collective-permute-done.6 = bf16[27,128,128]{2,1,0:T(8,128)(2,1)S(1)} collective-permute-done((bf16[27,128,128]{2,1,0:T(8,128)(2,1)S(1)}, bf16[27,128,128]{2,1,0:T(8,128)(2,1)S(1)}, u32[]{:S(2)}, u32[]{:S(2)}) %collective-permute-start.6) | collective-permute-done | bytes 884768 | tf_op jit(solution)/shard_map/ppermute | solution.py:281
  35.0 0.3 fusion
  35.3 11.4 %all_to_all.25 = bf16[4,864,128]{2,1,0:T(8,128)(2,1)S(1)} all-to-all(bf16[4,864,128]{2,1,0:T(8,128)(2,1)S(1)} %bitcast.55), channel_id=1, replica_groups={{0,128,256,384},{2,130,258,386},{4,132,260,388},{6,134,262,390},{8,136,..., dimensions={0} | all-to-all | bytes 1769472 | tf_op jit(solution)/shard_map/all_to_all | solution.py:261
  46.7 0.2 reduce_sum.36
  46.9 14.7 %all_to_all.26 = bf16[8,112,128]{2,1,0:T(8,128)(2,1)S(1)} all-to-all(bf16[8,112,128]{2,1,0:T(8,128)(2,1)S(1)} %bitcast.60), channel_id=1, replica_groups={{0,16,32,48,64,80,96,112},{2,18,34,50,66,82,98,114},{4,20,36,52,68,84,1..., dimensions={0} | all-to-all | bytes 458752 | tf_op jit(solution)/shard_map/all_to_all | solution.py:261
  61.7 27.4 %all_to_all.27 = bf16[8,112,128]{2,1,0:T(8,128)(2,1)S(1)} all-to-all(bf16[8,112,128]{2,1,0:T(8,128)(2,1)S(1)} %broadcast_in_dim.39), channel_id=1, replica_groups={{0,2,4,6,8,10,12,14},{16,18,20,22,24,26,28,30},{32,34,36,38,40,42,44,46..., dimensions={0} | all-to-all | bytes 458752 | tf_op jit(solution)/shard_map/all_to_all | solution.py:261
  89.2 10.6 %all_to_all.28 = bf16[8,112,128]{2,1,0:T(8,128)(2,1)S(1)} all-to-all(bf16[8,112,128]{2,1,0:T(8,128)(2,1)S(1)} %broadcast_in_dim.40), channel_id=1, replica_groups={{0,16,32,48,64,80,96,112},{2,18,34,50,66,82,98,114},{4,20,36,52,68,84,1..., dimensions={0} | all-to-all | bytes 458752 | tf_op jit(solution)/shard_map/all_to_all | solution.py:261
  99.8 0.0 copy-start
  99.9 0.1 broadcast_in_dim.41
  100.0 10.8 %all_to_all.29 = bf16[4,864,128]{2,1,0:T(8,128)(2,1)S(1)} all-to-all(bf16[4,864,128]{2,1,0:T(8,128)(2,1)S(1)} %broadcast_in_dim.41), channel_id=1, replica_groups={{0,128,256,384},{2,130,258,386},{4,132,260,388},{6,134,262,390},{8,136,..., dimensions={0} | all-to-all | bytes 1769472 | tf_op jit(solution)/shard_map/all_to_all | solution.py:261
  110.8 3.7 %collective-permute-start.7 = (bf16[27,128,128]{2,1,0:T(8,128)(2,1)S(1)}, bf16[27,128,128]{2,1,0:T(8,128)(2,1)S(1)}, u32[]{:S(2)}, u32[]{:S(2)}) collective-permute-start(bf16[27,128,128]{2,1,0:T(8,128)(2,1)S(1)} %bitcast.51), channel_id=1, source_target_pairs={{0,1},{1,0},{2,3},{3,2},{4,5},{5,4},{6,7},{7,6},{8,9},{9,8},{10,11... | collective-permute-start | bytes 2654216 | tf_op jit(solution)/shard_map/ppermute | solution.py:333
  114.5 0.0 copy-done
  114.6 2.1 %input_gradient.1 = (bf16[4,8,8,128]{3,2,1,0:T(8,128)(2,1)}, bf16[27,128,128]{2,1,0:T(8,128)(2,1)}, bf16[27,128,128]{2,1,0:T(8,128)(2,1)}) custom-call(s32[1]{0:T(128)} %bitcast.core_ref, bf16[6,6,16,384]{3,2,1,0:T(8,128)(2,1)S(1)} %get-tuple-element.10.pair_ref, bf16[27,128,128]{2,1,0:T(8,128)(2,1)S(1)} %bitcast.53, bf16[27,128,128]{2,1,0:T(8,128)(2,1)S(1)} %bitcast.52), custom_call_target="tpu_custom_call" | custom-call | flops 226492416 | bytes 2097152 | tf_op jit(solution)/shard_map/input_gradient/pallas_call | solution.py:337
  116.6 0.0 collective-permute-done.7.other_ref
  116.7 1.0 place_totals.1
  (33 shorter events, 0.5 us)
Async XLA Ops:
  0.6 7.0 %copy-start.2 = (bf16[4,8,8,128]{3,2,1,0:T(8,128)(2,1)S(1)}, bf16[4,8,8,128]{3,2,1,0:T(8,128)(2,1)}, u32[]{:S(2)}) copy-start(bf16[4,8,8,128]{3,2,1,0:T(8,128)(2,1)} %param.6) | copy-start | bytes 196612
  1.7 6.0 %collective-permute-start.1 = (bf16[24,8,128]{2,1,0:T(8,128)(2,1)S(1)}, bf16[24,8,128]{2,1,0:T(8,128)(2,1)S(1)}, u32[]{:S(2)}, u32[]{:S(2)}) collective-permute-start(bf16[24,8,128]{2,1,0:T(8,128)(2,1)S(1)} %pad_maximum_fusion.8), channel_id=1, source_target_pairs={{128,0},{256,128},{384,256},{129,1},{257,129},{385,257},{130,2},{2... | collective-permute-start | bytes 147464 | tf_op jit(solution)/shard_map/ppermute | solution.py:26
  3.0 5.7 %collective-permute-start = (bf16[24,8,128]{2,1,0:T(8,128)(2,1)S(1)}, bf16[24,8,128]{2,1,0:T(8,128)(2,1)S(1)}, u32[]{:S(2)}, u32[]{:S(2)}) collective-permute-start(bf16[24,8,128]{2,1,0:T(8,128)(2,1)S(1)} %pad_maximum_fusion.7), channel_id=1, source_target_pairs={{0,128},{128,256},{256,384},{1,129},{129,257},{257,385},{2,130},{1... | collective-permute-start | bytes 147464 | tf_op jit(solution)/shard_map/ppermute | solution.py:26
  8.8 6.3 %collective-permute-start.3 = (bf16[22,8,128]{2,1,0:T(8,128)(2,1)S(1)}, bf16[22,8,128]{2,1,0:T(8,128)(2,1)S(1)}, u32[]{:S(2)}, u32[]{:S(2)}) collective-permute-start(bf16[22,8,128]{2,1,0:T(8,128)(2,1)S(1)} %pad_maximum_fusion.10), channel_id=1, source_target_pairs={{32,0},{64,32},{96,64},{33,1},{65,33},{97,65},{34,2},{66,34},{98,6... | collective-permute-start | bytes 135176 | tf_op jit(solution)/shard_map/ppermute | solution.py:26
  10.1 6.0 %collective-permute-start.2 = (bf16[22,8,128]{2,1,0:T(8,128)(2,1)S(1)}, bf16[22,8,128]{2,1,0:T(8,128)(2,1)S(1)}, u32[]{:S(2)}, u32[]{:S(2)}) collective-permute-start(bf16[22,8,128]{2,1,0:T(8,128)(2,1)S(1)} %pad_maximum_fusion.9), channel_id=1, source_target_pairs={{0,32},{32,64},{64,96},{1,33},{33,65},{65,97},{2,34},{34,66},{66,9... | collective-permute-start | bytes 135176 | tf_op jit(solution)/shard_map/ppermute | solution.py:26
  16.2 12.1 %copy-start.1 = (bf16[3,3,3,128,128]{4,3,2,1,0:T(8,128)(2,1)S(1)}, bf16[3,3,3,128,128]{4,3,2,1,0:T(8,128)(2,1)}, u32[]{:S(2)}) copy-start(bf16[3,3,3,128,128]{4,3,2,1,0:T(8,128)(2,1)} %param.11) | copy-start | bytes 2654212
  16.4 10.4 %collective-permute-start.5 = (bf16[156,2,128]{2,1,0:T(2,128)(2,1)S(1)}, bf16[156,2,128]{2,1,0:T(2,128)(2,1)S(1)}, u32[]{:S(2)}, u32[]{:S(2)}) collective-permute-start(bf16[156,2,128]{2,1,0:T(2,128)(2,1)S(1)} %bitcast.80), channel_id=1, source_target_pairs={{1,2},{2,1},{3,4},{4,3},{5,6},{6,5},{7,8},{8,7},{9,10},{10,9},{11,... | collective-permute-start | bytes 239624 | tf_op jit(solution)/shard_map/ppermute | solution.py:64
  22.3 5.4 %collective-permute-start.4 = (bf16[156,2,128]{2,1,0:T(2,128)(2,1)S(1)}, bf16[156,2,128]{2,1,0:T(2,128)(2,1)S(1)}, u32[]{:S(2)}, u32[]{:S(2)}) collective-permute-start(bf16[156,2,128]{2,1,0:T(2,128)(2,1)S(1)} %get-tuple-element.17), channel_id=1, source_target_pairs={{0,1},{1,0},{2,3},{3,2},{4,5},{5,4},{6,7},{7,6},{8,9},{9,8},{10,11... | collective-permute-start | bytes 239624 | tf_op jit(solution)/shard_map/ppermute | solution.py:65
  30.6 4.3 %collective-permute-start.6 = (bf16[27,128,128]{2,1,0:T(8,128)(2,1)S(1)}, bf16[27,128,128]{2,1,0:T(8,128)(2,1)S(1)}, u32[]{:S(2)}, u32[]{:S(2)}) collective-permute-start(bf16[27,128,128]{2,1,0:T(8,128)(2,1)S(1)} %slice_bitcast_fusion), channel_id=1, source_target_pairs={{0,1},{1,0},{2,3},{3,2},{4,5},{5,4},{6,7},{7,6},{8,9},{9,8},{10,11... | collective-permute-start | bytes 2654216 | tf_op jit(solution)/shard_map/ppermute | solution.py:281
  99.8 14.7 %copy-start = (bf16[3,3,3,128,128]{4,3,2,1,0:T(8,128)(2,1)S(1)}, bf16[3,3,3,128,128]{4,3,2,1,0:T(8,128)(2,1)}, u32[]{:S(2)}) copy-start(bf16[3,3,3,128,128]{4,3,2,1,0:T(8,128)(2,1)} %param.10) | copy-start | bytes 2654212
  110.8 5.8 %collective-permute-start.7 = (bf16[27,128,128]{2,1,0:T(8,128)(2,1)S(1)}, bf16[27,128,128]{2,1,0:T(8,128)(2,1)S(1)}, u32[]{:S(2)}, u32[]{:S(2)}) collective-permute-start(bf16[27,128,128]{2,1,0:T(8,128)(2,1)S(1)} %bitcast.51), channel_id=1, source_target_pairs={{0,1},{1,0},{2,3},{3,2},{4,5},{5,4},{6,7},{7,6},{8,9},{9,8},{10,11... | collective-permute-start | bytes 2654216 | tf_op jit(solution)/shard_map/ppermute | solution.py:333

commit v7 on v6

--- a/solution.py
+++ b/solution.py
@@ -13,7 +13,6 @@
 Z = ("gh", "gw", "gc")
 EVERY = ("gx", "gy", "gh", "gw", "gc")
 C = 128
-GROUP = 9
 PITCH = 16
 F32 = jnp.float32
 BF16 = jnp.bfloat16
@@ -118,22 +117,6 @@
         part = (part * scale).astype(BF16)
         for k in range(3):
             out_ref[slot, t * 3 + k] = part[:, k * C : (k + 1) * C]
-
-
-def input_grads(ref, w_ref, nx, ny):
-    total = None
-    for group in range(0, 9, GROUP):
-        numbers = range(group, min(group + GROUP, 9))
-        cells = [window(ref, taps()[t], nx, ny) for t in numbers]
-        weights = [w_ref[3 * t + k] for t in numbers for k in range(3)]
-        part = lax.dot_general(
-            jnp.concatenate(cells, axis=1),
-            jnp.concatenate(weights, axis=1),
-            (((1,), (1,)), ((), ())),
-            preferred_element_type=F32,
-        )
-        total = part if total is None else total + part
-    return total
 
 
 def two_planes(ref, w_ref, nx, ny):
@@ -198,7 +181,7 @@
     on_core(core_ref, one_ref, two_ref, start)
     nx, ny, nz, _ = out_ref.shape
     half = ny // 2
-    total = input_grads(pair_ref, w_ref, nx, half)
+    total = two_planes(pair_ref, w_ref, nx, half)
     total = total.reshape(nx, half, PITCH, C).astype(BF16)
     out_ref[:, :half] = total[:, :, :nz]
     out_ref[:, half:] = total[:, :, nz:]

time: 118 us -> 118 us (level)
  no operation moved by 1% of the time
where the time goes in v7:
time: 118 us
  blocking collectives  75 us (64%)
  starting transfers between devices  28.4 us (24%)
  Pallas kernels  5.28 us (4%)
  waiting for transfers between devices  5.01 us (4%)
  other arithmetic  2.41 us (2%)
    all_to_all x5, blocking collectives, exchanged(): lax.all_to_all(pieces, EVERY, 0, 0, axis_index_groups=groups, tiled=True)  75 us
    ppermute x4, starting transfers between devices, exchange(): return (lax.ppermute(up, axis, right), lax.ppermute(down, axis, left))  12 us
    ppermute x1, starting transfers between devices, extend(): far = lax.ppermute(jnp.where(upper, last, first), Z, outer)  5.88 us
    ppermute x1, starting transfers between devices, extend(): near = lax.ppermute(jnp.where(upper, first, last), Z, inner)  4.5 us
    ppermute x1, starting transfers between devices, on_device(): other = lax.ppermute(mine, 'gc', [(0, 1), (1, 0)])  3.73 us
  transfers between devices with their start and end apart: 8, of which 4 were waited for; matrix products, arithmetic and copies ran while one was open for 0% of the time, Pallas kernels for 2%

profile of v7, /device:TPU:1, one launch (start us, length us, event | category | flops | bytes accessed | tf_op | source)
XLA Modules:
  0.0 117.6 jit_solution(15133061510328939059)
XLA Ops:
  0.6 0.0 copy-start.2
  0.6 1.0 fusion.1
  1.7 1.3 %collective-permute-start.1 = (bf16[24,8,128]{2,1,0:T(8,128)(2,1)S(1)}, bf16[24,8,128]{2,1,0:T(8,128)(2,1)S(1)}, u32[]{:S(2)}, u32[]{:S(2)}) collective-permute-start(bf16[24,8,128]{2,1,0:T(8,128)(2,1)S(1)} %pad_maximum_fusion.8), channel_id=1, source_target_pairs={{128,0},{256,128},{384,256},{129,1},{257,129},{385,257},{130,2},{2... | collective-permute-start | bytes 147464 | tf_op jit(solution)/shard_map/ppermute | solution.py:25
  3.0 4.6 %collective-permute-start = (bf16[24,8,128]{2,1,0:T(8,128)(2,1)S(1)}, bf16[24,8,128]{2,1,0:T(8,128)(2,1)S(1)}, u32[]{:S(2)}, u32[]{:S(2)}) collective-permute-start(bf16[24,8,128]{2,1,0:T(8,128)(2,1)S(1)} %pad_maximum_fusion.7), channel_id=1, source_target_pairs={{0,128},{128,256},{256,384},{1,129},{129,257},{257,385},{2,130},{1... | collective-permute-start | bytes 147464 | tf_op jit(solution)/shard_map/ppermute | solution.py:25
  7.6 0.0 copy-done.2
  7.7 0.0 collective-permute-done.1
  7.7 1.1 collective-permute-done
  8.8 1.3 %collective-permute-start.3 = (bf16[22,8,128]{2,1,0:T(8,128)(2,1)S(1)}, bf16[22,8,128]{2,1,0:T(8,128)(2,1)S(1)}, u32[]{:S(2)}, u32[]{:S(2)}) collective-permute-start(bf16[22,8,128]{2,1,0:T(8,128)(2,1)S(1)} %pad_maximum_fusion.10), channel_id=1, source_target_pairs={{32,0},{64,32},{96,64},{33,1},{65,33},{97,65},{34,2},{66,34},{98,6... | collective-permute-start | bytes 135176 | tf_op jit(solution)/shard_map/ppermute | solution.py:25
  10.1 4.9 %collective-permute-start.2 = (bf16[22,8,128]{2,1,0:T(8,128)(2,1)S(1)}, bf16[22,8,128]{2,1,0:T(8,128)(2,1)S(1)}, u32[]{:S(2)}, u32[]{:S(2)}) collective-permute-start(bf16[22,8,128]{2,1,0:T(8,128)(2,1)S(1)} %pad_maximum_fusion.9), channel_id=1, source_target_pairs={{0,32},{32,64},{64,96},{1,33},{33,65},{65,97},{2,34},{34,66},{66,9... | collective-permute-start | bytes 135176 | tf_op jit(solution)/shard_map/ppermute | solution.py:25
  15.1 0.1 pad.13.clone
  15.1 0.0 collective-permute-done.3
  15.1 1.0 collective-permute-done.2
  16.2 0.0 copy-start.1
  16.3 0.1 broadcast_select_fusion.3
  16.4 5.9 %collective-permute-start.5 = (bf16[156,2,128]{2,1,0:T(2,128)(2,1)S(1)}, bf16[156,2,128]{2,1,0:T(2,128)(2,1)S(1)}, u32[]{:S(2)}, u32[]{:S(2)}) collective-permute-start(bf16[156,2,128]{2,1,0:T(2,128)(2,1)S(1)} %bitcast.80), channel_id=1, source_target_pairs={{1,2},{2,1},{3,4},{4,3},{5,6},{6,5},{7,8},{8,7},{9,10},{10,9},{11,... | collective-permute-start | bytes 239624 | tf_op jit(solution)/shard_map/ppermute | solution.py:63
  22.3 4.5 %collective-permute-start.4 = (bf16[156,2,128]{2,1,0:T(2,128)(2,1)S(1)}, bf16[156,2,128]{2,1,0:T(2,128)(2,1)S(1)}, u32[]{:S(2)}, u32[]{:S(2)}) collective-permute-start(bf16[156,2,128]{2,1,0:T(2,128)(2,1)S(1)} %get-tuple-element.17), channel_id=1, source_target_pairs={{0,1},{1,0},{2,3},{3,2},{4,5},{5,4},{6,7},{7,6},{8,9},{9,8},{10,11... | collective-permute-start | bytes 239624 | tf_op jit(solution)/shard_map/ppermute | solution.py:64
  26.9 0.0 collective-permute-done.5
  26.9 0.9 collective-permute-done.4
  27.8 0.5 maximum_maximum_fusion.lines_ref
  28.3 0.0 copy-done.1
  28.3 2.3 %kernel_gradients.1 = (bf16[2,27,128,128]{3,2,1,0:T(8,128)(2,1)S(1)}, bf16[6,6,16,384]{3,2,1,0:T(8,128)(2,1)S(1)}) custom-call(s32[1]{0:T(128)} %bitcast.core_ref, bf16[156,16,128]{2,1,0:T(8,128)(2,1)S(1)} %maximum_maximum_fusion.lines_ref, bf16[4,4,16,128]{3,2,1,0:T(8,128)(2,1)S(1)} %pad_maximum_fusion.5.hidden_ref, ...), custom_call_target="tpu_custom_call" | custom-call | flops 905969664 | bytes 6291456 | tf_op jit(solution)/shard_map/kernel_gradients/pallas_call | solution.py:291
  30.5 0.1 slice_bitcast_fusion
  30.6 2.3 %collective-permute-start.6 = (bf16[27,128,128]{2,1,0:T(8,128)(2,1)S(1)}, bf16[27,128,128]{2,1,0:T(8,128)(2,1)S(1)}, u32[]{:S(2)}, u32[]{:S(2)}) collective-permute-start(bf16[27,128,128]{2,1,0:T(8,128)(2,1)S(1)} %slice_bitcast_fusion), channel_id=1, source_target_pairs={{0,1},{1,0},{2,3},{3,2},{4,5},{5,4},{6,7},{7,6},{8,9},{9,8},{10,11... | collective-permute-start | bytes 2654216 | tf_op jit(solution)/shard_map/ppermute | solution.py:264
  32.9 2.0 %collective-permute-done.6 = bf16[27,128,128]{2,1,0:T(8,128)(2,1)S(1)} collective-permute-done((bf16[27,128,128]{2,1,0:T(8,128)(2,1)S(1)}, bf16[27,128,128]{2,1,0:T(8,128)(2,1)S(1)}, u32[]{:S(2)}, u32[]{:S(2)}) %collective-permute-start.6) | collective-permute-done | bytes 884768 | tf_op jit(solution)/shard_map/ppermute | solution.py:264
  35.0 0.3 fusion
  35.3 11.4 %all_to_all.25 = bf16[4,864,128]{2,1,0:T(8,128)(2,1)S(1)} all-to-all(bf16[4,864,128]{2,1,0:T(8,128)(2,1)S(1)} %bitcast.55), channel_id=1, replica_groups={{0,128,256,384},{2,130,258,386},{4,132,260,388},{6,134,262,390},{8,136,..., dimensions={0} | all-to-all | bytes 1769472 | tf_op jit(solution)/shard_map/all_to_all | solution.py:244
  46.7 0.2 reduce_sum.36
  46.9 14.7 %all_to_all.26 = bf16[8,112,128]{2,1,0:T(8,128)(2,1)S(1)} all-to-all(bf16[8,112,128]{2,1,0:T(8,128)(2,1)S(1)} %bitcast.60), channel_id=1, replica_groups={{0,16,32,48,64,80,96,112},{2,18,34,50,66,82,98,114},{4,20,36,52,68,84,1..., dimensions={0} | all-to-all | bytes 458752 | tf_op jit(solution)/shard_map/all_to_all | solution.py:244
  61.7 27.4 %all_to_all.27 = bf16[8,112,128]{2,1,0:T(8,128)(2,1)S(1)} all-to-all(bf16[8,112,128]{2,1,0:T(8,128)(2,1)S(1)} %broadcast_in_dim.39), channel_id=1, replica_groups={{0,2,4,6,8,10,12,14},{16,18,20,22,24,26,28,30},{32,34,36,38,40,42,44,46..., dimensions={0} | all-to-all | bytes 458752 | tf_op jit(solution)/shard_map/all_to_all | solution.py:244
  89.2 10.6 %all_to_all.28 = bf16[8,112,128]{2,1,0:T(8,128)(2,1)S(1)} all-to-all(bf16[8,112,128]{2,1,0:T(8,128)(2,1)S(1)} %broadcast_in_dim.40), channel_id=1, replica_groups={{0,16,32,48,64,80,96,112},{2,18,34,50,66,82,98,114},{4,20,36,52,68,84,1..., dimensions={0} | all-to-all | bytes 458752 | tf_op jit(solution)/shard_map/all_to_all | solution.py:244
  99.8 0.0 copy-start
  99.9 0.1 broadcast_in_dim.41
  100.0 10.8 %all_to_all.29 = bf16[4,864,128]{2,1,0:T(8,128)(2,1)S(1)} all-to-all(bf16[4,864,128]{2,1,0:T(8,128)(2,1)S(1)} %broadcast_in_dim.41), channel_id=1, replica_groups={{0,128,256,384},{2,130,258,386},{4,132,260,388},{6,134,262,390},{8,136,..., dimensions={0} | all-to-all | bytes 1769472 | tf_op jit(solution)/shard_map/all_to_all | solution.py:244
  110.8 3.7 %collective-permute-start.7 = (bf16[27,128,128]{2,1,0:T(8,128)(2,1)S(1)}, bf16[27,128,128]{2,1,0:T(8,128)(2,1)S(1)}, u32[]{:S(2)}, u32[]{:S(2)}) collective-permute-start(bf16[27,128,128]{2,1,0:T(8,128)(2,1)S(1)} %bitcast.51), channel_id=1, source_target_pairs={{0,1},{1,0},{2,3},{3,2},{4,5},{5,4},{6,7},{7,6},{8,9},{9,8},{10,11... | collective-permute-start | bytes 2654216 | tf_op jit(solution)/shard_map/ppermute | solution.py:316
  114.5 0.0 copy-done
  114.6 2.0 %input_gradient.1 = (bf16[4,8,8,128]{3,2,1,0:T(8,128)(2,1)}, bf16[27,128,128]{2,1,0:T(8,128)(2,1)}, bf16[27,128,128]{2,1,0:T(8,128)(2,1)}) custom-call(s32[1]{0:T(128)} %bitcast.core_ref, bf16[6,6,16,384]{3,2,1,0:T(8,128)(2,1)S(1)} %get-tuple-element.10.pair_ref, bf16[27,128,128]{2,1,0:T(8,128)(2,1)S(1)} %bitcast.53, bf16[27,128,128]{2,1,0:T(8,128)(2,1)S(1)} %bitcast.52), custom_call_target="tpu_custom_call" | custom-call | flops 226492416 | bytes 2097152 | tf_op jit(solution)/shard_map/input_gradient/pallas_call | solution.py:320
  116.6 0.0 collective-permute-done.7.other_ref
  116.6 1.0 place_totals.1
  (33 shorter events, 0.5 us)
Async XLA Ops:
  0.6 7.0 %copy-start.2 = (bf16[4,8,8,128]{3,2,1,0:T(8,128)(2,1)S(1)}, bf16[4,8,8,128]{3,2,1,0:T(8,128)(2,1)}, u32[]{:S(2)}) copy-start(bf16[4,8,8,128]{3,2,1,0:T(8,128)(2,1)} %param.6) | copy-start | bytes 196612
  1.7 6.0 %collective-permute-start.1 = (bf16[24,8,128]{2,1,0:T(8,128)(2,1)S(1)}, bf16[24,8,128]{2,1,0:T(8,128)(2,1)S(1)}, u32[]{:S(2)}, u32[]{:S(2)}) collective-permute-start(bf16[24,8,128]{2,1,0:T(8,128)(2,1)S(1)} %pad_maximum_fusion.8), channel_id=1, source_target_pairs={{128,0},{256,128},{384,256},{129,1},{257,129},{385,257},{130,2},{2... | collective-permute-start | bytes 147464 | tf_op jit(solution)/shard_map/ppermute | solution.py:25
  3.0 5.7 %collective-permute-start = (bf16[24,8,128]{2,1,0:T(8,128)(2,1)S(1)}, bf16[24,8,128]{2,1,0:T(8,128)(2,1)S(1)}, u32[]{:S(2)}, u32[]{:S(2)}) collective-permute-start(bf16[24,8,128]{2,1,0:T(8,128)(2,1)S(1)} %pad_maximum_fusion.7), channel_id=1, source_target_pairs={{0,128},{128,256},{256,384},{1,129},{129,257},{257,385},{2,130},{1... | collective-permute-start | bytes 147464 | tf_op jit(solution)/shard_map/ppermute | solution.py:25
  8.8 6.3 %collective-permute-start.3 = (bf16[22,8,128]{2,1,0:T(8,128)(2,1)S(1)}, bf16[22,8,128]{2,1,0:T(8,128)(2,1)S(1)}, u32[]{:S(2)}, u32[]{:S(2)}) collective-permute-start(bf16[22,8,128]{2,1,0:T(8,128)(2,1)S(1)} %pad_maximum_fusion.10), channel_id=1, source_target_pairs={{32,0},{64,32},{96,64},{33,1},{65,33},{97,65},{34,2},{66,34},{98,6... | collective-permute-start | bytes 135176 | tf_op jit(solution)/shard_map/ppermute | solution.py:25
  10.1 6.0 %collective-permute-start.2 = (bf16[22,8,128]{2,1,0:T(8,128)(2,1)S(1)}, bf16[22,8,128]{2,1,0:T(8,128)(2,1)S(1)}, u32[]{:S(2)}, u32[]{:S(2)}) collective-permute-start(bf16[22,8,128]{2,1,0:T(8,128)(2,1)S(1)} %pad_maximum_fusion.9), channel_id=1, source_target_pairs={{0,32},{32,64},{64,96},{1,33},{33,65},{65,97},{2,34},{34,66},{66,9... | collective-permute-start | bytes 135176 | tf_op jit(solution)/shard_map/ppermute | solution.py:25
  16.2 12.1 %copy-start.1 = (bf16[3,3,3,128,128]{4,3,2,1,0:T(8,128)(2,1)S(1)}, bf16[3,3,3,128,128]{4,3,2,1,0:T(8,128)(2,1)}, u32[]{:S(2)}) copy-start(bf16[3,3,3,128,128]{4,3,2,1,0:T(8,128)(2,1)} %param.11) | copy-start | bytes 2654212
  16.4 10.4 %collective-permute-start.5 = (bf16[156,2,128]{2,1,0:T(2,128)(2,1)S(1)}, bf16[156,2,128]{2,1,0:T(2,128)(2,1)S(1)}, u32[]{:S(2)}, u32[]{:S(2)}) collective-permute-start(bf16[156,2,128]{2,1,0:T(2,128)(2,1)S(1)} %bitcast.80), channel_id=1, source_target_pairs={{1,2},{2,1},{3,4},{4,3},{5,6},{6,5},{7,8},{8,7},{9,10},{10,9},{11,... | collective-permute-start | bytes 239624 | tf_op jit(solution)/shard_map/ppermute | solution.py:63
  22.3 5.4 %collective-permute-start.4 = (bf16[156,2,128]{2,1,0:T(2,128)(2,1)S(1)}, bf16[156,2,128]{2,1,0:T(2,128)(2,1)S(1)}, u32[]{:S(2)}, u32[]{:S(2)}) collective-permute-start(bf16[156,2,128]{2,1,0:T(2,128)(2,1)S(1)} %get-tuple-element.17), channel_id=1, source_target_pairs={{0,1},{1,0},{2,3},{3,2},{4,5},{5,4},{6,7},{7,6},{8,9},{9,8},{10,11... | collective-permute-start | bytes 239624 | tf_op jit(solution)/shard_map/ppermute | solution.py:64
  30.6 4.3 %collective-permute-start.6 = (bf16[27,128,128]{2,1,0:T(8,128)(2,1)S(1)}, bf16[27,128,128]{2,1,0:T(8,128)(2,1)S(1)}, u32[]{:S(2)}, u32[]{:S(2)}) collective-permute-start(bf16[27,128,128]{2,1,0:T(8,128)(2,1)S(1)} %slice_bitcast_fusion), channel_id=1, source_target_pairs={{0,1},{1,0},{2,3},{3,2},{4,5},{5,4},{6,7},{7,6},{8,9},{9,8},{10,11... | collective-permute-start | bytes 2654216 | tf_op jit(solution)/shard_map/ppermute | solution.py:264
  99.8 14.7 %copy-start = (bf16[3,3,3,128,128]{4,3,2,1,0:T(8,128)(2,1)S(1)}, bf16[3,3,3,128,128]{4,3,2,1,0:T(8,128)(2,1)}, u32[]{:S(2)}) copy-start(bf16[3,3,3,128,128]{4,3,2,1,0:T(8,128)(2,1)} %param.10) | copy-start | bytes 2654212
  110.8 5.8 %collective-permute-start.7 = (bf16[27,128,128]{2,1,0:T(8,128)(2,1)S(1)}, bf16[27,128,128]{2,1,0:T(8,128)(2,1)S(1)}, u32[]{:S(2)}, u32[]{:S(2)}) collective-permute-start(bf16[27,128,128]{2,1,0:T(8,128)(2,1)S(1)} %bitcast.51), channel_id=1, source_target_pairs={{0,1},{1,0},{2,3},{3,2},{4,5},{5,4},{6,7},{7,6},{8,9},{9,8},{10,11... | collective-permute-start | bytes 2654216 | tf_op jit(solution)/shard_map/ppermute | solution.py:316
